TPU v7x, 32 devices: a whole 2x2x4 slice. The times are simulated.
32 devices in a mesh: batch: 16 (over z, y, x), seq: 2 (over core).
Axes of the slice: x: 2, y: 2, z: 4, core: 2. Of those that a mesh axis runs over, the one named last changes fastest.
Arguments:
- frames: bfloat16 [32, 128, 1536], P('batch', 'seq'), may hold values from -6 to 6
- prompt: bfloat16 [32, 128, 768], P('batch'), may hold values from -6 to 6
- clip_frames: int32 [32, 4], P('batch'), may hold values from 0 to 128, as said below
- upstream: bfloat16 [32, 128, 1536], P('batch', 'seq'), may hold values from -6 to 6
- first_gain: float32 [1536], P(('batch', 'seq')), may hold values from 0.5 to 1.5
- first_shift: float32 [1536], P(('batch', 'seq')), may hold values from -2 to 2
- self_project: float32 [1536, 4608], P(('batch', 'seq')), may hold values from -0.15625 to 0.15625
- self_output: float32 [1536, 1536], P(('batch', 'seq')), may hold values from -1.25 to 1.25
- second_gain: float32 [1536], P(('batch', 'seq')), may hold values from 0.5 to 1.5
- second_shift: float32 [1536], P(('batch', 'seq')), may hold values from -2 to 2
- cross_query: float32 [1536, 1536], P(('batch', 'seq')), may hold values from -0.15625 to 0.15625
- cross_memory: float32 [768, 3072], P(('batch', 'seq')), may hold values from -0.21875 to 0.21875
- cross_output: float32 [1536, 1536], P(('batch', 'seq')), may hold values from -0.625 to 0.625
- third_gain: float32 [1536], P(('batch', 'seq')), may hold values from 0.5 to 1.5
- third_shift: float32 [1536], P(('batch', 'seq')), may hold values from -2 to 2
- feed_input: float32 [2, 6144, 1536], P(None, ('batch', 'seq')), may hold values from -0.15625 to 0.15625
- feed_lift: float32 [2, 6144], P(None, ('batch', 'seq')), may hold values from -2 to 2
- feed_output: float32 [6144, 1536], P(('batch', 'seq')), may hold values from -0.109375 to 0.109375
- feed_offset: float32 [1536], P(('batch', 'seq')), may hold values from -2 to 2
Outputs:
- layer_output: bfloat16 [32, 128, 1536], P('batch', 'seq')
- frame_grad: float32 [32, 128, 1536], P('batch', 'seq')
- grad_first_gain: float32 [1536], P(('batch', 'seq'))
- grad_first_shift: float32 [1536], P(('batch', 'seq'))
- grad_self_project: float32 [1536, 4608], P(('batch', 'seq'))
- grad_self_output: float32 [1536, 1536], P(('batch', 'seq'))
- grad_second_gain: float32 [1536], P(('batch', 'seq'))
- grad_second_shift: float32 [1536], P(('batch', 'seq'))
- grad_cross_query: float32 [1536, 1536], P(('batch', 'seq'))
- grad_cross_memory: float32 [768, 3072], P(('batch', 'seq'))
- grad_cross_output: float32 [1536, 1536], P(('batch', 'seq'))
- grad_third_gain: float32 [1536], P(('batch', 'seq'))
- grad_third_shift: float32 [1536], P(('batch', 'seq'))
- grad_feed_input: float32 [2, 6144, 1536], P(None, ('batch', 'seq'))
- grad_feed_lift: float32 [2, 6144], P(None, ('batch', 'seq'))
- grad_feed_output: float32 [6144, 1536], P(('batch', 'seq'))
- grad_feed_offset: float32 [1536], P(('batch', 'seq'))
Inputs may be any that keep to these rules, and one draw needn't show every extreme that they name: `clip_frames`: each row's clip frame counts sum to 128. Among the 2 rows of one batch device, one row, drawn from the seed, is a single clip of 128 frames followed by empty slots; every other row is cut at 3 frames drawn at random.
All inputs are finite; a program needn't handle non-finite values.
Results may differ from a plain program's by a relative error of at most 0.02.
Values may be sent and summed in bfloat16 or wider, within the bound.
No kernel may reach another device: no remote copies, remote signals or barrier semaphores. Data moves between devices by JAX's collectives and lax.ppermute only.
A program may use at most 384 MiB of HBM per device.

v0:
```python
import jax
import jax.numpy as jnp
import numpy as np
from jax import lax
from jax.experimental import pallas as pl
from jax.experimental.pallas import tpu as pltpu
from jax.sharding import PartitionSpec as P

HEAD_DIM = 64
EPS = 1e-05
NEG = -1e30
B = "batch"
S = "seq"
AX = (B, S)


def narrow(value):
    return value.astype(jnp.bfloat16)


def widen(value):
    return value.astype(jnp.float32)


def mult(left, right, form):
    return jnp.einsum(form, left, right, preferred_element_type=jnp.float32)


def dot(left, right):
    return lax.dot_general(left, right, (((1,), (0,)), ((), ())), preferred_element_type=jnp.float32)


def dot_t(left, right):
    return lax.dot_general(left, right, (((1,), (1,)), ((), ())), preferred_element_type=jnp.float32)


def tdot(left, right):
    return lax.dot_general(left, right, (((0,), (0,)), ((), ())), preferred_element_type=jnp.float32)


def standardize(values):
    center = values - jnp.mean(values, -1, keepdims=True)
    inverse = lax.rsqrt(jnp.mean(center * center, -1, keepdims=True) + EPS)
    return (center * inverse, inverse)


def norm_back(incoming, normed, inverse, gain):
    scaled = incoming * gain
    inner = (
        scaled
        - jnp.mean(scaled, -1, keepdims=True)
        - normed * jnp.mean(scaled * normed, -1, keepdims=True)
    )
    return (inner * inverse, jnp.sum(incoming * normed, 0), jnp.sum(incoming, 0))


def clip_tables(lengths, places):
    ends = jnp.cumsum(lengths, 1)
    later = places[None, :, None] >= ends[:, None, :]
    ident = jnp.sum(later.astype(jnp.int32), 2)
    starts = jnp.max(jnp.where(later, ends[:, None, :], 0), 2)
    return (ident, places[None, :] - starts)


def turn(values, offsets, sign):
    half = values.shape[-1] // 2
    freq = 10000.0 ** (-jnp.arange(half, dtype=jnp.float32) / half)
    angle = offsets.astype(jnp.float32)[..., None, None] * freq
    cosine = jnp.cos(angle)
    sine = sign * jnp.sin(angle)
    first = values[..., :half]
    second = values[..., half:]
    return jnp.concatenate([first * cosine - second * sine, second * cosine + first * sine], -1)


def softmax_back(probs, prob_grad):
    return probs * (prob_grad - jnp.sum(probs * prob_grad, -1, keepdims=True))


def hop(value, mask):
    count = lax.axis_size(B) * lax.axis_size(S)
    return lax.ppermute(value, AX, [(i, i ^ mask) for i in range(count)])


def masks_of(order):
    masks = [0]
    for mask in order:
        masks = masks + [old ^ mask for old in masks]
    return masks


def gather(value, order):
    for mask in order:
        value = jnp.concatenate([value, hop(value, mask)], 0)
    return value


def scatter_rest(value, order):
    for mask in reversed(order):
        half = value.shape[0] // 2
        sent = value[half:]
        value = widen(value[:half]) + widen(hop(narrow(sent), mask))
    return value


def scatter_made(make, count, order):
    half = count // 2
    got = hop(narrow(make(half, half)), order[-1])
    kept = make(0, half) + widen(got)
    return scatter_rest(kept, order[:-1])


def gather_halves(value, split, masks, seq_masks):
    known = [0]
    for mask in reversed(masks[2:]):
        value = jnp.concatenate([value, hop(value, mask)], 0)
        known = known + [old ^ mask for old in known]
    halves = []
    for columns, (first, last) in (
        (value[:, :split], (masks[0], masks[1])),
        (value[:, split:], (masks[1], masks[0])),
    ):
        columns = jnp.concatenate([columns, hop(columns, first)], 0)
        have = known + [old ^ first for old in known]
        pieces = [(columns, have), (hop(columns, last), [old ^ last for old in have])]
        for mask in seq_masks:
            pieces = pieces + [(hop(piece, mask), [m ^ mask for m in have]) for piece, have in pieces]
        halves.append(pieces)
    return halves


def settle(halves, targets, widths, me):
    pieces = [(h, piece, have) for h in range(2) for piece, have in halves[h]]
    total = sum(len(have) for h, piece, have in pieces if h == 0)
    rows = pieces[0][1].shape[0] // len(pieces[0][2])
    if rows % 16:
        outs = [[] for _ in widths]
        for h in range(2):
            have = sum([have for _, have in halves[h]], [])
            table = np.zeros(total, np.int32)
            table[np.array(have)] = np.arange(total)
            place = jnp.asarray(table)[me ^ jnp.arange(total, dtype=jnp.int32)]
            blocks = jnp.concatenate([piece for piece, _ in halves[h]], 0).reshape(total, rows, -1)
            blocks = jnp.take(blocks, place, axis=0).reshape(total * rows, -1)
            for source, out, _, count in targets[h]:
                outs[out].append(blocks[:, source : source + count])
        return [jnp.concatenate(out, 1) for out in outs]

    def body(me_ref, *refs):
        ins = refs[: len(pieces)]
        outs = refs[len(pieces) : len(pieces) + len(widths)]
        held = refs[len(pieces) + len(widths) : -2]
        in_sems, out_sems = refs[-2:]
        loads = []
        for i in range(len(pieces)):
            load = pltpu.make_async_copy(ins[i], held[i], in_sems.at[i])
            load.start()
            loads.append(load)
        stores = []
        for i, (h, _, have) in enumerate(pieces):
            loads[i].wait()
            for j, mask in enumerate(have):
                start = pl.multiple_of((me_ref[0] ^ mask) * rows, rows)
                for source, out, column, count in targets[h]:
                    store = pltpu.make_async_copy(
                        held[i].at[pl.ds(j * rows, rows), pl.ds(source, count)],
                        outs[out].at[pl.ds(start, rows), pl.ds(column, count)],
                        out_sems.at[len(stores)],
                    )
                    store.start()
                    stores.append(store)
        for store in stores:
            store.wait()

    count = sum(len(have) * len(targets[h]) for h, _, have in pieces)
    size = 2 * sum(piece.size for _, piece, _ in pieces)
    return pl.pallas_call(
        body,
        out_shape=[jax.ShapeDtypeStruct((total * rows, width), jnp.bfloat16) for width in widths],
        in_specs=[pl.BlockSpec(memory_space=pltpu.SMEM)]
        + [pl.BlockSpec(memory_space=pl.ANY)] * len(pieces),
        out_specs=[pl.BlockSpec(memory_space=pl.ANY)] * len(widths),
        scratch_shapes=[pltpu.VMEM(piece.shape, jnp.bfloat16) for _, piece, _ in pieces]
        + [pltpu.SemaphoreType.DMA((len(pieces),)), pltpu.SemaphoreType.DMA((count,))],
        compiler_params=pltpu.CompilerParams(vmem_limit_bytes=size + (4 << 20)),
        cost_estimate=pl.CostEstimate(flops=0, bytes_accessed=2 * size, transcendentals=0),
    )(me.reshape(1), *[piece for _, piece, _ in pieces])


def scatter_weight(turned, grads, masks, seq_masks):
    size = turned.shape[1]
    value = None
    for mask in reversed(seq_masks):
        half = size // 2
        if value is None:
            sent = narrow(tdot(turned[:, half:], grads))
            kept = narrow(tdot(turned[:, :half], grads))
        else:
            sent, kept = value[half:], value[:half]
        value = narrow(widen(kept) + widen(hop(sent, mask)))
        size = half
    width = value.shape[1]
    value = value.reshape(2, 2, -1, width)
    split = width // 2
    left, right = value[..., :split], value[..., split:]
    left = narrow(widen(left[0]) + widen(hop(left[1], masks[1])))
    right = narrow(widen(right[:, 0]) + widen(hop(right[:, 1], masks[0])))
    left = widen(left[0]) + widen(hop(left[1], masks[0]))
    right = widen(right[0]) + widen(hop(right[1], masks[1]))
    value = narrow(jnp.concatenate([left, right], 1))
    for mask in masks[2:]:
        half = value.shape[0] // 2
        value = widen(value[:half]) + widen(hop(narrow(value[half:]), mask))
    return value


def order_matrix(size, order, me):
    masks = jnp.asarray(np.array(masks_of(order), np.int32))
    rows = size // masks.shape[0]
    source = ((me ^ masks)[:, None] * rows + jnp.arange(rows, dtype=jnp.int32)[None, :]).reshape(-1)
    return (jnp.arange(size, dtype=jnp.int32)[:, None] == source[None, :]).astype(jnp.bfloat16)


def local(
    frames,
    prompt,
    clip_frames,
    upstream,
    first_gain,
    first_shift,
    self_project,
    self_output,
    second_gain,
    second_shift,
    cross_query,
    cross_memory,
    cross_output,
    third_gain,
    third_shift,
    feed_input,
    feed_lift,
    feed_output,
    feed_offset,
):
    row_count, frame_count, width = frames.shape
    heads = width // HEAD_DIM
    token_count = row_count * frame_count
    scale = HEAD_DIM ** (-0.5)
    batch_count = lax.axis_size(B)
    seq_count = lax.axis_size(S)
    device_count = batch_count * seq_count
    seq_place = lax.axis_index(S)
    me = lax.axis_index(B) * seq_count + seq_place
    row_length = frame_count * seq_count
    memory_count = prompt.shape[1]
    memory_share = memory_count // seq_count
    share = first_gain.shape[0]

    seq_masks = [1 << i for i in range(seq_count.bit_length() - 1)]
    batch_masks = [seq_count << i for i in range(batch_count.bit_length() - 1)]
    order = batch_masks[:1:-1] + batch_masks[:2] + seq_masks
    near = batch_masks[:3]
    far = batch_masks[3:]
    token_orders = [near[j:] + near[:j] + seq_masks for j in range(3)]
    third = (token_count * 3 // 8) // 16 * 16
    cuts = [0, third, 2 * third, token_count]

    vectors = [first_gain, first_shift, second_gain, second_shift, third_gain, third_shift, feed_offset]
    vectors = jnp.pad(jnp.stack(vectors, 1), ((0, 0), (0, 128 - len(vectors))))
    split = 3 * width // 2
    halves = gather_halves(
        narrow(jnp.concatenate([vectors, self_project], 1)), 128 + split, batch_masks, seq_masks
    )
    packed, triple_low = settle(
        halves, [[(0, 0, 0, 128), (128, 1, 0, split)], [(0, 1, split, split)]], [128, 3 * width], me
    )
    gain_one, shift_one, gain_two, shift_two, gain_three, shift_three, drop_bias = widen(
        jnp.transpose(packed[:, :7])
    )
    memory_rows = jnp.concatenate([cross_memory[:, :width], cross_memory[:, width:]], 0)
    memory_rows = jnp.pad(memory_rows, ((0, share - memory_rows.shape[0]), (0, 0)))
    halves = gather_halves(
        narrow(jnp.concatenate([self_output, cross_query, cross_output, memory_rows], 1)),
        2 * width,
        batch_masks,
        seq_masks,
    )
    self_low, ask_low, cross_low, memory_low = settle(
        halves,
        [[(0, 0, 0, width), (width, 1, 0, width)], [(0, 2, 0, width), (width, 3, 0, width)]],
        [width] * 4,
        me,
    )
    memory_low = memory_low.reshape(device_count, share, width)[:, : 2 * cross_memory.shape[0]]
    memory_low = memory_low.reshape(device_count, 2, cross_memory.shape[0], width)
    memory_low = jnp.concatenate(
        [memory_low[:, p].reshape(-1, width) for p in range(2)], 1
    )
    lift_low = narrow(feed_input)
    drop_low = narrow(feed_output)
    lift_bias = feed_lift
    for mask in far:
        lift_low = jnp.concatenate([lift_low, hop(lift_low, mask)], 1)
        drop_low = jnp.concatenate([drop_low, hop(drop_low, mask)], 0)
        lift_bias = jnp.concatenate([lift_bias, hop(lift_bias, mask)], 1)
    unit_count = drop_low.shape[0]
    lift_low = lift_low.reshape(2 * unit_count, width)
    lift_bias = widen(narrow(lift_bias.reshape(2 * unit_count)))

    def gather_tokens(value):
        parts = [gather(value[cuts[p] : cuts[p + 1]], token_orders[p]) for p in range(3)]
        return jnp.concatenate(parts, 0)

    upstream_tokens = upstream.reshape(token_count, width)
    feed_cotangent = gather_tokens(upstream_tokens)

    own_places = seq_place * frame_count + jnp.arange(frame_count, dtype=jnp.int32)
    key_order = masks_of(seq_masks)
    key_places = jnp.concatenate(
        [(seq_place ^ k) * frame_count + jnp.arange(frame_count, dtype=jnp.int32) for k in key_order]
    )
    own_clip, own_offset = clip_tables(clip_frames, own_places)
    key_clip = clip_tables(clip_frames, key_places)[0]
    visible = own_clip[:, None, :, None] == key_clip[:, None, None, :]
    prompt_turned = jnp.concatenate(
        [
            lax.dynamic_slice_in_dim(prompt, (seq_place ^ k) * memory_share, memory_share, 1)
            for k in key_order
        ],
        1,
    )
    prompt_flat = prompt_turned.reshape(-1, prompt.shape[2])

    def split_heads(value):
        return value.reshape(row_count, -1, heads, HEAD_DIM)

    inputs = widen(frames).reshape(token_count, width)
    normed_one, inverse_one = standardize(inputs)
    hidden_one = narrow(normed_one * gain_one + shift_one)
    triple = dot(hidden_one, triple_low)
    query = narrow(turn(split_heads(triple[:, :width]), own_offset, 1.0) * scale)
    own_keys = narrow(turn(split_heads(triple[:, width : 2 * width]), own_offset, 1.0))
    own_values = narrow(triple[:, 2 * width :])
    pairs = jnp.concatenate([own_keys.reshape(token_count, width), own_values], 1)
    pairs = pairs.reshape(1, row_count, frame_count, 2 * width)
    pairs = gather(pairs, seq_masks)
    pairs = jnp.transpose(pairs, (1, 0, 2, 3)).reshape(row_count, row_length, 2, heads, HEAD_DIM)
    all_keys = pairs[:, :, 0]
    all_values = pairs[:, :, 1]
    scores = jnp.where(visible, mult(query, all_keys, "rqhd,rkhd->rhqk"), NEG)
    probs = jax.nn.softmax(scores, -1)
    self_mixed = narrow(mult(narrow(probs), all_values, "rhqk,rkhd->rqhd"))
    self_mixed = self_mixed.reshape(token_count, width)
    after_self = inputs + dot(self_mixed, self_low)
    normed_two, inverse_two = standardize(after_self)
    hidden_two = narrow(normed_two * gain_two + shift_two)
    asking = split_heads(narrow(dot(hidden_two, ask_low) * scale))
    memory = narrow(dot(prompt_flat, memory_low)).reshape(
        row_count, memory_count, 2, heads, HEAD_DIM
    )
    memory_keys = memory[:, :, 0]
    memory_values = memory[:, :, 1]
    cross_probs = jax.nn.softmax(mult(asking, memory_keys, "rqhd,rkhd->rhqk"), -1)
    cross_mixed = narrow(mult(narrow(cross_probs), memory_values, "rhqk,rkhd->rqhd"))
    cross_mixed = cross_mixed.reshape(token_count, width)
    after_cross = after_self + dot(cross_mixed, cross_low)
    normed_three, inverse_three = standardize(after_cross)
    hidden_three = narrow(normed_three * gain_three + shift_three)

    feed_rows = gather_tokens(hidden_three)
    group_count = len(masks_of(token_orders[0]))
    starts = [group_count * cut for cut in cuts]
    middle_grad = widen(narrow(dot_t(feed_cotangent, drop_low)))
    lifted = dot_t(feed_rows, lift_low) + lift_bias
    value_part = lifted[:, :unit_count]
    gate_part = lifted[:, unit_count:]
    sigma = jax.nn.sigmoid(gate_part)
    middle = narrow(value_part * gate_part * sigma)
    lift_grad = narrow(
        jnp.concatenate(
            [
                middle_grad * gate_part * sigma,
                middle_grad * value_part * sigma * (1.0 + gate_part * (1.0 - sigma)),
            ],
            1,
        )
    )

    def scatter_tokens(rows, weight):
        sums = []
        for p in range(3):
            part = rows[starts[p] : starts[p + 1]]
            make = lambda start, size, part=part: dot(part[start : start + size], weight)
            sums.append(scatter_made(make, part.shape[0], token_orders[p]))
        return jnp.concatenate(sums, 0)

    feed_back = scatter_tokens(lift_grad, lift_low)
    feed_term = scatter_tokens(middle, drop_low)
    layer_output = after_cross + feed_term + drop_bias

    def shed_units(make, lift):
        spans = [make(k) for k in range(1 << len(far))]
        for mask in reversed(far):
            half = len(spans) // 2
            got = [hop(span if lift else narrow(span), mask) for span in spans[half:]]
            spans = [a + widen(b) for a, b in zip(spans[:half], got)]
        return spans[0]

    units = feed_output.shape[0]
    wide_grad = lift_grad.reshape(-1, 2, unit_count)

    def lift_rows(k):
        rows = wide_grad[:, :, k * units : (k + 1) * units]
        return tdot(rows.reshape(-1, 2 * units), feed_rows)

    def drop_rows(k):
        return tdot(middle[:, k * units : (k + 1) * units], feed_cotangent)

    def bias_rows(k):
        return jnp.sum(widen(wide_grad[:, :, k * units : (k + 1) * units]), 0)

    grad_lift = shed_units(lift_rows, False).reshape(2, units, width)
    grad_drop = shed_units(drop_rows, False)
    grad_lift_bias = shed_units(bias_rows, True)

    matrix = order_matrix(width, order, me)

    def weight_grad(rows, grads):
        return scatter_weight(narrow(dot(rows, matrix)), grads, batch_masks, seq_masks)

    outer_grad = widen(upstream_tokens)
    grad_drop_bias = jnp.sum(outer_grad, 0)
    back_three, grad_gain_three, grad_shift_three = norm_back(
        feed_back, normed_three, inverse_three, gain_three
    )
    cross_out_grad = outer_grad + back_three
    cross_branch = narrow(cross_out_grad)
    cross_mixed_grad = split_heads(narrow(dot_t(cross_branch, cross_low)))
    grad_cross = weight_grad(cross_mixed, cross_branch)
    cross_score_grad = narrow(
        softmax_back(cross_probs, mult(cross_mixed_grad, memory_values, "rqhd,rkhd->rhqk"))
    )
    asking_grad = narrow(
        (mult(cross_score_grad, memory_keys, "rhqk,rkhd->rqhd") * scale).reshape(token_count, width)
    )
    memory_key_grad = mult(cross_score_grad, asking, "rhqk,rqhd->rkhd")
    memory_value_grad = mult(narrow(cross_probs), cross_mixed_grad, "rhqk,rqhd->rkhd")
    memory_grad = narrow(
        jnp.stack([memory_key_grad, memory_value_grad], 2).reshape(row_count, memory_count, 2 * width)
    )
    back_two, grad_gain_two, grad_shift_two = norm_back(
        dot_t(asking_grad, ask_low), normed_two, inverse_two, gain_two
    )
    grad_ask = weight_grad(hidden_two, asking_grad)

    def shed_frames(value):
        value = value.reshape(row_count, seq_count, -1, value.shape[-1])
        for mask in reversed(seq_masks):
            half = value.shape[1] // 2
            value = widen(value[:, :half]) + widen(hop(narrow(value[:, half:]), mask))
        return value.reshape(-1, value.shape[-1])

    memory_own = narrow(shed_frames(memory_grad))
    prompt_own = prompt_flat.reshape(row_count, memory_count, -1)[:, :memory_share]
    prompt_own = prompt_own.reshape(-1, prompt.shape[2])
    prompt_own = narrow(dot(prompt_own, order_matrix(prompt.shape[2], order, me)))
    grad_memory = scatter_weight(prompt_own, memory_own, batch_masks, seq_masks)
    self_out_grad = cross_out_grad + back_two
    self_branch = narrow(self_out_grad)
    self_mixed_grad = split_heads(narrow(dot_t(self_branch, self_low)))
    grad_self = weight_grad(self_mixed, self_branch)
    score_grad = narrow(softmax_back(probs, mult(self_mixed_grad, all_values, "rqhd,rkhd->rhqk")))
    query_grad = mult(score_grad, all_keys, "rhqk,rkhd->rqhd") * scale
    key_grad = mult(score_grad, query, "rhqk,rqhd->rkhd")
    value_grad = mult(narrow(probs), self_mixed_grad, "rhqk,rqhd->rkhd")
    pair_grad = narrow(
        jnp.stack([key_grad, value_grad], 2).reshape(row_count, row_length, 2 * width)
    )
    own_pair_grad = shed_frames(pair_grad)
    query_back = narrow(turn(query_grad, own_offset, -1.0)).reshape(token_count, width)
    key_back = narrow(turn(split_heads(own_pair_grad[:, :width]), own_offset, -1.0))
    key_back = key_back.reshape(token_count, width)
    value_back = narrow(own_pair_grad[:, width:])
    triple_back = jnp.concatenate([query_back, key_back, value_back], 1)
    back_hidden = dot_t(triple_back, triple_low)
    back_one, grad_gain_one, grad_shift_one = norm_back(
        back_hidden, normed_one, inverse_one, gain_one
    )
    grad_triple = weight_grad(hidden_one, triple_back)
    frame_grad = self_out_grad + back_one

    sums = jnp.stack(
        [
            grad_gain_one,
            grad_shift_one,
            grad_gain_two,
            grad_shift_two,
            grad_gain_three,
            grad_shift_three,
            grad_drop_bias,
        ],
        0,
    ).reshape(7, device_count, share)
    sums = jnp.transpose(sums, (1, 0, 2)).reshape(device_count, 7 * share)
    sums = jnp.pad(sums, ((0, 0), (0, 1024 - 7 * share)))
    sums = jnp.take(sums, me ^ jnp.asarray(np.array(masks_of(order), np.int32)), axis=0)
    sums = sums.reshape(device_count, 8, 128)
    for mask in reversed(order):
        half = sums.shape[0] // 2
        sums = sums[:half] + hop(sums[half:], mask)
    sums = sums.reshape(1024)[: 7 * share].reshape(7, share)

    shape = frames.shape
    return (
        narrow(layer_output).reshape(shape),
        frame_grad.reshape(shape),
        sums[0],
        sums[1],
        grad_triple,
        grad_self,
        sums[2],
        sums[3],
        grad_ask,
        grad_memory,
        grad_cross,
        sums[4],
        sums[5],
        grad_lift,
        grad_lift_bias,
        grad_drop,
        sums[6],
    )


def solution(mesh):
    both = P(AX)
    wide = P(AX, None)
    rows = P(B, S, None)
    units = P(None, AX, None)
    in_specs = (
        rows,
        P(B, None, None),
        P(B, None),
        rows,
        both,
        both,
        wide,
        wide,
        both,
        both,
        wide,
        wide,
        wide,
        both,
        both,
        units,
        P(None, AX),
        wide,
        both,
    )
    out_specs = (
        rows,
        rows,
        both,
        both,
        wide,
        wide,
        both,
        both,
        wide,
        wide,
        wide,
        both,
        both,
        units,
        P(None, AX),
        wide,
        both,
    )
    return jax.shard_map(local, mesh=mesh, in_specs=in_specs, out_specs=out_specs, check_vma=False)
```

profile of v0, /device:TPU:0, one launch (start us, length us, event | category | flops | bytes accessed | tf_op | source)
XLA Modules:
  0.0 901.4 jit_solution(18125143536583763654)
XLA Ops:
  35.9 6.8 collective-permute-done.53
  43.3 14.5 %collective-permute-done = bf16[48,4736]{1,0:T(8,128)(2,1)S(1)} collective-permute-done((bf16[48,4736]{1,0:T(8,128)(2,1)}, bf16[48,4736]{1,0:T(8,128)(2,1)S(1)}, u32[]{:S(2)}, u32[]{:S(2)}) %collective-permute-start) | collective-permute-done | bytes 454688 | tf_op jit(solution)/shard_map/ppermute | solution.py:82
  60.9 28.9 %collective-permute-done.1 = bf16[96,4736]{1,0:T(8,128)(2,1)S(1)} collective-permute-done((bf16[96,4736]{1,0:T(8,128)(2,1)S(1)}, bf16[96,4736]{1,0:T(8,128)(2,1)S(1)}, u32[]{:S(2)}, u32[]{:S(2)}) %collective-permute-start.1) | collective-permute-done | bytes 909344 | tf_op jit(solution)/shard_map/ppermute | solution.py:82
  93.2 15.4 %collective-permute-done.6 = bf16[192,2304]{1,0:T(8,128)(2,1)S(1)} collective-permute-done((bf16[192,2304]{1,0:T(8,128)(2,1)S(1)}, bf16[192,2304]{1,0:T(8,128)(2,1)S(1)}, u32[]{:S(2)}, u32[]{:S(2)}) %collective-permute-start.6) | collective-permute-done | bytes 884768 | tf_op jit(solution)/shard_map/ppermute | solution.py:82
  121.9 30.4 %collective-permute-done.7.refs_5_ = bf16[384,2304]{1,0:T(8,128)(2,1)S(1)} collective-permute-done((bf16[384,2304]{1,0:T(8,128)(2,1)S(1)}, bf16[384,2304]{1,0:T(8,128)(2,1)S(1)}, u32[]{:S(2)}, u32[]{:S(2)}) %collective-permute-start.7) | collective-permute-done | bytes 1769504 | tf_op jit(solution)/shard_map/ppermute | solution.py:82
  153.6 21.1 %collective-permute-done.13 = bf16[192,3072]{1,0:T(8,128)(2,1)S(1)} collective-permute-done((bf16[192,3072]{1,0:T(8,128)(2,1)S(1)}, bf16[192,3072]{1,0:T(8,128)(2,1)S(1)}, u32[]{:S(2)}, u32[]{:S(2)}) %collective-permute-start.13) | collective-permute-done | bytes 1179680 | tf_op jit(solution)/shard_map/ppermute | solution.py:82
  177.8 22.0 %collective-permute-done.17 = bf16[192,3072]{1,0:T(8,128)(2,1)S(1)} collective-permute-done((bf16[192,3072]{1,0:T(8,128)(2,1)S(1)}, bf16[192,3072]{1,0:T(8,128)(2,1)S(1)}, u32[]{:S(2)}, u32[]{:S(2)}) %collective-permute-start.17) | collective-permute-done | bytes 1179680 | tf_op jit(solution)/shard_map/ppermute | solution.py:82
  208.0 6.7 shard_map.341
  239.7 11.9 %collective-permute-done.34 = bf16[2,192]{1,0:T(2,128)(2,1)} collective-permute-done((bf16[2,192]{1,0:T(2,128)(2,1)}, bf16[2,192]{1,0:T(2,128)(2,1)}, u32[]{:S(2)}, u32[]{:S(2)}) %collective-permute-start.34) | collective-permute-done | bytes 800 | tf_op jit(solution)/shard_map/ppermute | solution.py:82
  289.1 8.4 fusion.38
  303.1 9.1 %shard_map.342 = (bf16[1536,1536]{1,0:T(8,128)(2,1)S(1)}, bf16[1536,1536]{1,0:T(8,128)(2,1)S(1)}, bf16[1536,1536]{1,0:T(8,128)(2,1)S(1)}, bf16[1536,1536]{1,0:T(8,128)(2,1)}) custom-call(s32[1]{0:T(128)} %bitcast.1.me_ref, bf16[384,3072]{1,0:T(8,128)(2,1)S(1)} %pad_maximum_fusion.1.refs_0_, bf16[384,3072]{1,0:T(8,128)(2,1)} %collective-permute-done.14.refs_1_, ...), custom_call_target="tpu_custom_call" | custom-call | bytes 37748736 | tf_op jit(solution)/shard_map/pallas_call | solution.py:177
  383.9 9.9 %collective-permute-done.27 = bf16[192,1536]{1,0:T(8,128)(2,1)S(1)} collective-permute-done((bf16[192,1536]{1,0:T(8,128)(2,1)S(1)}, bf16[192,1536]{1,0:T(8,128)(2,1)S(1)}, u32[]{:S(2)}, u32[]{:S(2)}) %collective-permute-start.27) | collective-permute-done | bytes 589856 | tf_op jit(solution)/shard_map/ppermute | solution.py:82
  452.2 39.6 %collective-permute-done.115 = f32[2,192]{1,0:T(2,128)S(1)} collective-permute-done((f32[2,192]{1,0:T(2,128)S(1)}, f32[2,192]{1,0:T(2,128)S(1)}, u32[]{:S(2)}, u32[]{:S(2)}) %collective-permute-start.115) | collective-permute-done | bytes 1568 | tf_op jit(solution)/shard_map/ppermute | solution.py:82
  504.6 12.5 %collective-permute-done.114 = bf16[384,1536]{1,0:T(8,128)(2,1)S(1)} collective-permute-done((bf16[384,1536]{1,0:T(8,128)(2,1)S(1)}, bf16[384,1536]{1,0:T(8,128)(2,1)S(1)}, u32[]{:S(2)}, u32[]{:S(2)}) %collective-permute-start.114) | collective-permute-done | bytes 1179680 | tf_op jit(solution)/shard_map/ppermute | solution.py:82
  528.5 24.7 %collective-permute-done.46 = bf16[64,1536]{1,0:T(8,128)(2,1)S(1)} collective-permute-done((bf16[64,1536]{1,0:T(8,128)(2,1)S(1)}, bf16[64,1536]{1,0:T(8,128)(2,1)S(1)}, u32[]{:S(2)}, u32[]{:S(2)}) %collective-permute-start.46) | collective-permute-done | bytes 196640 | tf_op jit(solution)/shard_map/ppermute | solution.py:82
  630.4 8.5 fusion.41
  684.5 10.8 %multiply_reduce_fusion.4 = (f32[1536]{0:T(1024)S(1)}, f32[128]{0:T(128)S(1)}, f32[128]{0:T(128)S(1)}, f32[1536]{0:T(1024)S(1)}, f32[128,1536]{1,0:T(8,128)}) fusion(bf16[2,64,1536]{2,1,0:T(8,128)(2,1)S(1)} %copy-done.8, f32[128]{0:T(128)S(1)} %copy-done.94, f32[128]{0:T(128)S(1)} %copy-done.92, f32[1536]{0:T(1024)S(1)} %copy-done.75, ...), kind=kOutput, calls=%fused_computation.233 | convolution fusion | flops 1817441024 | bytes 16535552 | tf_op jit(solution)/shard_map/dot_general | solution.py:34
  728.5 6.4 collective-permute-done.108
  738.8 8.7 collective-permute-done.93
  783.5 6.4 collective-permute-done.112
  813.9 36.8 %collective-permute-done.102 = bf16[96,1536]{1,0:T(8,128)(2,1)S(1)} collective-permute-done((bf16[96,1536]{1,0:T(8,128)(2,1)S(1)}, bf16[96,1536]{1,0:T(8,128)(2,1)S(1)}, u32[]{:S(2)}, u32[]{:S(2)}) %collective-permute-start.102) | collective-permute-done | bytes 294944 | tf_op jit(solution)/shard_map/ppermute | solution.py:82
  856.4 8.5 collective-permute-done.80
  870.9 15.4 %collective-permute-done.83 = bf16[96,4608]{1,0:T(8,128)(2,1)S(1)} collective-permute-done((bf16[96,4608]{1,0:T(8,128)(2,1)S(1)}, bf16[96,4608]{1,0:T(8,128)(2,1)S(1)}, u32[]{:S(2)}, u32[]{:S(2)}) %collective-permute-start.83) | collective-permute-done | bytes 884768 | tf_op jit(solution)/shard_map/ppermute | solution.py:82
  887.9 12.2 %collective-permute-done.84 = bf16[48,4608]{1,0:T(8,128)(2,1)S(1)} collective-permute-done((bf16[48,4608]{1,0:T(8,128)(2,1)S(1)}, bf16[48,4608]{1,0:T(8,128)(2,1)S(1)}, u32[]{:S(2)}, u32[]{:S(2)}) %collective-permute-start.84) | collective-permute-done | bytes 442400 | tf_op jit(solution)/shard_map/ppermute | solution.py:82
  (795 shorter events, 522.0 us)
Async XLA Ops:
  34.3 57.0 %collective-permute-start.50 = (bf16[192,1536]{1,0:T(8,128)(2,1)S(1)}, bf16[192,1536]{1,0:T(8,128)(2,1)S(1)}, u32[]{:S(2)}, u32[]{:S(2)}) collective-permute-start(bf16[192,1536]{1,0:T(8,128)(2,1)S(1)} %pad_maximum_fusion.29), channel_id=1, source_target_pairs={{0,8},{1,9},{2,10},{3,11},{4,12},{5,13},{6,14},{7,15},{8,0},{9,1},... | collective-permute-start | bytes 1769480 | tf_op jit(solution)/shard_map/ppermute | solution.py:82
  59.5 55.1 %collective-permute-start.12 = (bf16[96,6144]{1,0:T(8,128)(2,1)S(1)}, bf16[96,6144]{1,0:T(8,128)(2,1)S(1)}, u32[]{:S(2)}, u32[]{:S(2)}) collective-permute-start(bf16[96,6144]{1,0:T(8,128)(2,1)S(1)} %pad_maximum_fusion.10), channel_id=1, source_target_pairs={{0,8},{1,9},{2,10},{3,11},{4,12},{5,13},{6,14},{7,15},{8,0},{9,1},... | collective-permute-start | bytes 3538952 | tf_op jit(solution)/shard_map/ppermute | solution.py:82
  118.4 56.2 %collective-permute-start.13 = (bf16[192,3072]{1,0:T(8,128)(2,1)S(1)}, bf16[192,3072]{1,0:T(8,128)(2,1)S(1)}, u32[]{:S(2)}, u32[]{:S(2)}) collective-permute-start(bf16[192,3072]{1,0:T(8,128)(2,1)S(1)} %get-tuple-element.89), channel_id=1, source_target_pairs={{0,2},{1,3},{2,0},{3,1},{4,6},{5,7},{6,4},{7,5},{8,10},{9,11},{10,... | collective-permute-start | bytes 3538952 | tf_op jit(solution)/shard_map/ppermute | solution.py:82
  121.4 83.0 %collective-permute-start.8 = (bf16[384,2304]{1,0:T(8,128)(2,1)S(1)}, bf16[384,2304]{1,0:T(8,128)(2,1)S(1)}, u32[]{:S(2)}, u32[]{:S(2)}) collective-permute-start(bf16[384,2304]{1,0:T(8,128)(2,1)S(1)} %pad_maximum_fusion.6.refs_4_), channel_id=1, source_target_pairs={{0,1},{1,0},{2,3},{3,2},{4,5},{5,4},{6,7},{7,6},{8,9},{9,8},{10,11... | collective-permute-start | bytes 5308424 | tf_op jit(solution)/shard_map/ppermute | solution.py:82
  121.4 83.0 %collective-permute-start.4 = (bf16[384,2432]{1,0:T(8,128)(2,1)S(1)}, bf16[384,2432]{1,0:T(8,128)(2,1)S(1)}, u32[]{:S(2)}, u32[]{:S(2)}) collective-permute-start(bf16[384,2432]{1,0:T(8,128)(2,1)S(1)} %pad_maximum_fusion.4.refs_0_), channel_id=1, source_target_pairs={{0,1},{1,0},{2,3},{3,2},{4,5},{5,4},{6,7},{7,6},{8,9},{9,8},{10,11... | collective-permute-start | bytes 5603336 | tf_op jit(solution)/shard_map/ppermute | solution.py:82
  152.3 54.7 %collective-permute-start.9 = (bf16[384,2304]{1,0:T(8,128)(2,1)S(1)}, bf16[384,2304]{1,0:T(8,128)(2,1)S(1)}, u32[]{:S(2)}, u32[]{:S(2)}) collective-permute-start(bf16[384,2304]{1,0:T(8,128)(2,1)S(1)} %collective-permute-done.7.refs_5_), channel_id=1, source_target_pairs={{0,1},{1,0},{2,3},{3,2},{4,5},{5,4},{6,7},{7,6},{8,9},{9,8},{10,11... | collective-permute-start | bytes 5308424 | tf_op jit(solution)/shard_map/ppermute | solution.py:82
  152.3 55.2 %collective-permute-start.5 = (bf16[384,2432]{1,0:T(8,128)(2,1)S(1)}, bf16[384,2432]{1,0:T(8,128)(2,1)S(1)}, u32[]{:S(2)}, u32[]{:S(2)}) collective-permute-start(bf16[384,2432]{1,0:T(8,128)(2,1)S(1)} %collective-permute-done.3.refs_1_), channel_id=1, source_target_pairs={{0,1},{1,0},{2,3},{3,2},{4,5},{5,4},{6,7},{7,6},{8,9},{9,8},{10,11... | collective-permute-start | bytes 5603336 | tf_op jit(solution)/shard_map/ppermute | solution.py:82
  199.7 55.2 %collective-permute-start.33 = (bf16[2,192,1536]{2,1,0:T(8,128)(2,1)}, bf16[2,192,1536]{2,1,0:T(8,128)(2,1)}, u32[]{:S(2)}, u32[]{:S(2)}) collective-permute-start(bf16[2,192,1536]{2,1,0:T(8,128)(2,1)} %convert_element_type.692), channel_id=1, source_target_pairs={{0,16},{1,17},{2,18},{3,19},{4,20},{5,21},{6,22},{7,23},{8,24},{9,... | collective-permute-start | bytes 3538952 | tf_op jit(solution)/shard_map/ppermute | solution.py:82
  204.4 51.0 %collective-permute-start.56 = (bf16[32,1536]{1,0:T(8,128)(2,1)}, bf16[32,1536]{1,0:T(8,128)(2,1)}, u32[]{:S(2)}, u32[]{:S(2)}) collective-permute-start(bf16[32,1536]{1,0:T(8,128)(2,1)} %get-tuple-element.102), channel_id=1, source_target_pairs={{0,8},{1,9},{2,10},{3,11},{4,12},{5,13},{6,14},{7,15},{8,0},{9,1},... | collective-permute-start | bytes 294920 | tf_op jit(solution)/shard_map/ppermute | solution.py:82
  265.0 164.1 %collective-permute-start.35 = (bf16[192,1536]{1,0:T(8,128)(2,1)S(1)}, bf16[192,1536]{1,0:T(8,128)(2,1)}, u32[]{:S(2)}, u32[]{:S(2)}) collective-permute-start(bf16[192,1536]{1,0:T(8,128)(2,1)S(1)} %convert_element_type.696), channel_id=1, source_target_pairs={{0,16},{1,17},{2,18},{3,19},{4,20},{5,21},{6,22},{7,23},{8,24},{9,... | collective-permute-start | bytes 1769480 | tf_op jit(solution)/shard_map/ppermute | solution.py:82
  302.5 58.8 %collective-permute-start.57 = (bf16[64,1536]{1,0:T(8,128)(2,1)}, bf16[64,1536]{1,0:T(8,128)(2,1)S(1)}, u32[]{:S(2)}, u32[]{:S(2)}) collective-permute-start(bf16[64,1536]{1,0:T(8,128)(2,1)} %pad_maximum_fusion.46), channel_id=1, source_target_pairs={{0,2},{1,3},{2,0},{3,1},{4,6},{5,7},{6,4},{7,5},{8,10},{9,11},{10,... | collective-permute-start | bytes 589832 | tf_op jit(solution)/shard_map/ppermute | solution.py:82
  437.2 55.3 %collective-permute-start.116 = (bf16[192,1536]{1,0:T(8,128)(2,1)S(1)}, bf16[192,1536]{1,0:T(8,128)(2,1)S(1)}, u32[]{:S(2)}, u32[]{:S(2)}) collective-permute-start(bf16[192,1536]{1,0:T(8,128)(2,1)S(1)} %convolution_convert_fusion.18), channel_id=1, source_target_pairs={{0,16},{1,17},{2,18},{3,19},{4,20},{5,21},{6,22},{7,23},{8,24},{9,... | collective-permute-start | bytes 1769480 | tf_op jit(solution)/shard_map/ppermute | solution.py:82
  438.3 53.5 %collective-permute-start.115 = (f32[2,192]{1,0:T(2,128)S(1)}, f32[2,192]{1,0:T(2,128)S(1)}, u32[]{:S(2)}, u32[]{:S(2)}) collective-permute-start(f32[2,192]{1,0:T(2,128)S(1)} %get-tuple-element.49), channel_id=1, source_target_pairs={{0,16},{1,17},{2,18},{3,19},{4,20},{5,21},{6,22},{7,23},{8,24},{9,... | collective-permute-start | bytes 4616 | tf_op jit(solution)/shard_map/ppermute | solution.py:82
  443.6 73.5 %collective-permute-start.114 = (bf16[384,1536]{1,0:T(8,128)(2,1)S(1)}, bf16[384,1536]{1,0:T(8,128)(2,1)S(1)}, u32[]{:S(2)}, u32[]{:S(2)}) collective-permute-start(bf16[384,1536]{1,0:T(8,128)(2,1)S(1)} %convolution_convert_fusion.10), channel_id=1, source_target_pairs={{0,16},{1,17},{2,18},{3,19},{4,20},{5,21},{6,22},{7,23},{8,24},{9,... | collective-permute-start | bytes 3538952 | tf_op jit(solution)/shard_map/ppermute | solution.py:82
  445.9 52.6 %collective-permute-start.36 = (bf16[384,1536]{1,0:T(8,128)(2,1)S(1)}, bf16[384,1536]{1,0:T(8,128)(2,1)S(1)}, u32[]{:S(2)}, u32[]{:S(2)}) collective-permute-start(bf16[384,1536]{1,0:T(8,128)(2,1)S(1)} %convolution_convert_fusion.15), channel_id=1, source_target_pairs={{0,1},{1,0},{2,3},{3,2},{4,5},{5,4},{6,7},{7,6},{8,9},{9,8},{10,11... | collective-permute-start | bytes 3538952 | tf_op jit(solution)/shard_map/ppermute | solution.py:82
  517.1 51.8 %collective-permute-start.37 = (bf16[192,1536]{1,0:T(8,128)(2,1)S(1)}, bf16[192,1536]{1,0:T(8,128)(2,1)S(1)}, u32[]{:S(2)}, u32[]{:S(2)}) collective-permute-start(bf16[192,1536]{1,0:T(8,128)(2,1)S(1)} %slice.1268), channel_id=1, source_target_pairs={{0,8},{1,9},{2,10},{3,11},{4,12},{5,13},{6,14},{7,15},{8,0},{9,1},... | collective-permute-start | bytes 1769480 | tf_op jit(solution)/shard_map/ppermute | solution.py:82
  522.9 51.0 %collective-permute-start.61 = (bf16[192,1536]{1,0:T(8,128)(2,1)S(1)}, bf16[192,1536]{1,0:T(8,128)(2,1)S(1)}, u32[]{:S(2)}, u32[]{:S(2)}) collective-permute-start(bf16[192,1536]{1,0:T(8,128)(2,1)S(1)} %slice.1266), channel_id=1, source_target_pairs={{0,8},{1,9},{2,10},{3,11},{4,12},{5,13},{6,14},{7,15},{8,0},{9,1},... | collective-permute-start | bytes 1769480 | tf_op jit(solution)/shard_map/ppermute | solution.py:82
  604.6 111.9 %collective-permute-start.107 = (bf16[768,1536]{1,0:T(8,128)(2,1)}, bf16[768,1536]{1,0:T(8,128)(2,1)}, u32[]{:S(2)}, u32[]{:S(2)}) collective-permute-start(bf16[768,1536]{1,0:T(8,128)(2,1)} %convolution_convert_fusion.4), channel_id=1, source_target_pairs={{0,1},{1,0},{2,3},{3,2},{4,5},{5,4},{6,7},{7,6},{8,9},{9,8},{10,11... | collective-permute-start | bytes 7077896 | tf_op jit(solution)/shard_map/ppermute | solution.py:82
  618.3 79.0 %collective-permute-start.99 = (bf16[2,1,64,3072]{3,2,1,0:T(8,128)(2,1)}, bf16[2,1,64,3072]{3,2,1,0:T(8,128)(2,1)}, u32[]{:S(2)}, u32[]{:S(2)}) collective-permute-start(bf16[2,1,64,3072]{3,2,1,0:T(8,128)(2,1)} %slice.950), channel_id=1, source_target_pairs={{0,1},{1,0},{2,3},{3,2},{4,5},{5,4},{6,7},{7,6},{8,9},{9,8},{10,11... | collective-permute-start | bytes 2359304 | tf_op jit(solution)/shard_map/ppermute | solution.py:82
  626.4 95.8 %collective-permute-start.92 = (bf16[768,1536]{1,0:T(8,128)(2,1)}, bf16[768,1536]{1,0:T(8,128)(2,1)}, u32[]{:S(2)}, u32[]{:S(2)}) collective-permute-start(bf16[768,1536]{1,0:T(8,128)(2,1)} %convolution_convert_fusion.6), channel_id=1, source_target_pairs={{0,1},{1,0},{2,3},{3,2},{4,5},{5,4},{6,7},{7,6},{8,9},{9,8},{10,11... | collective-permute-start | bytes 7077896 | tf_op jit(solution)/shard_map/ppermute | solution.py:82
  661.1 63.6 %collective-permute-start.85 = (bf16[768,1536]{1,0:T(8,128)(2,1)}, bf16[768,1536]{1,0:T(8,128)(2,1)}, u32[]{:S(2)}, u32[]{:S(2)}) collective-permute-start(bf16[768,1536]{1,0:T(8,128)(2,1)} %convolution_convert_fusion.8), channel_id=1, source_target_pairs={{0,1},{1,0},{2,3},{3,2},{4,5},{5,4},{6,7},{7,6},{8,9},{9,8},{10,11... | collective-permute-start | bytes 7077896 | tf_op jit(solution)/shard_map/ppermute | solution.py:82
  699.7 64.5 %collective-permute-start.100 = (bf16[384,3072]{1,0:T(8,128)(2,1)S(1)}, bf16[384,3072]{1,0:T(8,128)(2,1)S(1)}, u32[]{:S(2)}, u32[]{:S(2)}) collective-permute-start(bf16[384,3072]{1,0:T(8,128)(2,1)S(1)} %convolution_convert_fusion.2), channel_id=1, source_target_pairs={{0,1},{1,0},{2,3},{3,2},{4,5},{5,4},{6,7},{7,6},{8,9},{9,8},{10,11... | collective-permute-start | bytes 7077896 | tf_op jit(solution)/shard_map/ppermute | solution.py:82
  747.6 58.9 %collective-permute-start.78 = (bf16[768,4608]{1,0:T(8,128)(2,1)S(1)}, bf16[768,4608]{1,0:T(8,128)(2,1)S(1)}, u32[]{:S(2)}, u32[]{:S(2)}) collective-permute-start(bf16[768,4608]{1,0:T(8,128)(2,1)S(1)} %convolution_convert_fusion), channel_id=1, source_target_pairs={{0,1},{1,0},{2,3},{3,2},{4,5},{5,4},{6,7},{7,6},{8,9},{9,8},{10,11... | collective-permute-start | bytes 21233672 | tf_op jit(solution)/shard_map/ppermute | solution.py:82
  802.2 66.6 %collective-permute-start.91 = (bf16[48,1536]{1,0:T(8,128)(2,1)S(1)}, bf16[48,1536]{1,0:T(8,128)(2,1)S(1)}, u32[]{:S(2)}, u32[]{:S(2)}) collective-permute-start(bf16[48,1536]{1,0:T(8,128)(2,1)S(1)} %slice.1283), channel_id=1, source_target_pairs={{0,16},{1,17},{2,18},{3,19},{4,20},{5,21},{6,22},{7,23},{8,24},{9,... | collective-permute-start | bytes 442376 | tf_op jit(solution)/shard_map/ppermute | solution.py:82
  (205 other events, 3259.7 us)
where the time goes:
time: 907 us; the launch traced here: 901 us
  waiting for transfers between devices  436 us (48%)
  local copies, waits for them, and re-layouts  139 us (15%)
  matrix products  135 us (15%)
  starting transfers between devices  106 us (12%)
  other arithmetic  65.1 us (7%)
  Pallas kernels  15.8 us (2%)
    ppermute x117, waiting for transfers between devices, hop(): return lax.ppermute(value, AX, [(i, i ^ mask) for i in range(count)])  436 us
    ppermute x117, starting transfers between devices, hop(): return lax.ppermute(value, AX, [(i, i ^ mask) for i in range(count)])  106 us
    dot_general x22, matrix products, dot(): lax.dot_general(left, right, (((1,), (0,)), ((), ())), preferred_element_...  40.3 us
    unnamed x255, local copies, waits for them, and re-layouts  36.6 us
    dot_general x11, matrix products, mult(): return jnp.einsum(form, left, right, preferred_element_type=jnp.float32)  33.7 us
    dot_general x14, matrix products, tdot(): lax.dot_general(left, right, (((0,), (0,)), ((), ())), preferred_element_...  30.2 us
    dot_general x6, matrix products, dot_t(): lax.dot_general(left, right, (((1,), (1,)), ((), ())), preferred_element_...  28.2 us
    convert_element_type x9, local copies, waits for them, and re-layouts, narrow(): return value.astype(jnp.bfloat16)  22 us
  transfers between devices with their start and end apart: 117, of which 55 were waited for; matrix products, arithmetic and copies ran while one was open for 33% of the time, Pallas kernels for 2%

commit v1 on v0

v1 whole, which is shorter than its diff:
```python
import jax
import jax.numpy as jnp
import numpy as np
from jax import lax
from jax.experimental import pallas as pl
from jax.experimental.pallas import tpu as pltpu
from jax.sharding import PartitionSpec as P

HEAD_DIM = 64
LANES = 512
UNITS = ["unit0", "unit1", "unit2", "unit3", "unit4", "unit5"]
EPS = 1e-05
NEG = -1e30
B = "batch"
S = "seq"
AX = (B, S)


def narrow(value):
    return value.astype(jnp.bfloat16)


def widen(value):
    return value.astype(jnp.float32)


def mult(left, right, form):
    return jnp.einsum(form, left, right, preferred_element_type=jnp.float32)


def dot(left, right):
    return lax.dot_general(left, right, (((1,), (0,)), ((), ())), preferred_element_type=jnp.float32)


def dot_t(left, right):
    return lax.dot_general(left, right, (((1,), (1,)), ((), ())), preferred_element_type=jnp.float32)


def tdot(left, right):
    return lax.dot_general(left, right, (((0,), (0,)), ((), ())), preferred_element_type=jnp.float32)


def standardize(values):
    center = values - jnp.mean(values, -1, keepdims=True)
    inverse = lax.rsqrt(jnp.mean(center * center, -1, keepdims=True) + EPS)
    return (center * inverse, inverse)


def norm_back(incoming, normed, inverse, gain):
    scaled = incoming * gain
    inner = (
        scaled
        - jnp.mean(scaled, -1, keepdims=True)
        - normed * jnp.mean(scaled * normed, -1, keepdims=True)
    )
    return (
        inner * inverse,
        jnp.sum(incoming * normed, 0, keepdims=True),
        jnp.sum(incoming, 0, keepdims=True),
    )


def clip_tables(lengths, places):
    ends = jnp.cumsum(lengths, 1)
    later = places[None, :, None] >= ends[:, None, :]
    ident = jnp.sum(later.astype(jnp.int32), 2)
    starts = jnp.max(jnp.where(later, ends[:, None, :], 0), 2)
    return (ident, places[None, :] - starts)


def softmax_back(probs, prob_grad):
    return probs * (prob_grad - jnp.sum(probs * prob_grad, -1, keepdims=True))


def hop(value, mask):
    count = lax.axis_size(B) * lax.axis_size(S)
    return lax.ppermute(value, AX, [(i, i ^ mask) for i in range(count)])


def volley(values, masks):
    values = lax.optimization_barrier(tuple(values))
    return lax.optimization_barrier(tuple(hop(value, mask) for value, mask in zip(values, masks)))


def masks_of(order):
    masks = [0]
    for mask in order:
        masks = masks + [old ^ mask for old in masks]
    return masks


def gather(value, order):
    for mask in order:
        value = jnp.concatenate([value, hop(value, mask)], 0)
    return value


def settle(halves, targets, widths, me):
    pieces = [(h, piece, have) for h in range(2) for piece, have in halves[h]]
    total = sum(len(have) for h, piece, have in pieces if h == 0)
    rows = pieces[0][1].shape[0] // len(pieces[0][2])
    if rows % 16:
        outs = [[] for _ in widths]
        for h in range(2):
            have = sum([have for _, have in halves[h]], [])
            table = np.zeros(total, np.int32)
            table[np.array(have)] = np.arange(total)
            place = jnp.asarray(table)[me ^ jnp.arange(total, dtype=jnp.int32)]
            blocks = jnp.concatenate([piece for piece, _ in halves[h]], 0).reshape(total, rows, -1)
            blocks = jnp.take(blocks, place, axis=0).reshape(total * rows, -1)
            for source, out, _, count in targets[h]:
                outs[out].append(blocks[:, source : source + count])
        return [jnp.concatenate(out, 1) for out in outs]

    def body(me_ref, *refs):
        ins = refs[: len(pieces)]
        outs = refs[len(pieces) : len(pieces) + len(widths)]
        held = refs[len(pieces) + len(widths) : -2]
        in_sems, out_sems = refs[-2:]
        loads = []
        for i in range(len(pieces)):
            load = pltpu.make_async_copy(ins[i], held[i], in_sems.at[i])
            load.start()
            loads.append(load)
        stores = []
        for i, (h, _, have) in enumerate(pieces):
            loads[i].wait()
            for j, mask in enumerate(have):
                start = pl.multiple_of((me_ref[0] ^ mask) * rows, rows)
                for source, out, column, count in targets[h]:
                    store = pltpu.make_async_copy(
                        held[i].at[pl.ds(j * rows, rows), pl.ds(source, count)],
                        outs[out].at[pl.ds(start, rows), pl.ds(column, count)],
                        out_sems.at[len(stores)],
                    )
                    store.start()
                    stores.append(store)
        for store in stores:
            store.wait()

    count = sum(len(have) * len(targets[h]) for h, _, have in pieces)
    size = 2 * sum(piece.size for _, piece, _ in pieces)
    return pl.pallas_call(
        body,
        out_shape=[jax.ShapeDtypeStruct((total * rows, width), jnp.bfloat16) for width in widths],
        in_specs=[pl.BlockSpec(memory_space=pltpu.SMEM)]
        + [pl.BlockSpec(memory_space=pl.ANY)] * len(pieces),
        out_specs=[pl.BlockSpec(memory_space=pl.ANY)] * len(widths),
        scratch_shapes=[pltpu.VMEM(piece.shape, jnp.bfloat16) for _, piece, _ in pieces]
        + [pltpu.SemaphoreType.DMA((len(pieces),)), pltpu.SemaphoreType.DMA((count,))],
        compiler_params=pltpu.CompilerParams(vmem_limit_bytes=size + (4 << 20)),
        cost_estimate=pl.CostEstimate(flops=0, bytes_accessed=size // 16, transcendentals=0),
    )(me.reshape(1), *[piece for _, piece, _ in pieces])


class Traffic:
    def __init__(self):
        self.flows = {}
        self.done = {}

    def turn(self, outs, new=None, step=None):
        names = list(self.flows) if step is None else [n for n in step if n in self.flows]
        gots = sum([self.flows[name][1] for name in names], ())
        tied = lax.optimization_barrier(gots + tuple(outs))
        outs = tied[len(gots) :]
        started = []
        for name in names:
            flow, got = self.flows.pop(name)
            got, tied = tied[: len(got)], tied[len(got) :]
            try:
                started.append((name, flow, flow.send(got)))
            except StopIteration as end:
                self.done[name] = end.value
        if new is not None:
            flows = new(self.done)
            for name, flow in ((name, flow) for name, flow in flows.items() if flow is not None):
                started.append((name, flow, next(flow)))
        sents = sum([sent for _, _, sent in started], ())
        tied = lax.optimization_barrier(sents + outs)
        for name, flow, sent in started:
            self.flows[name] = (flow, flow.send(tied[: len(sent)]))
            tied = tied[len(sent) :]
        return tied


def hops(values, masks):
    return tuple(hop(value, mask) for value, mask in zip(values, masks))


def once(values, masks):
    values = yield tuple(values)
    return (yield hops(values, masks))


def halve_pairs(pairs, orders):
    for step in list(zip(*orders))[::-1]:
        sent = yield tuple(sent for _, sent in pairs)
        got = yield hops(sent, step)
        sums = [(kept, part) for (kept, _), part in zip(pairs, got)]
        pairs = []
        for kept, part in sums:
            half = kept.shape[0] // 2
            pair = [widen(kept[cut]) + widen(part[cut]) for cut in (slice(half), slice(half, None))]
            pairs.append(pair if kept.ndim == 3 else [narrow(item) for item in pair])
    return [widen(kept) + widen(part) for kept, part in sums]


def halve_list_rows(value, masks):
    for mask in reversed(masks):
        half = value.shape[0] // 2
        sent = yield (value[half:],)
        (got,) = yield hops(sent, (mask,))
        value = value[:half] + got
    return value


def halve_list(blocks, masks):
    for mask in reversed(masks):
        half = len(blocks) // 2
        sent = yield tuple(narrow(block) for block in blocks[half:])
        got = yield hops(sent, (mask,) * half)
        blocks = [widen(a) + widen(b) for a, b in zip(blocks[:half], got)]
    return blocks[0]


def halve_rows(blocks, first, last, masks):
    for mask in reversed(masks):
        half = len(blocks) // 2
        sent = yield tuple(narrow(block[first:last]) for block in blocks[half:])
        got = yield hops(sent, (mask,) * half)
        blocks = [widen(a[first:last]) + widen(b) for a, b in zip(blocks[:half], got)]
        first, last = 0, last - first
    return blocks[0]


def double_each(parts, orders):
    for step in zip(*orders):
        parts = yield tuple(parts)
        got = yield hops(parts, step)
        parts = [jnp.concatenate(pair, 0) for pair in zip(parts, got)]
    return jnp.concatenate(parts, 0)


def double_list(value, masks):
    blocks = (value,)
    for mask in masks:
        blocks = yield blocks
        got = yield hops(blocks, (mask,) * len(blocks))
        blocks = tuple(blocks) + tuple(got)
    return blocks


def spin(value, cosine, sine):
    lane = lax.broadcasted_iota(jnp.int32, value.shape, 1)
    other = jnp.where(lane % 64 < 32, pltpu.roll(value, 96, 1), pltpu.roll(value, 32, 1))
    return value * cosine + other * sine


def spin_tables(offsets, sign):
    half = HEAD_DIM // 2
    freq = 10000.0 ** (-jnp.arange(half, dtype=jnp.float32) / half)
    angle = offsets.astype(jnp.float32).reshape(-1, 1) * freq
    cosine = jnp.cos(angle)
    sine = sign * jnp.sin(angle)
    return (jnp.concatenate([cosine] * 4, 1), jnp.concatenate([-sine, sine, -sine, sine], 1))


def hint():
    return pl.CostEstimate(flops=1 << 20, bytes_accessed=1 << 20, transcendentals=0)


def whole(array):
    return pl.BlockSpec(array.shape, lambda i: (0,) * array.ndim)


def like(shape, dtype=jnp.float32):
    return jax.ShapeDtypeStruct(shape, dtype)


BIG = pltpu.CompilerParams(vmem_limit_bytes=44 << 20)


def project(inputs, gain, shift, weight, tables, scale):
    rows, width = inputs.shape
    block = width // 2

    def body(in_ref, gain_ref, shift_ref, cos_ref, sin_ref, weight_ref, *outs):
        query_ref, pair_ref, normed_ref, inverse_ref, hidden_ref = outs
        step = pl.program_id(0)

        @pl.when(step == 0)
        def _():
            normed, inverse = standardize(widen(in_ref[...]))
            normed_ref[...] = normed
            inverse_ref[...] = inverse
            hidden_ref[...] = narrow(normed * gain_ref[...] + shift_ref[...])

        value = dot(hidden_ref[...], weight_ref[...])

        def turned(factor):
            parts = [
                spin(value[:, j : j + 128], cos_ref[...], sin_ref[...]) for j in range(0, block, 128)
            ]
            return [narrow(part * factor) for part in parts]

        @pl.when(step < 2)
        def _():
            for j, part in enumerate(turned(scale)):
                query_ref[:, 128 * j : 128 * j + 128] = part

        @pl.when((step >= 2) & (step < 4))
        def _():
            for j, part in enumerate(turned(1.0)):
                pair_ref[:, 128 * j : 128 * j + 128] = part

        @pl.when(step >= 4)
        def _():
            pair_ref[...] = narrow(value)

    def pair_place(i):
        return (jnp.maximum(i // 2 - 1, 0), jnp.where(i < 2, 0, i % 2))

    return pl.pallas_call(
        body,
        grid=(6,),
        out_shape=[
            like((rows, width), jnp.bfloat16),
            like((2 * rows, width), jnp.bfloat16),
            like((rows, width)),
            like((rows, 1)),
            like((rows, width), jnp.bfloat16),
        ],
        in_specs=[
            whole(inputs),
            whole(gain),
            whole(shift),
            whole(tables[0]),
            whole(tables[1]),
            pl.BlockSpec((width, block), lambda i: (0, i)),
        ],
        out_specs=[
            pl.BlockSpec((rows, block), lambda i: (0, jnp.minimum(i, 1))),
            pl.BlockSpec((rows, block), pair_place),
            pl.BlockSpec((rows, width), lambda i: (0, 0)),
            pl.BlockSpec((rows, 1), lambda i: (0, 0)),
            pl.BlockSpec((rows, width), lambda i: (0, 0)),
        ],
        compiler_params=BIG,
        cost_estimate=hint(),
    )(inputs, gain, shift, *tables, weight)


def ahead(mixed, low, before, gain, shift, ask=None, scale=1.0):
    rows, width = before.shape
    steps = width // LANES

    def body(mixed_ref, before_ref, gain_ref, shift_ref, *refs):
        low_ref, refs = refs[0], refs[1:]
        if ask is not None:
            ask_ref, refs = refs[0], refs[1:]
        sum_ref, normed_ref, inverse_ref, hidden_ref = refs[:4]
        step = pl.program_id(0)

        @pl.when(step < steps)
        def _():
            lanes = pl.ds(pl.multiple_of(step * LANES, LANES), LANES)
            sum_ref[:, lanes] = widen(before_ref[:, lanes]) + dot(mixed_ref[...], low_ref[...])

        @pl.when(step == steps - 1)
        def _():
            normed, inverse = standardize(sum_ref[...])
            normed_ref[...] = normed
            inverse_ref[...] = inverse
            hidden_ref[...] = narrow(normed * gain_ref[...] + shift_ref[...])

        if ask is not None:

            @pl.when(step >= steps)
            def _():
                refs[4][...] = narrow(dot(hidden_ref[...], ask_ref[...]) * scale)

    full = pl.BlockSpec((rows, width), lambda i: (0, 0))
    args = (mixed, before, gain, shift, low)
    specs = [whole(mixed), whole(before), whole(gain), whole(shift)]
    specs.append(pl.BlockSpec((width, LANES), lambda i: (0, jnp.minimum(i, steps - 1))))
    shapes = [
        like((rows, width)),
        like((rows, width)),
        like((rows, 1)),
        like((rows, width), jnp.bfloat16),
    ]
    outs = [full, full, pl.BlockSpec((rows, 1), lambda i: (0, 0)), full]
    if ask is not None:
        args = args + (ask,)
        specs.append(pl.BlockSpec((width, LANES), lambda i: (0, jnp.maximum(i - steps, 0))))
        shapes.append(like((rows, width), jnp.bfloat16))
        outs.append(pl.BlockSpec((rows, LANES), lambda i: (0, jnp.maximum(i - steps, 0))))
    return pl.pallas_call(
        body,
        grid=(steps if ask is None else 2 * steps,),
        out_shape=shapes,
        in_specs=specs,
        out_specs=outs,
        compiler_params=BIG,
        cost_estimate=hint(),
    )(*args)


def back(incoming, low, grads, normed, inverse, gain, out=None):
    rows, width = grads.shape
    block = LANES if low is None or low.shape[1] == width else LANES // 2
    first = 0 if low is None else width // block
    last = 0 if out is None else width // LANES
    norm_step = max(first - 1, 0)

    def body(in_ref, grad_ref, normed_ref, inverse_ref, gain_ref, *refs):
        if low is not None:
            low_ref, refs = refs[0], refs[1:]
        if out is not None:
            out_ref, refs = refs[0], refs[1:]
        sum_ref, gain_grad_ref, shift_grad_ref = refs[:3]
        held_ref = refs[-1]
        step = pl.program_id(0)
        if low is not None:

            @pl.when(step < first)
            def _():
                lanes = pl.ds(pl.multiple_of(step * block, block), block)
                held_ref[:, lanes] = dot_t(in_ref[...], low_ref[...])

        @pl.when(step == norm_step)
        def _():
            value = in_ref[...] if low is None else held_ref[...]
            inner, gain_grad, shift_grad = norm_back(
                value, normed_ref[...], inverse_ref[...], gain_ref[...]
            )
            total = widen(grad_ref[...]) + inner
            sum_ref[...] = total
            gain_grad_ref[...] = gain_grad
            shift_grad_ref[...] = shift_grad
            if out is not None:
                refs[3][...] = narrow(total)

        if out is not None:

            @pl.when(step >= first)
            def _():
                refs[4][...] = narrow(dot_t(refs[3][...], out_ref[...]))

    full = pl.BlockSpec((rows, width), lambda i: (0, 0))
    line = pl.BlockSpec((1, width), lambda i: (0, 0))
    args = (incoming, grads, normed, inverse, gain)
    specs = [whole(array) for array in args]
    if low is not None:
        args = args + (low,)
        specs.append(pl.BlockSpec((block, low.shape[1]), lambda i: (jnp.minimum(i, first - 1), 0)))
    shapes = [like((rows, width)), like((1, width)), like((1, width))]
    outs = [full, line, line]
    if out is not None:
        args = args + (out,)
        specs.append(pl.BlockSpec((LANES, width), lambda i: (jnp.maximum(i - first, 0), 0)))
        shapes = shapes + [like((rows, width), jnp.bfloat16)] * 2
        outs = outs + [full, pl.BlockSpec((rows, LANES), lambda i: (0, jnp.maximum(i - first, 0)))]
    return pl.pallas_call(
        body,
        grid=(first + last,),
        out_shape=shapes,
        in_specs=specs,
        out_specs=outs,
        scratch_shapes=[pltpu.VMEM((rows, width), jnp.float32)],
        compiler_params=BIG,
        cost_estimate=hint(),
    )(*args)


def feed_block(rows, ups, value_low, gate_low, drop_low, value_bias, gate_bias):
    count, width = rows.shape
    units = drop_low.shape[0]
    block = min(count, 256)

    def body(row_ref, up_ref, value_ref, gate_ref, drop_ref, value_bias_ref, gate_bias_ref, *outs):
        middle_ref, value_out, gate_out, back_ref, term_ref = outs
        middle_grad = widen(narrow(dot_t(up_ref[...], drop_ref[...])))
        value = dot_t(row_ref[...], value_ref[...]) + value_bias_ref[...]
        gate = dot_t(row_ref[...], gate_ref[...]) + gate_bias_ref[...]
        sigma = jax.nn.sigmoid(gate)
        middle = narrow(value * gate * sigma)
        value_grad = narrow(middle_grad * gate * sigma)
        gate_grad = narrow(middle_grad * value * sigma * (1.0 + gate * (1.0 - sigma)))
        middle_ref[...] = middle
        value_out[...] = value_grad
        gate_out[...] = gate_grad
        back_ref[...] = narrow(dot(value_grad, value_ref[...]) + dot(gate_grad, gate_ref[...]))
        term_ref[...] = narrow(dot(middle, drop_ref[...]))

    wide = pl.BlockSpec((block, width), lambda i: (i, 0))
    thin = pl.BlockSpec((block, units), lambda i: (i, 0))
    args = (rows, ups, value_low, gate_low, drop_low, value_bias, gate_bias)
    return pl.pallas_call(
        body,
        grid=(count // block,),
        out_shape=[like((count, units), jnp.bfloat16)] * 3 + [like((count, width), jnp.bfloat16)] * 2,
        in_specs=[wide, wide] + [whole(array) for array in args[2:]],
        out_specs=[thin] * 3 + [wide] * 2,
        compiler_params=BIG,
        cost_estimate=hint(),
    )(*args)


def unit_grad(lefts, rights, sums):
    units = lefts[0].shape[1]
    width = rights[0].shape[1]
    count = len(lefts)
    block = 128 if units % 128 == 0 else units

    def body(*refs):
        total = 0.0
        for left, right in zip(refs[:count], refs[count : 2 * count]):
            total = total + tdot(left[...], right[...])
        refs[2 * count][...] = narrow(total)
        if sums:
            refs[2 * count + 1][...] = sum(
                jnp.sum(widen(left[...]), 0, keepdims=True) for left in refs[:count]
            )

    specs = [pl.BlockSpec((left.shape[0], block), lambda i: (0, i)) for left in lefts]
    outs = [pl.BlockSpec((block, width), lambda i: (i, 0))]
    shapes = [like((units, width), jnp.bfloat16)]
    if sums:
        outs.append(pl.BlockSpec((1, block), lambda i: (0, i)))
        shapes.append(like((1, units)))
    return pl.pallas_call(
        body,
        grid=(units // block,),
        out_shape=shapes,
        in_specs=specs + [whole(right) for right in rights],
        out_specs=outs,
        compiler_params=BIG,
        cost_estimate=hint(),
    )(*lefts, *rights)


def spin_backward(query, pairs, got, cosine, sine):
    rows, width = query.shape

    def body(cos_ref, sin_ref, query_ref, own_ref, got_ref, out_ref):
        step = pl.program_id(0)

        @pl.when(step == 0)
        def _():
            out_ref[...] = query_ref[...]

        @pl.when(step == 1)
        def _():
            for j in range(0, width, 128):
                value = widen(own_ref[:, j : j + 128]) + widen(got_ref[:, j : j + 128])
                out_ref[:, j : j + 128] = narrow(spin(value, cos_ref[...], sin_ref[...]))

        @pl.when(step == 2)
        def _():
            out_ref[...] = narrow(widen(own_ref[...]) + widen(got_ref[...]))

    table = pl.BlockSpec((rows, 128), lambda i: (0, 0))
    part = pl.BlockSpec((rows, width), lambda i: (jnp.maximum(i - 1, 0), 0))
    return pl.pallas_call(
        body,
        grid=(3,),
        out_shape=jax.ShapeDtypeStruct((rows, 3 * width), jnp.bfloat16),
        in_specs=[table, table, pl.BlockSpec((rows, width), lambda i: (0, 0)), part, part],
        out_specs=pl.BlockSpec((rows, width), lambda i: (0, i)),
        cost_estimate=pl.CostEstimate(
            flops=24 * query.size, bytes_accessed=16 * query.size, transcendentals=0
        ),
    )(cosine, sine, query, pairs, got)


def two_heads(value):
    lane = lax.broadcasted_iota(jnp.int32, value.shape, 1)
    zero = jnp.zeros_like(value)
    first = jnp.where(lane < HEAD_DIM, value, zero)
    second = jnp.where(lane < HEAD_DIM, zero, value)
    return jnp.concatenate([first, second], 0)


def one_row(value):
    half = value.shape[0] // 2
    lane = lax.broadcasted_iota(jnp.int32, (half, value.shape[1]), 1)
    return jnp.where(lane < HEAD_DIM, value[:half], value[half:])


def row_probs(asked, keys, seen):
    scores = dot_t(asked, keys)
    if seen is not None:
        scores = jnp.where(jnp.concatenate([seen, seen], 0) > 0.5, scores, NEG)
    expo = jnp.exp(scores - jnp.max(scores, -1, keepdims=True))
    return expo / jnp.sum(expo, -1, keepdims=True)


def pair_rows(ref, part, r, lanes, row_count, block_count):
    keys = ref.shape[0] // (2 * row_count * block_count)
    starts = [((2 * b + part) * row_count + r) * keys for b in range(block_count)]
    return jnp.concatenate([ref[start : start + keys, lanes] for start in starts], 0)


def attend(query, pairs, seen, row_count, block_count):
    tokens, width = query.shape
    frames = tokens // row_count
    keys = pairs.shape[0] // (2 * row_count)

    def body(*refs):
        query_ref, pair_ref = refs[:2]
        out_ref = refs[-1]
        for r in range(row_count):
            span = slice(r * frames, (r + 1) * frames)
            for j in range(0, LANES, 128):
                lanes = slice(j, j + 128)
                asked = two_heads(query_ref[span, lanes])
                key = pair_rows(pair_ref, 0, r, lanes, row_count, block_count)
                value = pair_rows(pair_ref, 1, r, lanes, row_count, block_count)
                probs = row_probs(asked, key, refs[2][r] if seen is not None else None)
                out_ref[span, lanes] = narrow(one_row(dot(narrow(probs), value)))

    token_spec = pl.BlockSpec((tokens, LANES), lambda i: (0, i))
    args = (query, pairs)
    specs = [token_spec, pl.BlockSpec((pairs.shape[0], LANES), lambda i: (0, i))]
    if seen is not None:
        args = args + (seen,)
        specs.append(pl.BlockSpec(seen.shape, lambda i: (0, 0, 0)))
    return pl.pallas_call(
        body,
        grid=(width // LANES,),
        out_shape=jax.ShapeDtypeStruct((tokens, width), jnp.bfloat16),
        in_specs=specs,
        out_specs=token_spec,
        cost_estimate=pl.CostEstimate(
            flops=8 * tokens * width * keys,
            bytes_accessed=4 * query.size + 2 * pairs.size,
            transcendentals=0,
        ),
    )(*args)


def attend_back(query, pairs, seen, grads, tables, row_count, block_count, scale):
    tokens, width = query.shape
    frames = tokens // row_count
    keys = pairs.shape[0] // (2 * row_count)

    def body(*refs):
        query_ref, pair_ref, grad_ref = refs[:3]
        out_query, out_pair = refs[-2:]

        def put(part, r, lanes, value):
            count = keys // block_count
            for b in range(block_count):
                start = ((2 * b + part) * row_count + r) * count
                out_pair[start : start + count, lanes] = narrow(value[b * count : (b + 1) * count])

        for r in range(row_count):
            span = slice(r * frames, (r + 1) * frames)
            for j in range(0, LANES, 128):
                lanes = slice(j, j + 128)
                asked = two_heads(query_ref[span, lanes])
                grad = two_heads(grad_ref[span, lanes])
                key = pair_rows(pair_ref, 0, r, lanes, row_count, block_count)
                value = pair_rows(pair_ref, 1, r, lanes, row_count, block_count)
                probs = row_probs(asked, key, refs[5][r] if seen is not None else None)
                score_grad = narrow(softmax_back(probs, dot_t(grad, value)))
                back = one_row(dot(score_grad, key))
                if tables is not None:
                    back = spin(back, refs[3][span, :], refs[4][span, :])
                out_query[span, lanes] = narrow(back * scale)
                put(0, r, lanes, tdot(score_grad, asked))
                put(1, r, lanes, tdot(narrow(probs), grad))

    token_spec = pl.BlockSpec((tokens, LANES), lambda i: (0, i))
    pair_spec = pl.BlockSpec((pairs.shape[0], LANES), lambda i: (0, i))
    specs = [token_spec, pair_spec, token_spec]
    args = (query, pairs, grads)
    if tables is not None:
        specs = specs + [pl.BlockSpec((tokens, 128), lambda i: (0, 0))] * 2
        args = args + tuple(tables)
    if seen is not None:
        specs.append(pl.BlockSpec(seen.shape, lambda i: (0, 0, 0)))
        args = args + (seen,)
    return pl.pallas_call(
        body,
        grid=(width // LANES,),
        out_shape=[
            jax.ShapeDtypeStruct((tokens, width), jnp.bfloat16),
            jax.ShapeDtypeStruct(pairs.shape, jnp.bfloat16),
        ],
        in_specs=specs,
        out_specs=[token_spec, pair_spec],
        cost_estimate=pl.CostEstimate(
            flops=20 * tokens * width * keys,
            bytes_accessed=6 * query.size + 4 * pairs.size,
            transcendentals=0,
        ),
    )(*args)


def order_matrix(size, rows, order, me):
    masks = jnp.asarray(np.array(masks_of(order), np.int32))
    source = ((me ^ masks)[:, None] * rows + jnp.arange(rows, dtype=jnp.int32)[None, :]).reshape(-1)
    return (jnp.arange(size, dtype=jnp.int32)[:, None] == source[None, :]).astype(jnp.bfloat16)


def local(
    frames,
    prompt,
    clip_frames,
    upstream,
    first_gain,
    first_shift,
    self_project,
    self_output,
    second_gain,
    second_shift,
    cross_query,
    cross_memory,
    cross_output,
    third_gain,
    third_shift,
    feed_input,
    feed_lift,
    feed_output,
    feed_offset,
):
    row_count, frame_count, width = frames.shape
    heads = width // HEAD_DIM
    token_count = row_count * frame_count
    scale = HEAD_DIM ** (-0.5)
    batch_count = lax.axis_size(B)
    seq_count = lax.axis_size(S)
    device_count = batch_count * seq_count
    seq_place = lax.axis_index(S)
    me = lax.axis_index(B) * seq_count + seq_place
    share = first_gain.shape[0]

    seq_masks = [1 << i for i in range(seq_count.bit_length() - 1)]
    batch_masks = [seq_count << i for i in range(batch_count.bit_length() - 1)]
    near = batch_masks[:3]
    far = batch_masks[3:]
    x_mask, y_mask = batch_masks[:2]
    places = [(0, 3, 1, 2), (3, 1, 2, 0), (3, 2, 0, 1)]
    if len(batch_masks) != 4:
        places = [[(i + j) % len(batch_masks) for i in range(len(batch_masks))] for j in range(3)]
    tail_orders = [[batch_masks[i] for i in place] for place in places]
    near_orders = [near[j:] + near[:j] for j in range(3)]
    near_count = len(masks_of(near))
    third = (token_count * 3 // 8) // 16 * 16
    cuts = [0, third, 2 * third, token_count]
    units = feed_output.shape[0]

    vectors = [first_gain, first_shift, second_gain, second_shift, third_gain, third_shift, feed_offset]
    vectors = jnp.pad(jnp.stack(vectors, 1), ((0, 0), (0, 128 - len(vectors))))
    split = 3 * width // 2
    group_one = narrow(jnp.concatenate([vectors, self_project], 1))
    memory_rows = ((0, share // 2 - cross_memory.shape[0]), (0, 0))
    memory_rows = jnp.concatenate(
        [
            jnp.pad(cross_memory[:, :width], memory_rows),
            jnp.pad(cross_memory[:, width:], memory_rows),
        ],
        0,
    )
    group_two = narrow(jnp.concatenate([self_output, cross_query, cross_output, memory_rows], 1))
    lift_rows = jnp.pad(feed_lift, ((0, 14), (0, width - units)))
    feed_sent = narrow(
        jnp.concatenate([feed_input.reshape(2 * units, width), feed_output, lift_rows], 0)
    )
    known = [0]
    for mask in batch_masks[:1:-1]:
        group_one = jnp.concatenate([group_one, hop(group_one, mask)], 0)
        if len(known) == 1:
            group_one, group_two = lax.optimization_barrier((group_one, group_two))
        group_two = jnp.concatenate([group_two, hop(group_two, mask)], 0)
        known = known + [old ^ mask for old in known]
    known = [known + [old ^ mask for old in known] for mask in (x_mask, y_mask)]

    def pieces_of(columns, others):
        halves = []
        for h in range(2):
            have = known[h]
            pieces = [(columns[h], have), (others[h], [old ^ (y_mask, x_mask)[h] for old in have])]
            halves.append(pieces)
        return halves

    def add_core(halves, got):
        for h in range(2):
            halves[h] = halves[h] + [
                (piece, [old ^ seq_masks[0] for old in have])
                for piece, (_, have) in zip(got[h], halves[h])
            ]
            for mask in seq_masks[1:]:
                halves[h] = halves[h] + [
                    (hop(piece, mask), [old ^ mask for old in have]) for piece, have in halves[h]
                ]
        return halves

    core = seq_masks[0]
    traffic = Traffic()
    feed_cuts = [0, 3 * units // 4, 2 * units + units // 6, feed_sent.shape[0]]
    if units % 192:
        feed_cuts = [0, units, 2 * units, feed_sent.shape[0]]
    feed_parts = [feed_sent[feed_cuts[p] : feed_cuts[p + 1]] for p in range(3)]
    ones = (group_one[:, : 128 + split], group_one[:, 128 + split :])
    got = volley(ones + (feed_parts[0],), [x_mask, y_mask, far[0]])
    feed_got = [got[2]]
    ones = tuple(jnp.concatenate(pair, 0) for pair in zip(ones, got))
    got_one = volley(ones + ones + (feed_parts[1],), [y_mask, x_mask, core, core, far[0]])
    feed_got.append(got_one[4])
    twos = (group_two[:, : 2 * width], group_two[:, 2 * width :])
    got = volley(
        twos + got_one[:2] + (feed_parts[2],), [x_mask, y_mask, core, core, far[0]]
    )
    feed_got.append(got[4])
    twos = tuple(jnp.concatenate(pair, 0) for pair in zip(twos, got))
    halves = pieces_of(ones, got_one[:2])
    halves = add_core(halves, ((got_one[2], got[2]), (got_one[3], got[3])))
    new = {"two": once(twos + twos, [y_mask, x_mask, core, core])}
    pieces = traffic.turn([piece for have in halves for piece, _ in have], lambda done: new)
    count = len(pieces) // 2
    halves = [
        [(piece, have) for piece, (_, have) in zip(pieces[h * count : (h + 1) * count], halves[h])]
        for h in range(2)
    ]
    packed, triple_low = settle(
        halves, [[(0, 0, 0, 128), (128, 1, 0, split)], [(0, 1, split, split)]], [128, 3 * width], me
    )
    packed = dot_t(jnp.eye(8, 128, dtype=jnp.bfloat16), packed)
    gain_one, shift_one, gain_two, shift_two, gain_three, shift_three, drop_bias = [
        packed[j : j + 1] for j in range(7)
    ]

    def cut_tokens(value):
        return [value[cuts[p] : cuts[p + 1]] for p in range(3)]

    def token_pairs(value):
        pairs = []
        for p in range(3):
            first, last = near_count * cuts[p], near_count * cuts[p + 1]
            middle = (first + last) // 2
            pairs.append((narrow(value[first:middle]), narrow(value[middle:last])))
        return pairs

    upstream_tokens = upstream.reshape(token_count, width)

    own_places = seq_place * frame_count + jnp.arange(frame_count, dtype=jnp.int32)
    key_order = masks_of(seq_masks)
    key_places = jnp.concatenate(
        [(seq_place ^ k) * frame_count + jnp.arange(frame_count, dtype=jnp.int32) for k in key_order]
    )
    own_clip, own_offset = clip_tables(clip_frames, own_places)
    key_clip = clip_tables(clip_frames, key_places)[0]
    seen = widen(own_clip[:, :, None] == key_clip[:, None, :])
    prompt_flat = prompt.reshape(-1, prompt.shape[2])
    rows = cross_memory.shape[0]
    place = jnp.arange(prompt.shape[2], dtype=jnp.int32)
    place = place // rows * share + place % rows
    places = jnp.arange(width, dtype=jnp.int32)[None, :]
    prompt_spread = [
        narrow(dot(prompt_flat, (place[:, None] + j * (share // 2) == places).astype(jnp.bfloat16)))
        for j in range(2)
    ]
    prompt_spread = jnp.concatenate(prompt_spread, 0)
    turn_tables = spin_tables(own_offset, 1.0)
    back_tables = spin_tables(own_offset, -1.0)

    inputs = frames.reshape(token_count, width)
    query, pairs, normed_one, inverse_one, hidden_one = project(
        inputs, gain_one, shift_one, triple_low, turn_tables, scale
    )
    query, prompt_spread = traffic.turn(
        (query, prompt_spread), lambda done: {"pairs": double_list(pairs, seq_masks)}, step=[]
    )
    for _ in seq_masks:
        (query,) = traffic.turn((query,), step=["pairs"])
    pairs = jnp.concatenate(traffic.done["pairs"], 0)

    def turn_rows(rows, order):
        return narrow(dot(rows, order_matrix(rows.shape[1], rows.shape[1] // device_count, order, me)))

    self_mixed = attend(query, pairs, seen, row_count, seq_count)

    def started(done):
        return {
            "last": once(done["two"][:2], [core, core]),
            "up": double_each(cut_tokens(upstream_tokens), near_orders),
        }

    self_mixed, feed_sent, *feed_got = traffic.turn([self_mixed, feed_sent] + feed_got, started)
    got_two = traffic.done["two"]
    feed_all = jnp.concatenate([feed_sent] + feed_got, 0)
    for mask in far[1:]:
        feed_all = jnp.concatenate([feed_all, hop(feed_all, mask)], 0)
    feed_all = feed_all.reshape(-1, feed_sent.shape[0], width)
    value_low, gate_low, drop_low = [
        feed_all[:, j * units : (j + 1) * units].reshape(-1, width) for j in range(3)
    ]
    unit_count = drop_low.shape[0]
    value_bias, gate_bias = [
        widen(feed_all[:, 3 * units + j, :units].reshape(1, unit_count)) for j in range(2)
    ]
    self_mixed, value_low, gate_low, drop_low, value_bias, gate_bias = traffic.turn(
        (self_mixed, value_low, gate_low, drop_low, value_bias, gate_bias),
        lambda done: {"mixed": double_list(self_mixed, seq_masks)},
    )
    got = traffic.done["last"]
    halves = add_core(
        pieces_of(twos, got_two[:2]), ((got_two[2], got[0]), (got_two[3], got[1]))
    )
    lows = settle(
        halves,
        [[(0, 0, 0, width), (width, 1, 0, width)], [(0, 2, 0, width), (width, 3, 0, width)]],
        [width] * 4,
        me,
    )
    self_low, ask_low, cross_low, memory_low, self_mixed = traffic.turn(
        (*lows, self_mixed), lambda done: {"hidden": double_list(hidden_one, seq_masks)}
    )
    memory = narrow(dot(prompt_spread, memory_low))
    after_self, normed_two, inverse_two, hidden_two, asking = ahead(
        self_mixed, self_low, inputs, gain_two, shift_two, ask_low, scale
    )
    cross_mixed = attend(asking, memory, None, row_count, 1)
    (cross_mixed,) = traffic.turn(
        (cross_mixed,),
        lambda done: {
            "ups": double_list(done["up"], seq_masks),
            "hidden_two": double_list(hidden_two, seq_masks),
        },
    )
    after_cross, normed_three, inverse_three, hidden_three = ahead(
        cross_mixed, cross_low, after_self, gain_three, shift_three
    )

    hidden_three, cross_mixed = traffic.turn(
        (hidden_three, cross_mixed),
        lambda done: {
            "rows": double_each(cut_tokens(hidden_three), near_orders),
            "cross_mixed": double_list(cross_mixed, seq_masks),
        },
    )
    for _ in seq_masks[1:]:
        traffic.turn((), step=["ups", "cross_mixed", "hidden_two", "hidden", "mixed"])
    ups = traffic.done["ups"]
    hidden_all, mixed_all, asked_all = [
        jnp.concatenate(traffic.done[name], 0) for name in ("hidden", "mixed", "hidden_two")
    ]
    turned_triple = [turn_rows(hidden_all, order) for order in tail_orders]
    turned_triple = traffic.turn(turned_triple)
    cross_all = jnp.concatenate(traffic.done["cross_mixed"], 0)
    turned_memory = turn_rows(prompt_flat, tail_orders[2])
    turned_memory = jnp.concatenate([turned_memory] * seq_count, 0)
    turned_cross = turn_rows(cross_all, tail_orders[0])
    turned_ask = turn_rows(asked_all, tail_orders[1])
    turned_self = [turn_rows(mixed_all, order) for order in tail_orders]
    turned_cross, turned_ask, turned_memory, *turned_self = traffic.turn(
        [turned_cross, turned_ask, turned_memory] + turned_self,
        lambda done: {"all": double_list(done["rows"], seq_masks)} if "rows" in done else {},
    )
    while "rows" in traffic.flows:
        traffic.turn((), lambda done: {"all": double_list(done["rows"], seq_masks)} if "rows" in done else {})
    lows = (value_low, gate_low, drop_low, value_bias, gate_bias)
    results = [feed_block(traffic.done["rows"], ups[0], *lows)]
    results[0] = traffic.turn(results[0])
    for _ in seq_masks[1:]:
        traffic.turn((), step=["all"])
    feed_rows = traffic.done["all"]
    for rows, up in zip(feed_rows[1:], ups[1:]):
        results.append(feed_block(rows, up, *lows))
    middles, value_grads, gate_grads, back_sums, term_sums = [list(item) for item in zip(*results)]

    def back_flow():
        value = yield from halve_list(back_sums, seq_masks)
        return (yield from halve_pairs(token_pairs(value), near_orders))

    blocks = len(feed_rows)
    far_count = len(masks_of(far))
    tied = traffic.turn(middles + value_grads + gate_grads, lambda done: {"back": back_flow()})
    middles, value_grads, gate_grads = tied[:blocks], tied[blocks : 2 * blocks], tied[2 * blocks :]
    drop_grad = unit_grad(middles, ups, False)[0]
    tied = traffic.turn((drop_grad, *value_grads, *gate_grads))
    for _ in seq_masks[1:]:
        tied = traffic.turn(tied)
    drop_grad, value_grads, gate_grads = tied[0], tied[1 : 1 + blocks], tied[1 + blocks :]
    value_grad, value_bias_grad = unit_grad(value_grads, feed_rows, True)
    gate_grad, gate_bias_grad = unit_grad(gate_grads, feed_rows, True)
    value_grad, gate_grad, drop_grad = traffic.turn(
        (value_grad, gate_grad, drop_grad),
        lambda done: {"term": halve_list(term_sums, seq_masks)},
    )

    def unit_rows(k):
        rows = slice(k * units, (k + 1) * units)
        bias = jnp.concatenate([value_bias_grad[:, rows], gate_bias_grad[:, rows]], 0)
        bias = narrow(jnp.pad(bias, ((0, 14), (0, width - units))))
        return jnp.concatenate([value_grad[rows], gate_grad[rows], drop_grad[rows], bias], 0)

    unit_sums = [unit_rows(k) for k in range(far_count)]
    unit_sums = list(traffic.turn(unit_sums))
    for _ in seq_masks[1:]:
        traffic.turn((), step=["term"])
    unit_cuts = [0] + [units // 2 * j for j in range(1, 6)] + [3 * units + 16]
    if units % 32:
        unit_cuts = [0] + [3 * units + 16] * 6

    def unit_flow(p):
        if unit_cuts[p] < unit_cuts[p + 1]:
            return halve_rows(unit_sums, unit_cuts[p], unit_cuts[p + 1], far)

    while "back" in traffic.flows:
        unit_sums = list(traffic.turn(unit_sums))
    feed_back = jnp.concatenate(traffic.done["back"], 0)
    (feed_back,) = traffic.turn(
        (feed_back,),
        lambda done: {"term_near": halve_pairs(token_pairs(done["term"]), near_orders)},
    )
    cross_out_grad, grad_gain_three, grad_shift_three, cross_branch, cross_mixed_grad = back(
        feed_back, None, upstream_tokens, normed_three, inverse_three, gain_three, cross_low
    )

    def weight_pair(turned, *grads):
        half = turned.shape[1] // 2
        pair = []
        for columns in (turned[:, :half], turned[:, half:]):
            sums = [narrow(tdot(columns, grad)) for grad in grads]
            if len(grads) > 1:
                rows = cross_memory.shape[0]
                sums = [
                    jnp.pad(part.reshape(-1, rows, width), ((0, 0), (0, share // 2 - rows), (0, 0)))
                    for part in sums
                ]
                sums = [jnp.concatenate(sums, 1).reshape(-1, width)]
            pair.append(sums[0])
        return tuple(pair)

    (cross_mixed_grad,) = traffic.turn(
        (cross_mixed_grad,),
        lambda done: {"dc": double_list(cross_branch, seq_masks), "unit0": unit_flow(0)},
    )
    asking_grad, memory_grad = attend_back(
        asking, memory, None, cross_mixed_grad, None, row_count, 1, scale
    )
    asking_grad, memory_grad = traffic.turn(
        (asking_grad, memory_grad),
        lambda done: {
            "dq": double_list(asking_grad, seq_masks),
            "dm": double_list(memory_grad, seq_masks),
        },
    )
    for _ in seq_masks[1:]:
        traffic.turn((), step=["dc"])
    self_out_grad, grad_gain_two, grad_shift_two, self_branch, self_mixed_grad = back(
        asking_grad, ask_low, cross_out_grad, normed_two, inverse_two, gain_two, self_low
    )
    (self_mixed_grad,) = traffic.turn(
        (self_mixed_grad,),
        lambda done: {"da": double_list(self_branch, seq_masks)},
    )
    for _ in seq_masks[1:]:
        traffic.turn((), step=["dq", "dm", "da"])
    cross_pair = weight_pair(turned_cross, jnp.concatenate(traffic.done["dc"], 0))
    layer_output = narrow(
        after_cross + jnp.concatenate(traffic.done["term_near"], 0) + drop_bias
    )
    ask_pair = weight_pair(turned_ask, jnp.concatenate(traffic.done["dq"], 0))
    memory_all = traffic.done["dm"]
    half = memory_grad.shape[0] // 2
    memory_pair = weight_pair(
        turned_memory,
        jnp.concatenate([part[:half] for part in memory_all], 0),
        jnp.concatenate([part[half:] for part in memory_all], 0),
    )
    self_mixed_grad, layer_output = traffic.turn(
        (self_mixed_grad, layer_output),
        lambda done: {
            "first": halve_pairs([cross_pair, ask_pair, memory_pair], tail_orders),
            "unit1": unit_flow(1),
        },
    )
    query_back, pair_grad = attend_back(
        query, pairs, seen, self_mixed_grad, back_tables, row_count, seq_count, scale
    )

    def shed_frames(value):
        for mask in reversed(seq_masks):
            half = value.shape[0] // 2
            (sent,) = yield (value[half:],)
            (got,) = yield hops((sent,), (mask,))
            if mask > seq_masks[0]:
                value = narrow(widen(value[:half]) + widen(got))
        return value, got

    (query_back,) = traffic.turn((query_back,), lambda done: {"pair": shed_frames(pair_grad)}, step=[])
    for _ in seq_masks:
        (query_back,) = traffic.turn((query_back,), step=["pair"])
    triple_back = spin_backward(query_back, *traffic.done["pair"], *back_tables)
    (triple_back,) = traffic.turn(
        (triple_back,), lambda done: {"dt": double_list(triple_back, seq_masks)}
    )
    frame_grad, grad_gain_one, grad_shift_one = back(
        triple_back, triple_low, self_out_grad, normed_one, inverse_one, gain_one
    )
    branch_all = jnp.concatenate(traffic.done["da"], 0)
    third = width // 3
    self_pairs = [
        weight_pair(turned, branch_all[:, p * third : (p + 1) * third])
        for p, turned in enumerate(turned_self)
    ]

    frame_grad, *sums = traffic.turn(
        (
            frame_grad,
            grad_gain_one,
            grad_shift_one,
            grad_gain_two,
            grad_shift_two,
            grad_gain_three,
            grad_shift_three,
        ),
        lambda done: {"unit2": unit_flow(2)},
    )
    grad_drop_bias = jnp.sum(widen(upstream_tokens), 0, keepdims=True)
    sums = jnp.concatenate(sums + [grad_drop_bias], 0).reshape(7, device_count, share)
    sums = jnp.transpose(sums, (1, 0, 2)).reshape(device_count, 7 * share)
    sums = jnp.pad(sums, ((0, 0), (0, 1024 - 7 * share)))
    tail_masks = masks_of(tail_orders[0] + seq_masks)
    sums = jnp.take(sums, me ^ jnp.asarray(np.array(tail_masks, np.int32)), axis=0)
    sums = sums.reshape(device_count, 8, 128)
    for _ in seq_masks[1:]:
        traffic.turn((), step=["dt"])
    triple_all = jnp.concatenate(traffic.done["dt"], 0)
    triple_pairs = [
        weight_pair(turned, triple_all[:, p * width : (p + 1) * width])
        for p, turned in enumerate(turned_triple)
    ]
    triple_pairs = [
        tuple(jnp.concatenate(item, 1) for item in zip(*pair))
        for pair in zip(triple_pairs, self_pairs)
    ]
    tied = traffic.turn(
        sum(triple_pairs, ()), lambda done: {"sums": halve_list_rows(sums, seq_masks)}
    )
    triple_pairs = [tied[2 * p : 2 * p + 2] for p in range(3)]
    while "first" in traffic.flows or "sums" in traffic.flows:
        traffic.turn(())
    sums = traffic.done["sums"]
    half = sums.shape[0] // 2
    traffic.turn(
        (),
        lambda done: {
            "tail": halve_pairs(
                triple_pairs + [(sums[:half], sums[half:])], tail_orders + [tail_orders[0]]
            ),
            "unit3": unit_flow(3),
        },
    )
    traffic.turn((), lambda done: {"unit4": unit_flow(4)})
    traffic.turn((), lambda done: {"unit5": unit_flow(5)})
    while traffic.flows:
        traffic.turn(())
    parts = traffic.done["tail"]
    grad_cross, grad_ask, grad_memory = traffic.done["first"]
    grad_self = jnp.concatenate([part[:, width:] for part in parts[:3]], 1)
    unit_sums = jnp.concatenate([traffic.done[name] for name in UNITS if name in traffic.done], 0)
    grad_triple = jnp.concatenate([part[:, :width] for part in parts[:3]], 1)
    sums = parts[3].reshape(1024)[: 7 * share].reshape(7, share)
    grad_memory = grad_memory.reshape(2, share // 2, width)[:, : cross_memory.shape[0]]
    grad_memory = jnp.concatenate([grad_memory[0], grad_memory[1]], 1)
    grad_lift = unit_sums[: 2 * units].reshape(2, units, width)
    grad_drop = unit_sums[2 * units : 3 * units]
    grad_lift_bias = unit_sums[3 * units : 3 * units + 2, :units]

    shape = frames.shape
    return (
        layer_output.reshape(shape),
        frame_grad.reshape(shape),
        sums[0],
        sums[1],
        grad_triple,
        grad_self,
        sums[2],
        sums[3],
        grad_ask,
        grad_memory,
        grad_cross,
        sums[4],
        sums[5],
        grad_lift,
        grad_lift_bias,
        grad_drop,
        sums[6],
    )


def solution(mesh):
    both = P(AX)
    wide = P(AX, None)
    rows = P(B, S, None)
    units = P(None, AX, None)
    in_specs = (
        rows,
        P(B, None, None),
        P(B, None),
        rows,
        both,
        both,
        wide,
        wide,
        both,
        both,
        wide,
        wide,
        wide,
        both,
        both,
        units,
        P(None, AX),
        wide,
        both,
    )
    out_specs = (
        rows,
        rows,
        both,
        both,
        wide,
        wide,
        both,
        both,
        wide,
        wide,
        wide,
        both,
        both,
        units,
        P(None, AX),
        wide,
        both,
    )
    return jax.shard_map(local, mesh=mesh, in_specs=in_specs, out_specs=out_specs, check_vma=False)
```

time: 907 us -> 776 us (0.86)
  waiting for transfers between devices: 436 us -> 303 us
  Pallas kernels: 15.8 us -> 141 us
  matrix products: 135 us -> 53.4 us
  local copies, waits for them, and re-layouts: 139 us -> 78.5 us
  other arithmetic: 65.1 us -> 87.8 us
    ppermute x117 -> x109, waiting for transfers between devices: 436 us -> 303 us  [hop(): return lax.ppermute(value, AX, [(i, i ^ mask) for i in range(count)])]
    pallas_call x0 -> x16, Pallas kernels: none -> 126 us  [the longest x2 27.8 us: feed_block(): pl.pallas_call(body, grid=(count // block,), out_shape=[like((count, unit...]
    dot_general x11 -> x0, matrix products: 33.7 us -> none  [mult(): return jnp.einsum(form, left, right, preferred_element_type=jnp.float32)]
    dot_general x6 -> x1, matrix products: 28.2 us -> 0.2 us  [dot_t(): lax.dot_general(left, right, (((1,), (1,)), ((), ())), preferred_element_...]
    reshape x13 -> x0, local copies, waits for them, and re-layouts: 26.5 us -> none  [the longest x9 13.7 us: split_heads(): return value.reshape(row_count, -1, heads, HEAD_DIM)]
    convert_element_type x9 -> x1, local copies, waits for them, and re-layouts: 22 us -> 0.08 us  [spin_tables(): angle = offsets.astype(jnp.float32).reshape(-1, 1) * freq]
    concatenate x38 -> x45, other arithmetic: 18.9 us -> 39.2 us  [the longest x12 9.87 us: double_each(): parts = [jnp.concatenate(pair, 0) for pair in zip(parts, got)]]
    another operation x10 -> x0, local copies, waits for them, and re-layouts: 15 us -> none  [the longest x1 4.98 us: local(): jnp.stack([key_grad, value_grad], 2)]
  transfers between devices with their start and end apart: 117 -> 109, of which waited for: 55 -> 47; matrix products, arithmetic and copies ran while one was open for 33% -> 14% of each run, Pallas kernels for 2% -> 17%
where the time goes in v1:
time: 776 us; the launch traced here: 769 us
  waiting for transfers between devices  303 us (39%)
  Pallas kernels  141 us (18%)
  starting transfers between devices  102 us (13%)
  other arithmetic  87.8 us (11%)
  local copies, waits for them, and re-layouts  78.5 us (10%)
  matrix products  53.4 us (7%)
    ppermute x109, waiting for transfers between devices, hop(): return lax.ppermute(value, AX, [(i, i ^ mask) for i in range(count)])  303 us
    ppermute x109, starting transfers between devices, hop(): return lax.ppermute(value, AX, [(i, i ^ mask) for i in range(count)])  102 us
    unnamed x325, local copies, waits for them, and re-layouts  48.8 us
    pallas_call x2, Pallas kernels, feed_block(): pl.pallas_call(body, grid=(count // block,), out_shape=[like((count, unit...  27.8 us
    dot_general x12, matrix products, dot(): lax.dot_general(left, right, (((1,), (0,)), ((), ())), preferred_element_...  27.7 us
    pallas_call x2, Pallas kernels, attend_back(): pl.pallas_call(body, grid=(width // LANES,), out_shape=[jax.ShapeDtypeStr...  26.9 us
    dot_general x20, matrix products, tdot(): lax.dot_general(left, right, (((0,), (0,)), ((), ())), preferred_element_...  25.5 us
    convert_element_type x29, other arithmetic, narrow(): return value.astype(jnp.bfloat16)  20.3 us
  transfers between devices with their start and end apart: 109, of which 47 were waited for; matrix products, arithmetic and copies ran while one was open for 14% of the time, Pallas kernels for 17%

profile of v1, /device:TPU:0, one launch (start us, length us, event | category | flops | bytes accessed | tf_op | source)
XLA Modules:
  0.0 768.7 jit_solution(7449844449713594760)
XLA Ops:
  13.7 16.5 %collective-permute-done = bf16[48,4736]{1,0:T(8,128)(2,1)} collective-permute-done((bf16[48,4736]{1,0:T(8,128)(2,1)}, bf16[48,4736]{1,0:T(8,128)(2,1)}, u32[]{:S(2)}, u32[]{:S(2)}) %collective-permute-start) | collective-permute-done | bytes 454688 | tf_op jit(solution)/shard_map/ppermute | solution.py:77
  35.7 29.7 %collective-permute-done.3 = bf16[96,4736]{1,0:T(8,128)(2,1)S(1)} collective-permute-done((bf16[96,4736]{1,0:T(8,128)(2,1)S(1)}, bf16[96,4736]{1,0:T(8,128)(2,1)S(1)}, u32[]{:S(2)}, u32[]{:S(2)}) %collective-permute-start.3) | collective-permute-done | bytes 909344 | tf_op jit(solution)/shard_map/ppermute | solution.py:77
  73.9 15.9 %collective-permute-done.6 = bf16[144,1536]{1,0:T(8,128)(2,1)S(1)} collective-permute-done((bf16[144,1536]{1,0:T(8,128)(2,1)S(1)}, bf16[144,1536]{1,0:T(8,128)(2,1)S(1)}, u32[]{:S(2)}, u32[]{:S(2)}) %collective-permute-start.6) | collective-permute-done | bytes 442400 | tf_op jit(solution)/shard_map/ppermute | solution.py:77
  92.3 13.5 %collective-permute-done.2 = bf16[96,6144]{1,0:T(8,128)(2,1)S(1)} collective-permute-done((bf16[96,6144]{1,0:T(8,128)(2,1)S(1)}, bf16[96,6144]{1,0:T(8,128)(2,1)S(1)}, u32[]{:S(2)}, u32[]{:S(2)}) %collective-permute-start.2) | collective-permute-done | bytes 1179680 | tf_op jit(solution)/shard_map/ppermute | solution.py:77
  109.6 33.3 %collective-permute-done.11 = bf16[272,1536]{1,0:T(8,128)(2,1)S(1)} collective-permute-done((bf16[272,1536]{1,0:T(8,128)(2,1)S(1)}, bf16[272,1536]{1,0:T(8,128)(2,1)S(1)}, u32[]{:S(2)}, u32[]{:S(2)}) %collective-permute-start.11) | collective-permute-done | bytes 835616 | tf_op jit(solution)/shard_map/ppermute | solution.py:77
  152.0 24.1 %collective-permute-done.16 = bf16[176,1536]{1,0:T(8,128)(2,1)} collective-permute-done((bf16[176,1536]{1,0:T(8,128)(2,1)}, bf16[176,1536]{1,0:T(8,128)(2,1)}, u32[]{:S(2)}, u32[]{:S(2)}) %collective-permute-start.16) | collective-permute-done | bytes 540704 | tf_op jit(solution)/shard_map/ppermute | solution.py:77
  201.2 9.5 %shard_map.405 = (bf16[128,1536]{1,0:T(8,128)(2,1)S(1)}, bf16[256,1536]{1,0:T(8,128)(2,1)}, f32[128,1536]{1,0:T(8,128)S(1)}, f32[128,1]{1,0:T(8,128)S(1)}, bf16[128,1536]{1,0:T(8,128)(2,1)S(1)}) custom-call(bf16[128,1536]{1,0:T(8,128)(2,1)S(1)} %bitcast.91, f32[1,1536]{1,0:T(1,128)S(1)} %get-tuple-element.956.gain_ref, ...), custom_call_target="tpu_custom_call" | custom-call | flops 1048576 | bytes 1048576 | tf_op jit(solution)/shard_map/pallas_call | solution.py:323
  221.4 9.8 %shard_map.406.mixed_ref = bf16[128,1536]{1,0:T(8,128)(2,1)} custom-call(bf16[128,1536]{1,0:T(8,128)(2,1)} %copy-done.32, bf16[512,1536]{1,0:T(8,128)(2,1)} %constant_dynamic-update-slice_fusion.5.refs_1_, f32[2,64,128]{2,1,0:T(8,128)} %compare_convert_fusion.refs_2_.refs_5_), custom_call_target="tpu_custom_call" | custom-call | flops 201326592 | bytes 2359296 | tf_op jit(solution)/shard_map/pallas_call | solution.py:629
  268.0 9.0 %shard_map.407 = (bf16[1536,1536]{1,0:T(8,128)(2,1)S(1)}, bf16[1536,1536]{1,0:T(8,128)(2,1)S(1)}, bf16[1536,1536]{1,0:T(8,128)(2,1)S(1)}, bf16[1536,1536]{1,0:T(8,128)(2,1)}) custom-call(s32[1]{0:T(128)} %bitcast.9.me_ref, bf16[384,3072]{1,0:T(8,128)(2,1)S(1)} %pad_maximum_fusion.1.refs_0_, bf16[384,3072]{1,0:T(8,128)(2,1)} %collective-permute-done.17.refs_1_, ...), custom_call_target="tpu_custom_call" | custom-call | bytes 1179648 | tf_op jit(solution)/shard_map/pallas_call | solution.py:143
  303.9 10.1 %shard_map.409.mixed_ref = bf16[128,1536]{1,0:T(8,128)(2,1)} custom-call(bf16[128,1536]{1,0:T(8,128)(2,1)} %copy-done.33, bf16[512,1536]{1,0:T(8,128)(2,1)} %convolution_convert_fusion.refs_1_), custom_call_target="tpu_custom_call" | custom-call | flops 201326592 | bytes 2359296 | tf_op jit(solution)/shard_map/pallas_call | solution.py:629
  354.5 8.0 %collective-permute-done.46 = bf16[128,1536]{1,0:T(8,128)(2,1)S(1)} collective-permute-done((bf16[128,1536]{1,0:T(8,128)(2,1)S(1)}, bf16[128,1536]{1,0:T(8,128)(2,1)S(1)}, u32[]{:S(2)}, u32[]{:S(2)}) %collective-permute-start.46) | collective-permute-done | bytes 393248 | tf_op jit(solution)/shard_map/ppermute | solution.py:77
  369.3 13.9 %shard_map.411 = (bf16[1024,384]{1,0:T(8,128)(2,1)S(1)}, bf16[1024,384]{1,0:T(8,128)(2,1)S(1)}, bf16[1024,384]{1,0:T(8,128)(2,1)S(1)}, bf16[1024,1536]{1,0:T(8,128)(2,1)S(1)}, bf16[1024,1536]{1,0:T(8,128)(2,1)}) custom-call(bf16[1024,1536]{1,0:T(8,128)(2,1)} %copy-done.3, bf16[1024,1536]{1,0:T(8,128)(2,1)} %copy-done.10, bf16[384,1536]{1,0:T(8,128)(2,1)S(1)} %bitcast.86, ...), custom_call_target="tpu_custom_call" | custom-call | flops 1048576 | bytes 1048576 | tf_op jit(solution)/shard_map/pallas_call | solution.py:499
  389.2 13.9 %shard_map.412 = (bf16[1024,384]{1,0:T(8,128)(2,1)S(1)}, bf16[1024,384]{1,0:T(8,128)(2,1)S(1)}, bf16[1024,384]{1,0:T(8,128)(2,1)S(1)}, bf16[1024,1536]{1,0:T(8,128)(2,1)S(1)}, bf16[1024,1536]{1,0:T(8,128)(2,1)}) custom-call(bf16[1024,1536]{1,0:T(8,128)(2,1)} %copy-done.5, bf16[1024,1536]{1,0:T(8,128)(2,1)} %copy-done.12, bf16[384,1536]{1,0:T(8,128)(2,1)S(1)} %bitcast.87, ...), custom_call_target="tpu_custom_call" | custom-call | flops 1048576 | bytes 1048576 | tf_op jit(solution)/shard_map/pallas_call | solution.py:499
  474.8 13.3 %shard_map.417 = (bf16[128,1536]{1,0:T(8,128)(2,1)}, bf16[512,1536]{1,0:T(8,128)(2,1)}) custom-call(bf16[128,1536]{1,0:T(8,128)(2,1)} %copy-done.33, bf16[512,1536]{1,0:T(8,128)(2,1)} %convolution_convert_fusion.refs_1_, bf16[128,1536]{1,0:T(8,128)(2,1)} %copy-done.60), custom_call_target="tpu_custom_call" | custom-call | flops 503316480 | bytes 4325376 | tf_op jit(solution)/shard_map/pallas_call | solution.py:685
  497.2 6.9 shard_map.418
  520.3 13.6 %shard_map.419 = (bf16[128,1536]{1,0:T(8,128)(2,1)}, bf16[512,1536]{1,0:T(8,128)(2,1)}) custom-call(bf16[128,1536]{1,0:T(8,128)(2,1)} %copy-done.32, bf16[512,1536]{1,0:T(8,128)(2,1)} %constant_dynamic-update-slice_fusion.5.refs_1_, bf16[128,1536]{1,0:T(8,128)(2,1)} %copy-done.59, f32[128,128]{1,0:T(8,128)} %copy-done.36, ...), custom_call_target="tpu_custom_call" | custom-call | flops 503316480 | bytes 4325376 | tf_op jit(solution)/shard_map/pallas_call | solution.py:685
  562.9 10.2 %shard_map.421 = (f32[128,1536]{1,0:T(8,128)}, f32[1,1536]{1,0:T(1,128)S(1)}, f32[1,1536]{1,0:T(1,128)S(1)}) custom-call(bf16[128,4608]{1,0:T(8,128)(2,1)S(1)} %copy-done.14, f32[128,1536]{1,0:T(8,128)S(1)} %get-tuple-element.757.grad_ref, f32[128,1536]{1,0:T(8,128)S(1)} %copy-done.38, f32[128,1]{1,0:T(8,128)S(1)} %copy-done.64, ...), custom_call_target="tpu_custom_call" | custom-call | flops 1048576 | bytes 1048576 | tf_op jit(solution)/shard_map/pallas_call | solution.py:464
  607.5 10.8 %collective-permute-done.85 = bf16[96,1536]{1,0:T(8,128)(2,1)} collective-permute-done((bf16[96,1536]{1,0:T(8,128)(2,1)}, bf16[96,1536]{1,0:T(8,128)(2,1)}, u32[]{:S(2)}, u32[]{:S(2)}) %collective-permute-start.85) | collective-permute-done | bytes 294944 | tf_op jit(solution)/shard_map/ppermute | solution.py:77
  627.0 7.0 collective-permute-done.87
  647.8 32.6 %collective-permute-done.93 = f32[8,8,128]{2,1,0:T(8,128)S(1)} collective-permute-done((f32[8,8,128]{2,1,0:T(8,128)S(1)}, f32[8,8,128]{2,1,0:T(8,128)S(1)}, u32[]{:S(2)}, u32[]{:S(2)}) %collective-permute-start.93) | collective-permute-done | bytes 32800 | tf_op jit(solution)/shard_map/ppermute | solution.py:77
  689.1 12.3 %collective-permute-done.98 = f32[4,8,128]{2,1,0:T(8,128)S(1)} collective-permute-done((f32[4,8,128]{2,1,0:T(8,128)S(1)}, f32[4,8,128]{2,1,0:T(8,128)S(1)}, u32[]{:S(2)}, u32[]{:S(2)}) %collective-permute-start.98) | collective-permute-done | bytes 16416 | tf_op jit(solution)/shard_map/ppermute | solution.py:77
  725.4 10.4 %collective-permute-done.104 = bf16[112,1536]{1,0:T(8,128)(2,1)S(1)} collective-permute-done((bf16[112,1536]{1,0:T(8,128)(2,1)S(1)}, bf16[112,1536]{1,0:T(8,128)(2,1)S(1)}, u32[]{:S(2)}, u32[]{:S(2)}) %collective-permute-start.104) | collective-permute-done | bytes 344096 | tf_op jit(solution)/shard_map/ppermute | solution.py:77
  735.7 8.2 %collective-permute-done.100 = bf16[96,2048]{1,0:T(8,128)(2,1)S(1)} collective-permute-done((bf16[96,2048]{1,0:T(8,128)(2,1)S(1)}, bf16[96,2048]{1,0:T(8,128)(2,1)S(1)}, u32[]{:S(2)}, u32[]{:S(2)}) %collective-permute-start.100) | collective-permute-done | bytes 393248 | tf_op jit(solution)/shard_map/ppermute | solution.py:77
  752.4 8.8 %collective-permute-done.106 = bf16[48,2048]{1,0:T(8,128)(2,1)S(1)} collective-permute-done((bf16[48,2048]{1,0:T(8,128)(2,1)S(1)}, bf16[48,2048]{1,0:T(8,128)(2,1)S(1)}, u32[]{:S(2)}, u32[]{:S(2)}) %collective-permute-start.106) | collective-permute-done | bytes 196640 | tf_op jit(solution)/shard_map/ppermute | solution.py:77
  (779 shorter events, 424.0 us)
Async XLA Ops:
  31.3 34.1 %collective-permute-start.3 = (bf16[96,4736]{1,0:T(8,128)(2,1)S(1)}, bf16[96,4736]{1,0:T(8,128)(2,1)S(1)}, u32[]{:S(2)}, u32[]{:S(2)}) collective-permute-start(bf16[96,4736]{1,0:T(8,128)(2,1)S(1)} %pad_maximum_fusion.25), channel_id=1, source_target_pairs={{0,8},{1,9},{2,10},{3,11},{4,12},{5,13},{6,14},{7,15},{8,0},{9,1},... | collective-permute-start | bytes 2727944 | tf_op jit(solution)/shard_map/ppermute | solution.py:77
  32.2 39.0 %collective-permute-start.1 = (bf16[48,6144]{1,0:T(8,128)(2,1)S(1)}, bf16[48,6144]{1,0:T(8,128)(2,1)S(1)}, u32[]{:S(2)}, u32[]{:S(2)}) collective-permute-start(bf16[48,6144]{1,0:T(8,128)(2,1)S(1)} %maximum_maximum_fusion), channel_id=1, source_target_pairs={{0,16},{1,17},{2,18},{3,19},{4,20},{5,21},{6,22},{7,23},{8,24},{9,... | collective-permute-start | bytes 1769480 | tf_op jit(solution)/shard_map/ppermute | solution.py:77
  71.3 34.5 %collective-permute-start.2 = (bf16[96,6144]{1,0:T(8,128)(2,1)S(1)}, bf16[96,6144]{1,0:T(8,128)(2,1)S(1)}, u32[]{:S(2)}, u32[]{:S(2)}) collective-permute-start(bf16[96,6144]{1,0:T(8,128)(2,1)S(1)} %pad_maximum_fusion.19), channel_id=1, source_target_pairs={{0,8},{1,9},{2,10},{3,11},{4,12},{5,13},{6,14},{7,15},{8,0},{9,1},... | collective-permute-start | bytes 3538952 | tf_op jit(solution)/shard_map/ppermute | solution.py:77
  90.6 52.3 %collective-permute-start.8 = (bf16[384,2304]{1,0:T(8,128)(2,1)S(1)}, bf16[384,2304]{1,0:T(8,128)(2,1)}, u32[]{:S(2)}, u32[]{:S(2)}) collective-permute-start(bf16[384,2304]{1,0:T(8,128)(2,1)S(1)} %pad_maximum_fusion.8.refs_4_), channel_id=1, source_target_pairs={{0,2},{1,3},{2,0},{3,1},{4,6},{5,7},{6,4},{7,5},{8,10},{9,11},{10,... | collective-permute-start | bytes 5308424 | tf_op jit(solution)/shard_map/ppermute | solution.py:77
  91.2 51.7 %collective-permute-start.10 = (bf16[384,2304]{1,0:T(8,128)(2,1)S(1)}, bf16[384,2304]{1,0:T(8,128)(2,1)S(1)}, u32[]{:S(2)}, u32[]{:S(2)}) collective-permute-start(bf16[384,2304]{1,0:T(8,128)(2,1)S(1)} %pad_maximum_fusion.8.refs_4_), channel_id=1, source_target_pairs={{0,1},{1,0},{2,3},{3,2},{4,5},{5,4},{6,7},{7,6},{8,9},{9,8},{10,11... | collective-permute-start | bytes 5308424 | tf_op jit(solution)/shard_map/ppermute | solution.py:77
  91.2 52.9 %collective-permute-start.7 = (bf16[384,2432]{1,0:T(8,128)(2,1)S(1)}, bf16[384,2432]{1,0:T(8,128)(2,1)S(1)}, u32[]{:S(2)}, u32[]{:S(2)}) collective-permute-start(bf16[384,2432]{1,0:T(8,128)(2,1)S(1)} %pad_maximum_fusion.4.refs_0_), channel_id=1, source_target_pairs={{0,4},{1,5},{2,6},{3,7},{4,0},{5,1},{6,2},{7,3},{8,12},{9,13},{10,... | collective-permute-start | bytes 5603336 | tf_op jit(solution)/shard_map/ppermute | solution.py:77
  92.0 52.1 %collective-permute-start.9 = (bf16[384,2432]{1,0:T(8,128)(2,1)S(1)}, bf16[384,2432]{1,0:T(8,128)(2,1)S(1)}, u32[]{:S(2)}, u32[]{:S(2)}) collective-permute-start(bf16[384,2432]{1,0:T(8,128)(2,1)S(1)} %pad_maximum_fusion.4.refs_0_), channel_id=1, source_target_pairs={{0,1},{1,0},{2,3},{3,2},{4,5},{5,4},{6,7},{7,6},{8,9},{9,8},{10,11... | collective-permute-start | bytes 5603336 | tf_op jit(solution)/shard_map/ppermute | solution.py:77
  105.8 37.1 %collective-permute-start.11 = (bf16[272,1536]{1,0:T(8,128)(2,1)S(1)}, bf16[272,1536]{1,0:T(8,128)(2,1)S(1)}, u32[]{:S(2)}, u32[]{:S(2)}) collective-permute-start(bf16[272,1536]{1,0:T(8,128)(2,1)S(1)} %pad_maximum_fusion.27), channel_id=1, source_target_pairs={{0,16},{1,17},{2,18},{3,19},{4,20},{5,21},{6,22},{7,23},{8,24},{9,... | collective-permute-start | bytes 2506760 | tf_op jit(solution)/shard_map/ppermute | solution.py:77
  145.4 30.7 %collective-permute-start.14 = (bf16[384,2432]{1,0:T(8,128)(2,1)S(1)}, bf16[384,2432]{1,0:T(8,128)(2,1)}, u32[]{:S(2)}, u32[]{:S(2)}) collective-permute-start(bf16[384,2432]{1,0:T(8,128)(2,1)S(1)} %collective-permute-done.7.refs_1_), channel_id=1, source_target_pairs={{0,1},{1,0},{2,3},{3,2},{4,5},{5,4},{6,7},{7,6},{8,9},{9,8},{10,11... | collective-permute-start | bytes 5603336 | tf_op jit(solution)/shard_map/ppermute | solution.py:77
  145.5 30.6 %collective-permute-start.15 = (bf16[384,2304]{1,0:T(8,128)(2,1)}, bf16[384,2304]{1,0:T(8,128)(2,1)}, u32[]{:S(2)}, u32[]{:S(2)}) collective-permute-start(bf16[384,2304]{1,0:T(8,128)(2,1)} %collective-permute-done.8.refs_5_), channel_id=1, source_target_pairs={{0,1},{1,0},{2,3},{3,2},{4,5},{5,4},{6,7},{7,6},{8,9},{9,8},{10,11... | collective-permute-start | bytes 5308424 | tf_op jit(solution)/shard_map/ppermute | solution.py:77
  180.6 52.5 %collective-permute-start.17 = (bf16[384,3072]{1,0:T(8,128)(2,1)S(1)}, bf16[384,3072]{1,0:T(8,128)(2,1)}, u32[]{:S(2)}, u32[]{:S(2)}) collective-permute-start(bf16[384,3072]{1,0:T(8,128)(2,1)S(1)} %pad_maximum_fusion.1.refs_0_), channel_id=1, source_target_pairs={{0,4},{1,5},{2,6},{3,7},{4,0},{5,1},{6,2},{7,3},{8,12},{9,13},{10,... | collective-permute-start | bytes 7077896 | tf_op jit(solution)/shard_map/ppermute | solution.py:77
  181.6 52.4 %collective-permute-start.18 = (bf16[384,3072]{1,0:T(8,128)(2,1)}, bf16[384,3072]{1,0:T(8,128)(2,1)}, u32[]{:S(2)}, u32[]{:S(2)}) collective-permute-start(bf16[384,3072]{1,0:T(8,128)(2,1)} %pad_maximum_fusion.2.refs_4_), channel_id=1, source_target_pairs={{0,2},{1,3},{2,0},{3,1},{4,6},{5,7},{6,4},{7,5},{8,10},{9,11},{10,... | collective-permute-start | bytes 7077896 | tf_op jit(solution)/shard_map/ppermute | solution.py:77
  183.1 50.9 %collective-permute-start.19 = (bf16[384,3072]{1,0:T(8,128)(2,1)S(1)}, bf16[384,3072]{1,0:T(8,128)(2,1)}, u32[]{:S(2)}, u32[]{:S(2)}) collective-permute-start(bf16[384,3072]{1,0:T(8,128)(2,1)S(1)} %pad_maximum_fusion.1.refs_0_), channel_id=1, source_target_pairs={{0,1},{1,0},{2,3},{3,2},{4,5},{5,4},{6,7},{7,6},{8,9},{9,8},{10,11... | collective-permute-start | bytes 7077896 | tf_op jit(solution)/shard_map/ppermute | solution.py:77
  183.1 50.9 %collective-permute-start.20 = (bf16[384,3072]{1,0:T(8,128)(2,1)}, bf16[384,3072]{1,0:T(8,128)(2,1)}, u32[]{:S(2)}, u32[]{:S(2)}) collective-permute-start(bf16[384,3072]{1,0:T(8,128)(2,1)} %pad_maximum_fusion.2.refs_4_), channel_id=1, source_target_pairs={{0,1},{1,0},{2,3},{3,2},{4,5},{5,4},{6,7},{7,6},{8,9},{9,8},{10,11... | collective-permute-start | bytes 7077896 | tf_op jit(solution)/shard_map/ppermute | solution.py:77
  516.7 34.5 %collective-permute-start.73 = (bf16[384,1536]{1,0:T(8,128)(2,1)}, bf16[384,1536]{1,0:T(8,128)(2,1)}, u32[]{:S(2)}, u32[]{:S(2)}) collective-permute-start(bf16[384,1536]{1,0:T(8,128)(2,1)} %convolution_convert_fusion.10), channel_id=1, source_target_pairs={{0,8},{1,9},{2,10},{3,11},{4,12},{5,13},{6,14},{7,15},{8,0},{9,1},... | collective-permute-start | bytes 3538952 | tf_op jit(solution)/shard_map/ppermute | solution.py:77
  518.3 32.9 %collective-permute-start.74 = (bf16[384,1536]{1,0:T(8,128)(2,1)}, bf16[384,1536]{1,0:T(8,128)(2,1)}, u32[]{:S(2)}, u32[]{:S(2)}) collective-permute-start(bf16[384,1536]{1,0:T(8,128)(2,1)} %convolution_convert_fusion.9), channel_id=1, source_target_pairs={{0,2},{1,3},{2,0},{3,1},{4,6},{5,7},{6,4},{7,5},{8,10},{9,11},{10,... | collective-permute-start | bytes 3538952 | tf_op jit(solution)/shard_map/ppermute | solution.py:77
  518.6 32.6 %collective-permute-start.75 = (bf16[384,1536]{1,0:T(8,128)(2,1)}, bf16[384,1536]{1,0:T(8,128)(2,1)}, u32[]{:S(2)}, u32[]{:S(2)}) collective-permute-start(bf16[384,1536]{1,0:T(8,128)(2,1)} %bitcast.21), channel_id=1, source_target_pairs={{0,4},{1,5},{2,6},{3,7},{4,0},{5,1},{6,2},{7,3},{8,12},{9,13},{10,... | collective-permute-start | bytes 3538952 | tf_op jit(solution)/shard_map/ppermute | solution.py:77
  637.0 43.4 %collective-permute-start.90 = (bf16[384,2048]{1,0:T(8,128)(2,1)S(1)}, bf16[384,2048]{1,0:T(8,128)(2,1)S(1)}, u32[]{:S(2)}, u32[]{:S(2)}) collective-permute-start(bf16[384,2048]{1,0:T(8,128)(2,1)S(1)} %pad_maximum_fusion.13), channel_id=1, source_target_pairs={{0,8},{1,9},{2,10},{3,11},{4,12},{5,13},{6,14},{7,15},{8,0},{9,1},... | collective-permute-start | bytes 4718600 | tf_op jit(solution)/shard_map/ppermute | solution.py:77
  637.1 43.3 %collective-permute-start.91 = (bf16[384,2048]{1,0:T(8,128)(2,1)S(1)}, bf16[384,2048]{1,0:T(8,128)(2,1)S(1)}, u32[]{:S(2)}, u32[]{:S(2)}) collective-permute-start(bf16[384,2048]{1,0:T(8,128)(2,1)S(1)} %pad_maximum_fusion.15), channel_id=1, source_target_pairs={{0,2},{1,3},{2,0},{3,1},{4,6},{5,7},{6,4},{7,5},{8,10},{9,11},{10,... | collective-permute-start | bytes 4718600 | tf_op jit(solution)/shard_map/ppermute | solution.py:77
  638.8 41.7 %collective-permute-start.92 = (bf16[384,2048]{1,0:T(8,128)(2,1)S(1)}, bf16[384,2048]{1,0:T(8,128)(2,1)S(1)}, u32[]{:S(2)}, u32[]{:S(2)}) collective-permute-start(bf16[384,2048]{1,0:T(8,128)(2,1)S(1)} %pad_maximum_fusion.17), channel_id=1, source_target_pairs={{0,4},{1,5},{2,6},{3,7},{4,0},{5,1},{6,2},{7,3},{8,12},{9,13},{10,... | collective-permute-start | bytes 4718600 | tf_op jit(solution)/shard_map/ppermute | solution.py:77
  641.0 39.4 %collective-permute-start.93 = (f32[8,8,128]{2,1,0:T(8,128)S(1)}, f32[8,8,128]{2,1,0:T(8,128)S(1)}, u32[]{:S(2)}, u32[]{:S(2)}) collective-permute-start(f32[8,8,128]{2,1,0:T(8,128)S(1)} %slice.1098), channel_id=1, source_target_pairs={{0,8},{1,9},{2,10},{3,11},{4,12},{5,13},{6,14},{7,15},{8,0},{9,1},... | collective-permute-start | bytes 98312 | tf_op jit(solution)/shard_map/ppermute | solution.py:77
  643.0 37.4 %collective-permute-start.94 = (bf16[96,1536]{1,0:T(8,128)(2,1)S(1)}, bf16[96,1536]{1,0:T(8,128)(2,1)S(1)}, u32[]{:S(2)}, u32[]{:S(2)}) collective-permute-start(bf16[96,1536]{1,0:T(8,128)(2,1)S(1)} %copy-done.119), channel_id=1, source_target_pairs={{0,16},{1,17},{2,18},{3,19},{4,20},{5,21},{6,22},{7,23},{8,24},{9,... | collective-permute-start | bytes 884744 | tf_op jit(solution)/shard_map/ppermute | solution.py:77
  712.1 31.9 %collective-permute-start.100 = (bf16[96,2048]{1,0:T(8,128)(2,1)S(1)}, bf16[96,2048]{1,0:T(8,128)(2,1)S(1)}, u32[]{:S(2)}, u32[]{:S(2)}) collective-permute-start(bf16[96,2048]{1,0:T(8,128)(2,1)S(1)} %get-tuple-element.834), channel_id=1, source_target_pairs={{0,16},{1,17},{2,18},{3,19},{4,20},{5,21},{6,22},{7,23},{8,24},{9,... | collective-permute-start | bytes 1179656 | tf_op jit(solution)/shard_map/ppermute | solution.py:77
  714.0 30.0 %collective-permute-start.101 = (bf16[96,2048]{1,0:T(8,128)(2,1)S(1)}, bf16[96,2048]{1,0:T(8,128)(2,1)S(1)}, u32[]{:S(2)}, u32[]{:S(2)}) collective-permute-start(bf16[96,2048]{1,0:T(8,128)(2,1)S(1)} %get-tuple-element.835), channel_id=1, source_target_pairs={{0,4},{1,5},{2,6},{3,7},{4,0},{5,1},{6,2},{7,3},{8,12},{9,13},{10,... | collective-permute-start | bytes 1179656 | tf_op jit(solution)/shard_map/ppermute | solution.py:77
  (237 other events, 2345.5 us)

commit v2 on v1

--- a/solution.py
+++ b/solution.py
@@ -8,7 +8,7 @@
 
 HEAD_DIM = 64
 LANES = 512
-UNITS = ["unit0", "unit1", "unit2", "unit3", "unit4", "unit5"]
+UNITS = ["unit0", "unit1", "unit2", "unit3", "unit4"]
 EPS = 1e-05
 NEG = -1e30
 B = "batch"
@@ -69,7 +69,7 @@
 
 
 def softmax_back(probs, prob_grad):
-    return probs * (prob_grad - jnp.sum(probs * prob_grad, -1, keepdims=True))
+    return probs * (prob_grad - jnp.sum(probs * prob_grad, 0, keepdims=True))
 
 
 def hop(value, mask):
@@ -145,10 +145,10 @@
         out_shape=[jax.ShapeDtypeStruct((total * rows, width), jnp.bfloat16) for width in widths],
         in_specs=[pl.BlockSpec(memory_space=pltpu.SMEM)]
         + [pl.BlockSpec(memory_space=pl.ANY)] * len(pieces),
-        out_specs=[pl.BlockSpec(memory_space=pl.ANY)] * len(widths),
+        out_specs=[pl.BlockSpec(memory_space=pltpu.HBM)] * len(widths),
         scratch_shapes=[pltpu.VMEM(piece.shape, jnp.bfloat16) for _, piece, _ in pieces]
         + [pltpu.SemaphoreType.DMA((len(pieces),)), pltpu.SemaphoreType.DMA((count,))],
-        compiler_params=pltpu.CompilerParams(vmem_limit_bytes=size + (4 << 20)),
+        compiler_params=pltpu.CompilerParams(vmem_limit_bytes=size + (2 << 20)),
         cost_estimate=pl.CostEstimate(flops=0, bytes_accessed=size // 16, transcendentals=0),
     )(me.reshape(1), *[piece for _, piece, _ in pieces])
 
@@ -237,8 +237,9 @@
     for step in zip(*orders):
         parts = yield tuple(parts)
         got = yield hops(parts, step)
-        parts = [jnp.concatenate(pair, 0) for pair in zip(parts, got)]
-    return jnp.concatenate(parts, 0)
+        pairs = list(zip(parts, got))
+        parts = [jnp.concatenate(pair, 0) for pair in pairs]
+    return sum(pairs, ())
 
 
 def double_list(value, masks):
@@ -277,12 +278,13 @@
     return jax.ShapeDtypeStruct(shape, dtype)
 
 
-BIG = pltpu.CompilerParams(vmem_limit_bytes=44 << 20)
+def room(mebibytes):
+    return pltpu.CompilerParams(vmem_limit_bytes=mebibytes << 20)
 
 
 def project(inputs, gain, shift, weight, tables, scale):
     rows, width = inputs.shape
-    block = width // 2
+    block = width
 
     def body(in_ref, gain_ref, shift_ref, cos_ref, sin_ref, weight_ref, *outs):
         query_ref, pair_ref, normed_ref, inverse_ref, hidden_ref = outs
@@ -303,26 +305,23 @@
             ]
             return [narrow(part * factor) for part in parts]
 
-        @pl.when(step < 2)
+        @pl.when(step == 0)
         def _():
             for j, part in enumerate(turned(scale)):
                 query_ref[:, 128 * j : 128 * j + 128] = part
 
-        @pl.when((step >= 2) & (step < 4))
+        @pl.when(step == 1)
         def _():
             for j, part in enumerate(turned(1.0)):
                 pair_ref[:, 128 * j : 128 * j + 128] = part
 
-        @pl.when(step >= 4)
+        @pl.when(step == 2)
         def _():
             pair_ref[...] = narrow(value)
 
-    def pair_place(i):
-        return (jnp.maximum(i // 2 - 1, 0), jnp.where(i < 2, 0, i % 2))
-
     return pl.pallas_call(
         body,
-        grid=(6,),
+        grid=(3,),
         out_shape=[
             like((rows, width), jnp.bfloat16),
             like((2 * rows, width), jnp.bfloat16),
@@ -339,13 +338,13 @@
             pl.BlockSpec((width, block), lambda i: (0, i)),
         ],
         out_specs=[
-            pl.BlockSpec((rows, block), lambda i: (0, jnp.minimum(i, 1))),
-            pl.BlockSpec((rows, block), pair_place),
+            pl.BlockSpec((rows, block), lambda i: (0, 0)),
+            pl.BlockSpec((rows, block), lambda i: (jnp.maximum(i - 1, 0), 0)),
             pl.BlockSpec((rows, width), lambda i: (0, 0)),
             pl.BlockSpec((rows, 1), lambda i: (0, 0)),
             pl.BlockSpec((rows, width), lambda i: (0, 0)),
         ],
-        compiler_params=BIG,
+        compiler_params=room(22),
         cost_estimate=hint(),
     )(inputs, gain, shift, *tables, weight)
 
@@ -401,14 +400,14 @@
         out_shape=shapes,
         in_specs=specs,
         out_specs=outs,
-        compiler_params=BIG,
+        compiler_params=room(16),
         cost_estimate=hint(),
     )(*args)
 
 
 def back(incoming, low, grads, normed, inverse, gain, out=None):
     rows, width = grads.shape
-    block = LANES if low is None or low.shape[1] == width else LANES // 2
+    block = LANES
     first = 0 if low is None else width // block
     last = 0 if out is None else width // LANES
     norm_step = max(first - 1, 0)
@@ -468,7 +467,7 @@
         in_specs=specs,
         out_specs=outs,
         scratch_shapes=[pltpu.VMEM((rows, width), jnp.float32)],
-        compiler_params=BIG,
+        compiler_params=room(24),
         cost_estimate=hint(),
     )(*args)
 
@@ -502,7 +501,7 @@
         out_shape=[like((count, units), jnp.bfloat16)] * 3 + [like((count, width), jnp.bfloat16)] * 2,
         in_specs=[wide, wide] + [whole(array) for array in args[2:]],
         out_specs=[thin] * 3 + [wide] * 2,
-        compiler_params=BIG,
+        compiler_params=room(24),
         cost_estimate=hint(),
     )(*args)
 
@@ -535,7 +534,7 @@
         out_shape=shapes,
         in_specs=specs + [whole(right) for right in rights],
         out_specs=outs,
-        compiler_params=BIG,
+        compiler_params=room(24),
         cost_estimate=hint(),
     )(*lefts, *rights)
 
@@ -568,6 +567,7 @@
         out_shape=jax.ShapeDtypeStruct((rows, 3 * width), jnp.bfloat16),
         in_specs=[table, table, pl.BlockSpec((rows, width), lambda i: (0, 0)), part, part],
         out_specs=pl.BlockSpec((rows, width), lambda i: (0, i)),
+        compiler_params=room(8),
         cost_estimate=pl.CostEstimate(
             flops=24 * query.size, bytes_accessed=16 * query.size, transcendentals=0
         ),
@@ -589,71 +589,68 @@
 
 
 def row_probs(asked, keys, seen):
-    scores = dot_t(asked, keys)
+    scores = dot_t(keys, asked)
     if seen is not None:
-        scores = jnp.where(jnp.concatenate([seen, seen], 0) > 0.5, scores, NEG)
-    expo = jnp.exp(scores - jnp.max(scores, -1, keepdims=True))
-    return expo / jnp.sum(expo, -1, keepdims=True)
-
-
-def pair_rows(ref, part, r, lanes, row_count, block_count):
-    keys = ref.shape[0] // (2 * row_count * block_count)
-    starts = [((2 * b + part) * row_count + r) * keys for b in range(block_count)]
-    return jnp.concatenate([ref[start : start + keys, lanes] for start in starts], 0)
-
-
-def attend(query, pairs, seen, row_count, block_count):
+        scores = jnp.where(jnp.concatenate([seen, seen], 1) > 0.5, scores, NEG)
+    expo = jnp.exp(scores - jnp.max(scores, 0, keepdims=True))
+    return expo * (1.0 / jnp.sum(expo, 0, keepdims=True))
+
+
+def pair_rows(refs, part, r, lanes, row_count):
+    keys = refs[0].shape[0] // (2 * row_count)
+    start = (part * row_count + r) * keys
+    return jnp.concatenate([ref[start : start + keys, lanes] for ref in refs], 0)
+
+
+def attend(query, pairs, seen, row_count):
     tokens, width = query.shape
     frames = tokens // row_count
-    keys = pairs.shape[0] // (2 * row_count)
+    count = len(pairs)
 
     def body(*refs):
-        query_ref, pair_ref = refs[:2]
-        out_ref = refs[-1]
+        query_ref, pair_refs, out_ref = refs[0], refs[1 : 1 + count], refs[-1]
         for r in range(row_count):
             span = slice(r * frames, (r + 1) * frames)
             for j in range(0, LANES, 128):
                 lanes = slice(j, j + 128)
                 asked = two_heads(query_ref[span, lanes])
-                key = pair_rows(pair_ref, 0, r, lanes, row_count, block_count)
-                value = pair_rows(pair_ref, 1, r, lanes, row_count, block_count)
-                probs = row_probs(asked, key, refs[2][r] if seen is not None else None)
-                out_ref[span, lanes] = narrow(one_row(dot(narrow(probs), value)))
+                key, value = [pair_rows(pair_refs, p, r, lanes, row_count) for p in range(2)]
+                probs = row_probs(asked, key, refs[1 + count][r] if seen is not None else None)
+                out_ref[span, lanes] = narrow(one_row(tdot(narrow(probs), value)))
 
     token_spec = pl.BlockSpec((tokens, LANES), lambda i: (0, i))
-    args = (query, pairs)
-    specs = [token_spec, pl.BlockSpec((pairs.shape[0], LANES), lambda i: (0, i))]
+    args = (query, *pairs)
+    specs = [token_spec] + [pl.BlockSpec((pairs[0].shape[0], LANES), lambda i: (0, i))] * count
     if seen is not None:
         args = args + (seen,)
-        specs.append(pl.BlockSpec(seen.shape, lambda i: (0, 0, 0)))
+        specs.append(whole(seen))
     return pl.pallas_call(
         body,
         grid=(width // LANES,),
-        out_shape=jax.ShapeDtypeStruct((tokens, width), jnp.bfloat16),
+        out_shape=like((tokens, width), jnp.bfloat16),
         in_specs=specs,
         out_specs=token_spec,
-        cost_estimate=pl.CostEstimate(
-            flops=8 * tokens * width * keys,
-            bytes_accessed=4 * query.size + 2 * pairs.size,
-            transcendentals=0,
-        ),
+        compiler_params=room(8),
+        cost_estimate=hint(),
     )(*args)
 
 
-def attend_back(query, pairs, seen, grads, tables, row_count, block_count, scale):
+def attend_back(query, pairs, seen, grads, tables, row_count, scale):
     tokens, width = query.shape
     frames = tokens // row_count
-    keys = pairs.shape[0] // (2 * row_count)
+    count = len(pairs)
+    block = pairs[0].shape[0]
+    keys = block // (2 * row_count)
 
     def body(*refs):
-        query_ref, pair_ref, grad_ref = refs[:3]
+        query_ref, grad_ref, pair_refs = refs[0], refs[1], refs[2 : 2 + count]
+        rest = refs[2 + count :]
         out_query, out_pair = refs[-2:]
 
         def put(part, r, lanes, value):
-            count = keys // block_count
-            for b in range(block_count):
-                start = ((2 * b + part) * row_count + r) * count
-                out_pair[start : start + count, lanes] = narrow(value[b * count : (b + 1) * count])
+            for b in range(count):
+                start = b * block + (part * row_count + r) * keys
+                out_pair[start : start + keys, lanes] = narrow(value[b * keys : (b + 1) * keys])
 
         for r in range(row_count):
             span = slice(r * frames, (r + 1) * frames)
@@ -661,42 +658,85 @@
                 lanes = slice(j, j + 128)
                 asked = two_heads(query_ref[span, lanes])
                 grad = two_heads(grad_ref[span, lanes])
-                key = pair_rows(pair_ref, 0, r, lanes, row_count, block_count)
-                value = pair_rows(pair_ref, 1, r, lanes, row_count, block_count)
-                probs = row_probs(asked, key, refs[5][r] if seen is not None else None)
-                score_grad = narrow(softmax_back(probs, dot_t(grad, value)))
-                back = one_row(dot(score_grad, key))
+                key, value = [pair_rows(pair_refs, p, r, lanes, row_count) for p in range(2)]
+                probs = row_probs(asked, key, rest[2][r] if seen is not None else None)
+                score_grad = narrow(softmax_back(probs, dot_t(value, grad)))
+                result = one_row(tdot(score_grad, key))
                 if tables is not None:
-                    back = spin(back, refs[3][span, :], refs[4][span, :])
-                out_query[span, lanes] = narrow(back * scale)
-                put(0, r, lanes, tdot(score_grad, asked))
-                put(1, r, lanes, tdot(narrow(probs), grad))
+                    result = spin(result, rest[0][span, :], rest[1][span, :])
+                out_query[span, lanes] = narrow(result * scale)
+                put(0, r, lanes, dot(score_grad, asked))
+                put(1, r, lanes, dot(narrow(probs), grad))
 
     token_spec = pl.BlockSpec((tokens, LANES), lambda i: (0, i))
-    pair_spec = pl.BlockSpec((pairs.shape[0], LANES), lambda i: (0, i))
-    specs = [token_spec, pair_spec, token_spec]
-    args = (query, pairs, grads)
+    specs = [token_spec] * 2 + [pl.BlockSpec((block, LANES), lambda i: (0, i))] * count
+    args = (query, grads, *pairs)
     if tables is not None:
-        specs = specs + [pl.BlockSpec((tokens, 128), lambda i: (0, 0))] * 2
+        specs = specs + [whole(table) for table in tables]
         args = args + tuple(tables)
     if seen is not None:
-        specs.append(pl.BlockSpec(seen.shape, lambda i: (0, 0, 0)))
+        specs.append(whole(seen))
         args = args + (seen,)
     return pl.pallas_call(
         body,
         grid=(width // LANES,),
-        out_shape=[
-            jax.ShapeDtypeStruct((tokens, width), jnp.bfloat16),
-            jax.ShapeDtypeStruct(pairs.shape, jnp.bfloat16),
-        ],
+        out_shape=[like((tokens, width), jnp.bfloat16), like((count * block, width), jnp.bfloat16)],
         in_specs=specs,
-        out_specs=[token_spec, pair_spec],
-        cost_estimate=pl.CostEstimate(
-            flops=20 * tokens * width * keys,
-            bytes_accessed=6 * query.size + 4 * pairs.size,
-            transcendentals=0,
-        ),
+        out_specs=[token_spec, pl.BlockSpec((count * block, LANES), lambda i: (0, i))],
+        compiler_params=room(12),
+        cost_estimate=hint(),
     )(*args)
+
+
+def multiply(left, right):
+    rows, depth = left.shape
+    width = right.shape[1]
+
+    def body(left_ref, right_ref, out_ref):
+        out_ref[...] = narrow(dot(left_ref[...], right_ref[...]))
+
+    return pl.pallas_call(
+        body,
+        grid=(width // LANES,),
+        out_shape=like((rows, width), jnp.bfloat16),
+        in_specs=[whole(left), pl.BlockSpec((depth, LANES), lambda i: (0, i))],
+        out_specs=pl.BlockSpec((rows, LANES), lambda i: (0, i)),
+        compiler_params=room(12),
+        cost_estimate=hint(),
+    )(left, right)
+
+
+def weight_sums(lefts, rights):
+    rows = lefts[0].shape[1] // 2
+    widths = [right.shape[1] for right in rights]
+    count = len(lefts)
+    if rows % 128:
+        sums = [narrow(tdot(left, right)) for left, right in zip(lefts, rights)]
+        sums = jnp.concatenate(sums, 1)
+        return sums[:rows], sums[rows:]
+
+    def body(*refs):
+        for half in range(2):
+
+            @pl.when(pl.program_id(0) == half)
+            def _():
+                start = 0
+                for left, right, width in zip(refs[:count], refs[count : 2 * count], widths):
+                    lanes = slice(start, start + width)
+                    refs[2 * count + half][:, lanes] = narrow(tdot(left[...], right[...]))
+                    start = start + width
+
+    specs = [pl.BlockSpec((left.shape[0], rows), lambda i: (0, i)) for left in lefts]
+    out = pl.BlockSpec((rows, sum(widths)), lambda i: (0, 0))
+    return pl.pallas_call(
+        body,
+        grid=(2,),
+        out_shape=[like((rows, sum(widths)), jnp.bfloat16)] * 2,
+        in_specs=specs + [whole(right) for right in rights],
+        out_specs=[out, out],
+        compiler_params=room(14),
+        cost_estimate=hint(),
+    )(*lefts, *rights)
 
 
 def order_matrix(size, rows, order, me):
@@ -769,83 +809,6 @@
     feed_sent = narrow(
         jnp.concatenate([feed_input.reshape(2 * units, width), feed_output, lift_rows], 0)
     )
-    known = [0]
-    for mask in batch_masks[:1:-1]:
-        group_one = jnp.concatenate([group_one, hop(group_one, mask)], 0)
-        if len(known) == 1:
-            group_one, group_two = lax.optimization_barrier((group_one, group_two))
-        group_two = jnp.concatenate([group_two, hop(group_two, mask)], 0)
-        known = known + [old ^ mask for old in known]
-    known = [known + [old ^ mask for old in known] for mask in (x_mask, y_mask)]
-
-    def pieces_of(columns, others):
-        halves = []
-        for h in range(2):
-            have = known[h]
-            pieces = [(columns[h], have), (others[h], [old ^ (y_mask, x_mask)[h] for old in have])]
-            halves.append(pieces)
-        return halves
-
-    def add_core(halves, got):
-        for h in range(2):
-            halves[h] = halves[h] + [
-                (piece, [old ^ seq_masks[0] for old in have])
-                for piece, (_, have) in zip(got[h], halves[h])
-            ]
-            for mask in seq_masks[1:]:
-                halves[h] = halves[h] + [
-                    (hop(piece, mask), [old ^ mask for old in have]) for piece, have in halves[h]
-                ]
-        return halves
-
-    core = seq_masks[0]
-    traffic = Traffic()
-    feed_cuts = [0, 3 * units // 4, 2 * units + units // 6, feed_sent.shape[0]]
-    if units % 192:
-        feed_cuts = [0, units, 2 * units, feed_sent.shape[0]]
-    feed_parts = [feed_sent[feed_cuts[p] : feed_cuts[p + 1]] for p in range(3)]
-    ones = (group_one[:, : 128 + split], group_one[:, 128 + split :])
-    got = volley(ones + (feed_parts[0],), [x_mask, y_mask, far[0]])
-    feed_got = [got[2]]
-    ones = tuple(jnp.concatenate(pair, 0) for pair in zip(ones, got))
-    got_one = volley(ones + ones + (feed_parts[1],), [y_mask, x_mask, core, core, far[0]])
-    feed_got.append(got_one[4])
-    twos = (group_two[:, : 2 * width], group_two[:, 2 * width :])
-    got = volley(
-        twos + got_one[:2] + (feed_parts[2],), [x_mask, y_mask, core, core, far[0]]
-    )
-    feed_got.append(got[4])
-    twos = tuple(jnp.concatenate(pair, 0) for pair in zip(twos, got))
-    halves = pieces_of(ones, got_one[:2])
-    halves = add_core(halves, ((got_one[2], got[2]), (got_one[3], got[3])))
-    new = {"two": once(twos + twos, [y_mask, x_mask, core, core])}
-    pieces = traffic.turn([piece for have in halves for piece, _ in have], lambda done: new)
-    count = len(pieces) // 2
-    halves = [
-        [(piece, have) for piece, (_, have) in zip(pieces[h * count : (h + 1) * count], halves[h])]
-        for h in range(2)
-    ]
-    packed, triple_low = settle(
-        halves, [[(0, 0, 0, 128), (128, 1, 0, split)], [(0, 1, split, split)]], [128, 3 * width], me
-    )
-    packed = dot_t(jnp.eye(8, 128, dtype=jnp.bfloat16), packed)
-    gain_one, shift_one, gain_two, shift_two, gain_three, shift_three, drop_bias = [
-        packed[j : j + 1] for j in range(7)
-    ]
-
-    def cut_tokens(value):
-        return [value[cuts[p] : cuts[p + 1]] for p in range(3)]
-
-    def token_pairs(value):
-        pairs = []
-        for p in range(3):
-            first, last = near_count * cuts[p], near_count * cuts[p + 1]
-            middle = (first + last) // 2
-            pairs.append((narrow(value[first:middle]), narrow(value[middle:last])))
-        return pairs
-
-    upstream_tokens = upstream.reshape(token_count, width)
-
     own_places = seq_place * frame_count + jnp.arange(frame_count, dtype=jnp.int32)
     key_order = masks_of(seq_masks)
     key_places = jnp.concatenate(
@@ -853,7 +816,7 @@
     )
     own_clip, own_offset = clip_tables(clip_frames, own_places)
     key_clip = clip_tables(clip_frames, key_places)[0]
-    seen = widen(own_clip[:, :, None] == key_clip[:, None, :])
+    seen = widen(own_clip[:, None, :] == key_clip[:, :, None])
     prompt_flat = prompt.reshape(-1, prompt.shape[2])
     rows = cross_memory.shape[0]
     place = jnp.arange(prompt.shape[2], dtype=jnp.int32)
@@ -867,48 +830,143 @@
     turn_tables = spin_tables(own_offset, 1.0)
     back_tables = spin_tables(own_offset, -1.0)
 
+    def turn_rows(rows, matrix):
+        return narrow(dot(rows, matrix))
+
+    turned_memory = turn_rows(
+        prompt_flat, order_matrix(prompt.shape[2], cross_memory.shape[0], tail_orders[2], me)
+    )
+    turned_memory = jnp.concatenate([turned_memory] * seq_count, 0)
+    matrices = [order_matrix(width, share, order, me) for order in tail_orders]
+    upstream_tokens = upstream.reshape(token_count, width)
+    grad_drop_bias = jnp.sum(widen(upstream_tokens), 0, keepdims=True)
+    early = [prompt_spread, turned_memory, seen, grad_drop_bias]
+    early = early + matrices + list(turn_tables) + list(back_tables)
+
+    known = [0]
+    for mask in batch_masks[:1:-1]:
+        group_one = jnp.concatenate([group_one, hop(group_one, mask)], 0)
+        known = known + [old ^ mask for old in known]
+    known = [known + [old ^ mask for old in known] for mask in (x_mask, y_mask)]
+    group_one, group_two, *early = lax.optimization_barrier((group_one, group_two, *early))
+    prompt_spread, turned_memory, seen, grad_drop_bias = early[:4]
+    matrices, turn_tables, back_tables = early[4:7], early[7:9], early[9:]
+
+    def pieces_of(columns, others):
+        halves = []
+        for h in range(2):
+            have = known[h]
+            pieces = [(columns[h], have), (others[h], [old ^ (y_mask, x_mask)[h] for old in have])]
+            halves.append(pieces)
+        return halves
+
+    def add_core(halves, got):
+        for h in range(2):
+            halves[h] = halves[h] + [
+                (piece, [old ^ seq_masks[0] for old in have])
+                for piece, (_, have) in zip(got[h], halves[h])
+            ]
+            for mask in seq_masks[1:]:
+                halves[h] = halves[h] + [
+                    (hop(piece, mask), [old ^ mask for old in have]) for piece, have in halves[h]
+                ]
+        return halves
+
+    core = seq_masks[0]
+    traffic = Traffic()
+    feed_parts = [feed_sent[2 * units :], feed_sent[: 2 * units]]
+    ones = (group_one[:, : 128 + split], group_one[:, 128 + split :])
+    group_two = gather(group_two, batch_masks[:2:-1])
+    got = volley(ones, [x_mask, y_mask])
+    ones = tuple(jnp.concatenate(pair, 0) for pair in zip(ones, got))
+    got = volley(
+        ones + (feed_parts[0], group_two, ones[0]),
+        [y_mask, x_mask, far[0], batch_masks[2], core],
+    )
+    feed_got = [got[2]]
+    group_two = jnp.concatenate([group_two, got[3]], 0)
+    twos = (group_two[:, : 2 * width], group_two[:, 2 * width :])
+    got_one = got[:2] + got[4:]
+    got = volley(
+        twos + (ones[1],) + got_one[:2], [x_mask, y_mask, core, core, core]
+    )
+    got_one = got_one + got[2:]
+    twos = tuple(jnp.concatenate(pair, 0) for pair in zip(twos, got))
+    halves = pieces_of(ones, got_one[:2])
+    halves = add_core(halves, ((got_one[2], got_one[4]), (got_one[3], got_one[5])))
+    new = {
+        "two": once(twos + twos[:1], [y_mask, x_mask, core]),
+        "feed": once(feed_parts[1:], far[:1]),
+    }
+    pieces = traffic.turn([piece for have in halves for piece, _ in have], lambda done: new)
+    count = len(pieces) // 2
+    halves = [
+        [(piece, have) for piece, (_, have) in zip(pieces[h * count : (h + 1) * count], halves[h])]
+        for h in range(2)
+    ]
+    packed, triple_low = settle(
+        halves, [[(0, 0, 0, 128), (128, 1, 0, split)], [(0, 1, split, split)]], [128, 3 * width], me
+    )
+    packed = dot_t(jnp.eye(8, 128, dtype=jnp.bfloat16), packed)
+    gain_one, shift_one, gain_two, shift_two, gain_three, shift_three, drop_bias = [
+        packed[j : j + 1] for j in range(7)
+    ]
+
+    def cut_tokens(value):
+        return [value[cuts[p] : cuts[p + 1]] for p in range(3)]
+
+    def token_pairs(value):
+        pairs = []
+        for p in range(3):
+            first, last = near_count * cuts[p], near_count * cuts[p + 1]
+            middle = (first + last) // 2
+            pairs.append((narrow(value[first:middle]), narrow(value[middle:last])))
+        return pairs
+
     inputs = frames.reshape(token_count, width)
     query, pairs, normed_one, inverse_one, hidden_one = project(
         inputs, gain_one, shift_one, triple_low, turn_tables, scale
     )
-    query, prompt_spread = traffic.turn(
-        (query, prompt_spread), lambda done: {"pairs": double_list(pairs, seq_masks)}, step=[]
+    query, normed_one = traffic.turn(
+        (query, normed_one),
+        lambda done: {"pairs": double_list(pairs, seq_masks)},
+        step=[],
     )
     for _ in seq_masks:
         (query,) = traffic.turn((query,), step=["pairs"])
-    pairs = jnp.concatenate(traffic.done["pairs"], 0)
-
-    def turn_rows(rows, order):
-        return narrow(dot(rows, order_matrix(rows.shape[1], rows.shape[1] // device_count, order, me)))
-
-    self_mixed = attend(query, pairs, seen, row_count, seq_count)
+    pairs = traffic.done["pairs"]
+    self_mixed = attend(query, pairs, seen, row_count)
 
     def started(done):
         return {
-            "last": once(done["two"][:2], [core, core]),
+            "last": once((twos[1],) + done["two"][:2], [core] * 3),
             "up": double_each(cut_tokens(upstream_tokens), near_orders),
         }
 
-    self_mixed, feed_sent, *feed_got = traffic.turn([self_mixed, feed_sent] + feed_got, started)
+    self_mixed, *feed_all = traffic.turn([self_mixed] + feed_parts + feed_got, started)
     got_two = traffic.done["two"]
-    feed_all = jnp.concatenate([feed_sent] + feed_got, 0)
+    feed_all.append(traffic.done["feed"][0])
+    far_count = len(masks_of(far))
+    unit_count = far_count * units
+    drop_low, value_low, gate_low = [
+        jnp.concatenate([part[rows : rows + units] for part in feed_all[p::2]], 0)
+        for p, rows in ((0, 0), (1, 0), (1, units))
+    ]
+    biases = [part[units : units + 2, :units] for part in feed_all[::2]]
+    biases = jnp.concatenate(biases, 1)
     for mask in far[1:]:
-        feed_all = jnp.concatenate([feed_all, hop(feed_all, mask)], 0)
-    feed_all = feed_all.reshape(-1, feed_sent.shape[0], width)
-    value_low, gate_low, drop_low = [
-        feed_all[:, j * units : (j + 1) * units].reshape(-1, width) for j in range(3)
-    ]
-    unit_count = drop_low.shape[0]
-    value_bias, gate_bias = [
-        widen(feed_all[:, 3 * units + j, :units].reshape(1, unit_count)) for j in range(2)
-    ]
+        drop_low, value_low, gate_low = [
+            jnp.concatenate([low, hop(low, mask)], 0) for low in (drop_low, value_low, gate_low)
+        ]
+        biases = jnp.concatenate([biases, hop(biases, mask)], 1)
+    value_bias, gate_bias = widen(biases[:1]), widen(biases[1:])
     self_mixed, value_low, gate_low, drop_low, value_bias, gate_bias = traffic.turn(
         (self_mixed, value_low, gate_low, drop_low, value_bias, gate_bias),
         lambda done: {"mixed": double_list(self_mixed, seq_masks)},
     )
     got = traffic.done["last"]
     halves = add_core(
-        pieces_of(twos, got_two[:2]), ((got_two[2], got[0]), (got_two[3], got[1]))
+        pieces_of(twos, got_two[:2]), ((got_two[2], got[1]), (got[0], got[2]))
     )
     lows = settle(
         halves,
@@ -919,17 +977,14 @@
     self_low, ask_low, cross_low, memory_low, self_mixed = traffic.turn(
         (*lows, self_mixed), lambda done: {"hidden": double_list(hidden_one, seq_masks)}
     )
-    memory = narrow(dot(prompt_spread, memory_low))
     after_self, normed_two, inverse_two, hidden_two, asking = ahead(
         self_mixed, self_low, inputs, gain_two, shift_two, ask_low, scale
     )
-    cross_mixed = attend(asking, memory, None, row_count, 1)
+    asking, prompt_spread = lax.optimization_barrier((asking, prompt_spread))
+    memory = multiply(prompt_spread, memory_low)
+    cross_mixed = attend(asking, [memory], None, row_count)
     (cross_mixed,) = traffic.turn(
-        (cross_mixed,),
-        lambda done: {
-            "ups": double_list(done["up"], seq_masks),
-            "hidden_two": double_list(hidden_two, seq_masks),
-        },
+        (cross_mixed,), lambda done: {"asked": double_list(hidden_two, seq_masks)}
     )
     after_cross, normed_three, inverse_three, hidden_three = ahead(
         cross_mixed, cross_low, after_self, gain_three, shift_three
@@ -939,29 +994,34 @@
         (hidden_three, cross_mixed),
         lambda done: {
             "rows": double_each(cut_tokens(hidden_three), near_orders),
-            "cross_mixed": double_list(cross_mixed, seq_masks),
+            "crossed": double_list(cross_mixed, seq_masks),
         },
-    )
+        step=["asked"],
+    )
+    traffic.turn((), step=["rows", "crossed"])
+    up = jnp.concatenate(traffic.done["up"], 0)
+    traffic.turn((), lambda done: {"ups": double_list(up, seq_masks)}, step=["rows"])
     for _ in seq_masks[1:]:
-        traffic.turn((), step=["ups", "cross_mixed", "hidden_two", "hidden", "mixed"])
+        traffic.turn((), step=["asked", "crossed", "hidden", "mixed", "ups"])
+    hidden_all, mixed_all, asked_all, cross_all = [
+        jnp.concatenate(traffic.done[name], 0) for name in ("hidden", "mixed", "asked", "crossed")
+    ]
+    turned_triple = [turn_rows(hidden_all, matrix) for matrix in matrices]
+    turned_cross = turn_rows(cross_all, matrices[0])
+    turned_ask = turn_rows(asked_all, matrices[1])
+
+    def rows_there(done):
+        if "rows" not in done:
+            return {}
+        done["rows"] = jnp.concatenate(done["rows"], 0)
+        return {"all": double_list(done["rows"], seq_masks)}
+
+    turned_cross, turned_ask, mixed_all, *turned_triple = traffic.turn(
+        [turned_cross, turned_ask, mixed_all] + turned_triple, rows_there
+    )
+    while "rows" in traffic.flows:
+        traffic.turn((), rows_there)
     ups = traffic.done["ups"]
-    hidden_all, mixed_all, asked_all = [
-        jnp.concatenate(traffic.done[name], 0) for name in ("hidden", "mixed", "hidden_two")
-    ]
-    turned_triple = [turn_rows(hidden_all, order) for order in tail_orders]
-    turned_triple = traffic.turn(turned_triple)
-    cross_all = jnp.concatenate(traffic.done["cross_mixed"], 0)
-    turned_memory = turn_rows(prompt_flat, tail_orders[2])
-    turned_memory = jnp.concatenate([turned_memory] * seq_count, 0)
-    turned_cross = turn_rows(cross_all, tail_orders[0])
-    turned_ask = turn_rows(asked_all, tail_orders[1])
-    turned_self = [turn_rows(mixed_all, order) for order in tail_orders]
-    turned_cross, turned_ask, turned_memory, *turned_self = traffic.turn(
-        [turned_cross, turned_ask, turned_memory] + turned_self,
-        lambda done: {"all": double_list(done["rows"], seq_masks)} if "rows" in done else {},
-    )
-    while "rows" in traffic.flows:
-        traffic.turn((), lambda done: {"all": double_list(done["rows"], seq_masks)} if "rows" in done else {})
     lows = (value_low, gate_low, drop_low, value_bias, gate_bias)
     results = [feed_block(traffic.done["rows"], ups[0], *lows)]
     results[0] = traffic.turn(results[0])
@@ -977,7 +1037,6 @@
         return (yield from halve_pairs(token_pairs(value), near_orders))
 
     blocks = len(feed_rows)
-    far_count = len(masks_of(far))
     tied = traffic.turn(middles + value_grads + gate_grads, lambda done: {"back": back_flow()})
     middles, value_grads, gate_grads = tied[:blocks], tied[blocks : 2 * blocks], tied[2 * blocks :]
     drop_grad = unit_grad(middles, ups, False)[0]
@@ -987,35 +1046,50 @@
     drop_grad, value_grads, gate_grads = tied[0], tied[1 : 1 + blocks], tied[1 + blocks :]
     value_grad, value_bias_grad = unit_grad(value_grads, feed_rows, True)
     gate_grad, gate_bias_grad = unit_grad(gate_grads, feed_rows, True)
-    value_grad, gate_grad, drop_grad = traffic.turn(
-        (value_grad, gate_grad, drop_grad),
-        lambda done: {"term": halve_list(term_sums, seq_masks)},
-    )
-
-    def unit_rows(k):
-        rows = slice(k * units, (k + 1) * units)
-        bias = jnp.concatenate([value_bias_grad[:, rows], gate_bias_grad[:, rows]], 0)
-        bias = narrow(jnp.pad(bias, ((0, 14), (0, width - units))))
-        return jnp.concatenate([value_grad[rows], gate_grad[rows], drop_grad[rows], bias], 0)
-
-    unit_sums = [unit_rows(k) for k in range(far_count)]
-    unit_sums = list(traffic.turn(unit_sums))
+
+    def unit_blocks(grad):
+        return [grad[k * units : (k + 1) * units] for k in range(far_count)]
+
+    bias_grads = [
+        narrow(
+            jnp.pad(
+                jnp.concatenate(
+                    [bias[:, k * units : (k + 1) * units] for bias in (value_bias_grad, gate_bias_grad)], 0
+                ),
+                ((0, 14), (0, width - units)),
+            )
+        )
+        for k in range(far_count)
+    ]
+
+    def unit_flow(p):
+        blocks = unit_blocks((drop_grad, drop_grad, value_grad, value_grad, gate_grad)[p])
+        if p == 4:
+            blocks = [jnp.concatenate(pair, 0) for pair in zip(blocks, bias_grads)]
+            return halve_rows(blocks, 0, units + 16, far)
+        half = units // 2
+        return halve_rows(blocks, p % 2 * half, (p % 2 + 1) * half, far)
+
+    value_grad, gate_grad, drop_grad, mixed_all = traffic.turn(
+        (value_grad, gate_grad, drop_grad, mixed_all),
+        lambda done: {"term": halve_list(term_sums, seq_masks), "unit0": unit_flow(0)},
+    )
+    turned_self = [turn_rows(mixed_all, matrix) for matrix in matrices]
+
+    (*turned_self,) = traffic.turn(turned_self)
     for _ in seq_masks[1:]:
         traffic.turn((), step=["term"])
-    unit_cuts = [0] + [units // 2 * j for j in range(1, 6)] + [3 * units + 16]
-    if units % 32:
-        unit_cuts = [0] + [3 * units + 16] * 6
-
-    def unit_flow(p):
-        if unit_cuts[p] < unit_cuts[p + 1]:
-            return halve_rows(unit_sums, unit_cuts[p], unit_cuts[p + 1], far)
-
     while "back" in traffic.flows:
-        unit_sums = list(traffic.turn(unit_sums))
+        traffic.turn((), step=["back", "term"])
+
+    while "back" in traffic.flows:
+        unit_sums = list(traffic.turn(unit_sums, step=["back", "term"]))
     feed_back = jnp.concatenate(traffic.done["back"], 0)
     (feed_back,) = traffic.turn(
         (feed_back,),
-        lambda done: {"term_near": halve_pairs(token_pairs(done["term"]), near_orders)},
+        lambda done: {
+            "term_near": halve_pairs(token_pairs(done["term"]), near_orders),
+        },
     )
     cross_out_grad, grad_gain_three, grad_shift_three, cross_branch, cross_mixed_grad = back(
         feed_back, None, upstream_tokens, normed_three, inverse_three, gain_three, cross_low
@@ -1038,10 +1112,10 @@
 
     (cross_mixed_grad,) = traffic.turn(
         (cross_mixed_grad,),
-        lambda done: {"dc": double_list(cross_branch, seq_masks), "unit0": unit_flow(0)},
+        lambda done: {"dc": double_list(cross_branch, seq_masks), "unit1": unit_flow(1)},
     )
     asking_grad, memory_grad = attend_back(
-        asking, memory, None, cross_mixed_grad, None, row_count, 1, scale
+        asking, [memory], None, cross_mixed_grad, None, row_count, scale
     )
     asking_grad, memory_grad = traffic.turn(
         (asking_grad, memory_grad),
@@ -1057,7 +1131,7 @@
     )
     (self_mixed_grad,) = traffic.turn(
         (self_mixed_grad,),
-        lambda done: {"da": double_list(self_branch, seq_masks)},
+        lambda done: {"da": double_list(self_branch, seq_masks), "unit2": unit_flow(2)},
     )
     for _ in seq_masks[1:]:
         traffic.turn((), step=["dq", "dm", "da"])
@@ -1077,11 +1151,10 @@
         (self_mixed_grad, layer_output),
         lambda done: {
             "first": halve_pairs([cross_pair, ask_pair, memory_pair], tail_orders),
-            "unit1": unit_flow(1),
         },
     )
     query_back, pair_grad = attend_back(
-        query, pairs, seen, self_mixed_grad, back_tables, row_count, seq_count, scale
+        query, pairs, seen, self_mixed_grad, back_tables, row_count, scale
     )
 
     def shed_frames(value):
@@ -1105,11 +1178,6 @@
     )
     branch_all = jnp.concatenate(traffic.done["da"], 0)
     third = width // 3
-    self_pairs = [
-        weight_pair(turned, branch_all[:, p * third : (p + 1) * third])
-        for p, turned in enumerate(turned_self)
-    ]
-
     frame_grad, *sums = traffic.turn(
         (
             frame_grad,
@@ -1119,10 +1187,8 @@
             grad_shift_two,
             grad_gain_three,
             grad_shift_three,
-        ),
-        lambda done: {"unit2": unit_flow(2)},
-    )
-    grad_drop_bias = jnp.sum(widen(upstream_tokens), 0, keepdims=True)
+        )
+    )
     sums = jnp.concatenate(sums + [grad_drop_bias], 0).reshape(7, device_count, share)
     sums = jnp.transpose(sums, (1, 0, 2)).reshape(device_count, 7 * share)
     sums = jnp.pad(sums, ((0, 0), (0, 1024 - 7 * share)))
@@ -1133,12 +1199,16 @@
         traffic.turn((), step=["dt"])
     triple_all = jnp.concatenate(traffic.done["dt"], 0)
     triple_pairs = [
-        weight_pair(turned, triple_all[:, p * width : (p + 1) * width])
-        for p, turned in enumerate(turned_triple)
-    ]
-    triple_pairs = [
-        tuple(jnp.concatenate(item, 1) for item in zip(*pair))
-        for pair in zip(triple_pairs, self_pairs)
+        tuple(
+            weight_sums(
+                [turned_triple[p], turned_self[p]],
+                [
+                    triple_all[:, p * width : (p + 1) * width],
+                    branch_all[:, p * third : (p + 1) * third],
+                ],
+            )
+        )
+        for p in range(3)
     ]
     tied = traffic.turn(
         sum(triple_pairs, ()), lambda done: {"sums": halve_list_rows(sums, seq_masks)}
@@ -1154,25 +1224,25 @@
             "tail": halve_pairs(
                 triple_pairs + [(sums[:half], sums[half:])], tail_orders + [tail_orders[0]]
             ),
-            "unit3": unit_flow(3),
+            "unit4": unit_flow(4),
         },
     )
-    traffic.turn((), lambda done: {"unit4": unit_flow(4)})
-    traffic.turn((), lambda done: {"unit5": unit_flow(5)})
+    traffic.turn((), lambda done: {"unit3": unit_flow(3)})
     while traffic.flows:
         traffic.turn(())
     parts = traffic.done["tail"]
     grad_cross, grad_ask, grad_memory = traffic.done["first"]
     grad_self = jnp.concatenate([part[:, width:] for part in parts[:3]], 1)
-    unit_sums = jnp.concatenate([traffic.done[name] for name in UNITS if name in traffic.done], 0)
+    drop_sums = jnp.concatenate([traffic.done[name] for name in UNITS[:2]], 0)
+    value_sums = jnp.concatenate([traffic.done[name] for name in UNITS[2:4]], 0)
+    gate_sums = traffic.done[UNITS[4]]
     grad_triple = jnp.concatenate([part[:, :width] for part in parts[:3]], 1)
     sums = parts[3].reshape(1024)[: 7 * share].reshape(7, share)
     grad_memory = grad_memory.reshape(2, share // 2, width)[:, : cross_memory.shape[0]]
     grad_memory = jnp.concatenate([grad_memory[0], grad_memory[1]], 1)
-    grad_lift = unit_sums[: 2 * units].reshape(2, units, width)
-    grad_drop = unit_sums[2 * units : 3 * units]
-    grad_lift_bias = unit_sums[3 * units : 3 * units + 2, :units]
-
+    grad_lift = jnp.stack([value_sums, gate_sums[:units]], 0)
+    grad_drop = drop_sums
+    grad_lift_bias = gate_sums[units : units + 2, :units]
     shape = frames.shape
     return (
         layer_output.reshape(shape),

time: 776 us -> 667 us (0.86)
  other arithmetic: 87.8 us -> 49.2 us
  matrix products: 53.4 us -> 18.6 us
  Pallas kernels: 141 us -> 108 us
  local copies, waits for them, and re-layouts: 78.5 us -> 49.6 us
  waiting for transfers between devices: 303 us -> 327 us
    ppermute x109 -> x107, waiting for transfers between devices: 303 us -> 327 us  [hop(): return lax.ppermute(value, AX, [(i, i ^ mask) for i in range(count)])]
    dot_general x20 -> x8, matrix products: 25.5 us -> 4.12 us  [tdot(): lax.dot_general(left, right, (((0,), (0,)), ((), ())), preferred_element_...]
    pallas_call x5 -> x9, Pallas kernels: 56.4 us -> 40.7 us  [the longest x2 14.3 us: attend_back(): pl.pallas_call(body, grid=(width // LANES,), out_shape=[like((tokens, wid...]
    unnamed x325 -> x290, local copies, waits for them, and re-layouts: 48.8 us -> 33.5 us
    concatenate x26 -> x21, other arithmetic: 21.8 us -> 8.04 us  [the longest x3 3.43 us: local(): jnp.concatenate([part[rows:rows + units] for part in feed_all[p::2]], 0)]
    dot_general x12 -> x11, matrix products: 27.7 us -> 14.2 us  [dot(): lax.dot_general(left, right, (((1,), (0,)), ((), ())), preferred_element_...]
    convert_element_type x29, other arithmetic: 20.3 us -> 8.56 us  [narrow(): return value.astype(jnp.bfloat16)]
    ppermute x109 -> x107, starting transfers between devices: 102 us -> 98.6 us  [hop(): return lax.ppermute(value, AX, [(i, i ^ mask) for i in range(count)])]
  transfers between devices with their start and end apart: 109 -> 107, of which waited for: 47 -> 48; matrix products, arithmetic and copies ran while one was open for 14% -> 9% of each run, Pallas kernels for 17% -> 14%
where the time goes in v2:
time: 667 us; the launch traced here: 655 us
  waiting for transfers between devices  327 us (49%)
  Pallas kernels  108 us (16%)
  starting transfers between devices  98.6 us (15%)
  local copies, waits for them, and re-layouts  49.6 us (7%)
  other arithmetic  49.2 us (7%)
  matrix products  18.6 us (3%)
    ppermute x107, waiting for transfers between devices, hop(): return lax.ppermute(value, AX, [(i, i ^ mask) for i in range(count)])  327 us
    ppermute x107, starting transfers between devices, hop(): return lax.ppermute(value, AX, [(i, i ^ mask) for i in range(count)])  98.6 us
    unnamed x290, local copies, waits for them, and re-layouts  33.5 us
    pallas_call x2, Pallas kernels, feed_block(): pl.pallas_call(body, grid=(count // block,), out_shape=[like((count, unit...  23.2 us
    pallas_call x2, Pallas kernels, attend_back(): pl.pallas_call(body, grid=(width // LANES,), out_shape=[like((tokens, wid...  14.3 us
    dot_general x11, matrix products, dot(): lax.dot_general(left, right, (((1,), (0,)), ((), ())), preferred_element_...  14.2 us
    pallas_call x2, Pallas kernels, attend(): pl.pallas_call(body, grid=(width // LANES,), out_shape=like((tokens, widt...  14.1 us
    pallas_call x2, Pallas kernels, settle(): pl.pallas_call(body, out_shape=[jax.ShapeDtypeStruct((total * rows, width...  13.9 us
  transfers between devices with their start and end apart: 107, of which 48 were waited for; matrix products, arithmetic and copies ran while one was open for 9% of the time, Pallas kernels for 14%

profile of v2, /device:TPU:0, one launch (start us, length us, event | category | flops | bytes accessed | tf_op | source)
XLA Modules:
  0.0 654.7 jit_solution(15762990649649243303)
XLA Ops:
  31.2 20.4 %collective-permute-done.1 = bf16[96,4736]{1,0:T(8,128)(2,1)S(1)} collective-permute-done((bf16[96,4736]{1,0:T(8,128)(2,1)S(1)}, bf16[96,4736]{1,0:T(8,128)(2,1)S(1)}, u32[]{:S(2)}, u32[]{:S(2)}) %collective-permute-start.1) | collective-permute-done | bytes 909344 | tf_op jit(solution)/shard_map/ppermute | solution.py:77
  58.2 22.3 %collective-permute-done.2 = bf16[48,6144]{1,0:T(8,128)(2,1)S(1)} collective-permute-done((bf16[48,6144]{1,0:T(8,128)(2,1)S(1)}, bf16[48,6144]{1,0:T(8,128)(2,1)S(1)}, u32[]{:S(2)}, u32[]{:S(2)}) %collective-permute-start.2) | collective-permute-done | bytes 589856 | tf_op jit(solution)/shard_map/ppermute | solution.py:77
  88.1 35.8 %collective-permute-done.7 = bf16[208,1536]{1,0:T(8,128)(2,1)} collective-permute-done((bf16[208,1536]{1,0:T(8,128)(2,1)S(1)}, bf16[208,1536]{1,0:T(8,128)(2,1)}, u32[]{:S(2)}, u32[]{:S(2)}) %collective-permute-start.7) | collective-permute-done | bytes 639008 | tf_op jit(solution)/shard_map/ppermute | solution.py:77
  128.2 27.2 %collective-permute-done.10 = bf16[192,3072]{1,0:T(8,128)(2,1)S(1)} collective-permute-done((bf16[192,3072]{1,0:T(8,128)(2,1)S(1)}, bf16[192,3072]{1,0:T(8,128)(2,1)S(1)}, u32[]{:S(2)}, u32[]{:S(2)}) %collective-permute-start.10) | collective-permute-done | bytes 1179680 | tf_op jit(solution)/shard_map/ppermute | solution.py:77
  165.9 6.9 %shard_map.359 = (bf16[1536,128]{1,0:T(8,128)(2,1)S(1)}, bf16[1536,4608]{1,0:T(8,128)(2,1)S(1)}) custom-call(s32[1]{0:T(128)} %bitcast.13.me_ref, bf16[384,2432]{1,0:T(8,128)(2,1)S(1)} %pad_maximum_fusion.3.refs_0_, bf16[384,2432]{1,0:T(8,128)(2,1)S(1)} %collective-permute-done.5.refs_1_, bf16[384,2432]{1,0:T(8,128)(2,1)S(1)} %collective-permute-done.9.refs_2_, ...), custom_call_target="tpu_custom_call" | custom-call | bytes 909312 | tf_op jit(solution)/shard_map/pallas_call | solution.py:143
  181.2 7.0 %shard_map.361.mixed_ref = bf16[128,1536]{1,0:T(8,128)(2,1)S(1)} custom-call(bf16[128,1536]{1,0:T(8,128)(2,1)S(1)} %get-tuple-element.505.refs_0_, bf16[256,1536]{1,0:T(8,128)(2,1)S(1)} %get-tuple-element.503.refs_1_.refs_2_, bf16[256,1536]{1,0:T(8,128)(2,1)S(1)} %collective-permute-done.19.refs_2_.refs_3_, f32[2,128,64]{2,1,0:T(8,128)S(1)} %compare_convert_fusion.refs_3_.refs_6_), custom_call_target="tpu_custom_call" | custom-call | flops 1048576 | bytes 1048576 | tf_op jit(solution)/shard_map/pallas_call | solution.py:627
  188.2 26.1 %collective-permute-done.18 = bf16[384,1536]{1,0:T(8,128)(2,1)S(1)} collective-permute-done((bf16[384,1536]{1,0:T(8,128)(2,1)S(1)}, bf16[384,1536]{1,0:T(8,128)(2,1)S(1)}, u32[]{:S(2)}, u32[]{:S(2)}) %collective-permute-start.18) | collective-permute-done | bytes 1179680 | tf_op jit(solution)/shard_map/ppermute | solution.py:77
  234.2 7.0 %shard_map.362 = (bf16[1536,1536]{1,0:T(8,128)(2,1)S(1)}, bf16[1536,1536]{1,0:T(8,128)(2,1)S(1)}, bf16[1536,1536]{1,0:T(8,128)(2,1)S(1)}, bf16[1536,1536]{1,0:T(8,128)(2,1)}) custom-call(s32[1]{0:T(128)} %bitcast.13.me_ref, bf16[384,3072]{1,0:T(8,128)(2,1)S(1)} %copy-done.10, bf16[384,3072]{1,0:T(8,128)(2,1)S(1)} %copy-done.25, ...), custom_call_target="tpu_custom_call" | custom-call | bytes 1179648 | tf_op jit(solution)/shard_map/pallas_call | solution.py:143
  251.6 7.0 %shard_map.365.mixed_ref = bf16[128,1536]{1,0:T(8,128)(2,1)S(1)} custom-call(bf16[128,1536]{1,0:T(8,128)(2,1)S(1)} %get-tuple-element.567.refs_0_, bf16[512,1536]{1,0:T(8,128)(2,1)S(1)} %shard_map.364.refs_1_.refs_2_), custom_call_target="tpu_custom_call" | custom-call | flops 1048576 | bytes 1048576 | tf_op jit(solution)/shard_map/pallas_call | solution.py:627
  270.9 5.1 collective-permute-done.40
  289.7 7.6 %collective-permute-done.43 = bf16[128,1536]{1,0:T(8,128)(2,1)S(1)} collective-permute-done((bf16[128,1536]{1,0:T(8,128)(2,1)S(1)}, bf16[128,1536]{1,0:T(8,128)(2,1)S(1)}, u32[]{:S(2)}, u32[]{:S(2)}) %collective-permute-start.43) | collective-permute-done | bytes 393248 | tf_op jit(solution)/shard_map/ppermute | solution.py:77
  302.4 11.4 %shard_map.367 = (bf16[1024,384]{1,0:T(8,128)(2,1)S(1)}, bf16[1024,384]{1,0:T(8,128)(2,1)S(1)}, bf16[1024,384]{1,0:T(8,128)(2,1)S(1)}, bf16[1024,1536]{1,0:T(8,128)(2,1)S(1)}, bf16[1024,1536]{1,0:T(8,128)(2,1)S(1)}) custom-call(bf16[1024,1536]{1,0:T(8,128)(2,1)S(1)} %constant_dynamic-update-slice_fusion.11.row_ref.refs_2_, ...), custom_call_target="tpu_custom_call" | custom-call | flops 1048576 | bytes 1048576 | tf_op jit(solution)/shard_map/pallas_call | solution.py:498
  321.7 11.9 %shard_map.368 = (bf16[1024,384]{1,0:T(8,128)(2,1)S(1)}, bf16[1024,384]{1,0:T(8,128)(2,1)S(1)}, bf16[1024,384]{1,0:T(8,128)(2,1)S(1)}, bf16[1024,1536]{1,0:T(8,128)(2,1)}, bf16[1024,1536]{1,0:T(8,128)(2,1)S(1)}) custom-call(bf16[1024,1536]{1,0:T(8,128)(2,1)S(1)} %collective-permute-done.46.row_ref.refs_3_, bf16[1024,1536]{1,0:T(8,128)(2,1)S(1)} %copy-done.6, ...), custom_call_target="tpu_custom_call" | custom-call | flops 1048576 | bytes 1048576 | tf_op jit(solution)/shard_map/pallas_call | solution.py:498
  379.5 5.8 collective-permute-done.52
  413.1 7.0 %shard_map.373 = (bf16[128,1536]{1,0:T(8,128)(2,1)S(1)}, bf16[512,1536]{1,0:T(8,128)(2,1)S(1)}) custom-call(bf16[128,1536]{1,0:T(8,128)(2,1)S(1)} %copy-done.39, bf16[128,1536]{1,0:T(8,128)(2,1)S(1)} %get-tuple-element.715.refs_1_, bf16[512,1536]{1,0:T(8,128)(2,1)S(1)} %shard_map.364.refs_1_.refs_2_), custom_call_target="tpu_custom_call" | custom-call | flops 1048576 | bytes 1048576 | tf_op jit(solution)/shard_map/pallas_call | solution.py:680
  443.7 9.6 %collective-permute-done.73 = bf16[96,1536]{1,0:T(8,128)(2,1)S(1)} collective-permute-done((bf16[96,1536]{1,0:T(8,128)(2,1)S(1)}, bf16[96,1536]{1,0:T(8,128)(2,1)S(1)}, u32[]{:S(2)}, u32[]{:S(2)}) %collective-permute-start.73) | collective-permute-done | bytes 294944 | tf_op jit(solution)/shard_map/ppermute | solution.py:77
  455.8 7.3 %shard_map.375 = (bf16[128,1536]{1,0:T(8,128)(2,1)S(1)}, bf16[512,1536]{1,0:T(8,128)(2,1)S(1)}) custom-call(bf16[128,1536]{1,0:T(8,128)(2,1)S(1)} %copy-done.37, bf16[128,1536]{1,0:T(8,128)(2,1)S(1)} %get-tuple-element.755.refs_1_, bf16[256,1536]{1,0:T(8,128)(2,1)S(1)} %copy-done.17, bf16[256,1536]{1,0:T(8,128)(2,1)S(1)} %copy-done.19, ...), custom_call_target="tpu_custom_call" | custom-call | flops 1048576 | bytes 1048576 | tf_op jit(solution)/shard_map/pallas_call | solution.py:680
  466.3 15.0 %collective-permute-done.74 = bf16[384,1536]{1,0:T(8,128)(2,1)S(1)} collective-permute-done((bf16[384,1536]{1,0:T(8,128)(2,1)S(1)}, bf16[384,1536]{1,0:T(8,128)(2,1)S(1)}, u32[]{:S(2)}, u32[]{:S(2)}) %collective-permute-start.74) | collective-permute-done | bytes 1179680 | tf_op jit(solution)/shard_map/ppermute | solution.py:77
  487.1 6.3 shard_map.377
  528.4 7.4 %collective-permute-done.86 = bf16[48,1536]{1,0:T(8,128)(2,1)S(1)} collective-permute-done((bf16[48,1536]{1,0:T(8,128)(2,1)S(1)}, bf16[48,1536]{1,0:T(8,128)(2,1)S(1)}, u32[]{:S(2)}, u32[]{:S(2)}) %collective-permute-start.86) | collective-permute-done | bytes 147488 | tf_op jit(solution)/shard_map/ppermute | solution.py:77
  545.2 44.5 %collective-permute-done.92 = f32[8,8,128]{2,1,0:T(8,128)S(1)} collective-permute-done((f32[8,8,128]{2,1,0:T(8,128)S(1)}, f32[8,8,128]{2,1,0:T(8,128)S(1)}, u32[]{:S(2)}, u32[]{:S(2)}) %collective-permute-start.92) | collective-permute-done | bytes 32800 | tf_op jit(solution)/shard_map/ppermute | solution.py:77
  596.8 14.0 %collective-permute-done.97 = f32[4,8,128]{2,1,0:T(8,128)S(1)} collective-permute-done((f32[4,8,128]{2,1,0:T(8,128)S(1)}, f32[4,8,128]{2,1,0:T(8,128)S(1)}, u32[]{:S(2)}, u32[]{:S(2)}) %collective-permute-start.97) | collective-permute-done | bytes 16416 | tf_op jit(solution)/shard_map/ppermute | solution.py:77
  610.8 4.8 collective-permute-done.98
  623.3 15.2 %collective-permute-done.102 = f32[2,8,128]{2,1,0:T(8,128)S(1)} collective-permute-done((f32[2,8,128]{2,1,0:T(8,128)S(1)}, f32[2,8,128]{2,1,0:T(8,128)S(1)}, u32[]{:S(2)}, u32[]{:S(2)}) %collective-permute-start.102) | collective-permute-done | bytes 8224 | tf_op jit(solution)/shard_map/ppermute | solution.py:77
  (721 shorter events, 318.3 us)
Async XLA Ops:
  51.7 28.8 %collective-permute-start.2 = (bf16[48,6144]{1,0:T(8,128)(2,1)S(1)}, bf16[48,6144]{1,0:T(8,128)(2,1)S(1)}, u32[]{:S(2)}, u32[]{:S(2)}) collective-permute-start(bf16[48,6144]{1,0:T(8,128)(2,1)S(1)} %maximum_maximum_fusion), channel_id=1, source_target_pairs={{0,16},{1,17},{2,18},{3,19},{4,20},{5,21},{6,22},{7,23},{8,24},{9,... | collective-permute-start | bytes 1769480 | tf_op jit(solution)/shard_map/ppermute | solution.py:77
  55.1 25.5 %collective-permute-start.3 = (bf16[192,2432]{1,0:T(8,128)(2,1)S(1)}, bf16[192,2432]{1,0:T(8,128)(2,1)S(1)}, u32[]{:S(2)}, u32[]{:S(2)}) collective-permute-start(bf16[192,2432]{1,0:T(8,128)(2,1)S(1)} %slice.739), channel_id=1, source_target_pairs={{0,2},{1,3},{2,0},{3,1},{4,6},{5,7},{6,4},{7,5},{8,10},{9,11},{10,... | collective-permute-start | bytes 2801672 | tf_op jit(solution)/shard_map/ppermute | solution.py:77
  80.8 44.9 %collective-permute-start.5 = (bf16[384,2432]{1,0:T(8,128)(2,1)S(1)}, bf16[384,2432]{1,0:T(8,128)(2,1)S(1)}, u32[]{:S(2)}, u32[]{:S(2)}) collective-permute-start(bf16[384,2432]{1,0:T(8,128)(2,1)S(1)} %pad_maximum_fusion.3.refs_0_), channel_id=1, source_target_pairs={{0,4},{1,5},{2,6},{3,7},{4,0},{5,1},{6,2},{7,3},{8,12},{9,13},{10,... | collective-permute-start | bytes 5603336 | tf_op jit(solution)/shard_map/ppermute | solution.py:77
  82.4 43.3 %collective-permute-start.9 = (bf16[384,2432]{1,0:T(8,128)(2,1)S(1)}, bf16[384,2432]{1,0:T(8,128)(2,1)S(1)}, u32[]{:S(2)}, u32[]{:S(2)}) collective-permute-start(bf16[384,2432]{1,0:T(8,128)(2,1)S(1)} %pad_maximum_fusion.3.refs_0_), channel_id=1, source_target_pairs={{0,1},{1,0},{2,3},{3,2},{4,5},{5,4},{6,7},{7,6},{8,9},{9,8},{10,11... | collective-permute-start | bytes 5603336 | tf_op jit(solution)/shard_map/ppermute | solution.py:77
  82.4 43.3 %collective-permute-start.6 = (bf16[384,2304]{1,0:T(8,128)(2,1)S(1)}, bf16[384,2304]{1,0:T(8,128)(2,1)S(1)}, u32[]{:S(2)}, u32[]{:S(2)}) collective-permute-start(bf16[384,2304]{1,0:T(8,128)(2,1)S(1)} %pad_maximum_fusion.5.refs_4_), channel_id=1, source_target_pairs={{0,2},{1,3},{2,0},{3,1},{4,6},{5,7},{6,4},{7,5},{8,10},{9,11},{10,... | collective-permute-start | bytes 5308424 | tf_op jit(solution)/shard_map/ppermute | solution.py:77
  83.9 41.8 %collective-permute-start.8 = (bf16[96,6144]{1,0:T(8,128)(2,1)S(1)}, bf16[96,6144]{1,0:T(8,128)(2,1)S(1)}, u32[]{:S(2)}, u32[]{:S(2)}) collective-permute-start(bf16[96,6144]{1,0:T(8,128)(2,1)S(1)} %pad_maximum_fusion.9), channel_id=1, source_target_pairs={{0,8},{1,9},{2,10},{3,11},{4,12},{5,13},{6,14},{7,15},{8,0},{9,1},... | collective-permute-start | bytes 3538952 | tf_op jit(solution)/shard_map/ppermute | solution.py:77
  84.6 39.3 %collective-permute-start.7 = (bf16[208,1536]{1,0:T(8,128)(2,1)S(1)}, bf16[208,1536]{1,0:T(8,128)(2,1)}, u32[]{:S(2)}, u32[]{:S(2)}) collective-permute-start(bf16[208,1536]{1,0:T(8,128)(2,1)S(1)} %fusion.25), channel_id=1, source_target_pairs={{0,16},{1,17},{2,18},{3,19},{4,20},{5,21},{6,22},{7,23},{8,24},{9,... | collective-permute-start | bytes 1916936 | tf_op jit(solution)/shard_map/ppermute | solution.py:77
  126.0 29.6 %collective-permute-start.13 = (bf16[384,2432]{1,0:T(8,128)(2,1)S(1)}, bf16[384,2432]{1,0:T(8,128)(2,1)S(1)}, u32[]{:S(2)}, u32[]{:S(2)}) collective-permute-start(bf16[384,2432]{1,0:T(8,128)(2,1)S(1)} %collective-permute-done.5.refs_1_), channel_id=1, source_target_pairs={{0,1},{1,0},{2,3},{3,2},{4,5},{5,4},{6,7},{7,6},{8,9},{9,8},{10,11... | collective-permute-start | bytes 5603336 | tf_op jit(solution)/shard_map/ppermute | solution.py:77
  126.1 29.5 %collective-permute-start.12 = (bf16[384,2304]{1,0:T(8,128)(2,1)S(1)}, bf16[384,2304]{1,0:T(8,128)(2,1)S(1)}, u32[]{:S(2)}, u32[]{:S(2)}) collective-permute-start(bf16[384,2304]{1,0:T(8,128)(2,1)S(1)} %pad_maximum_fusion.5.refs_4_), channel_id=1, source_target_pairs={{0,1},{1,0},{2,3},{3,2},{4,5},{5,4},{6,7},{7,6},{8,9},{9,8},{10,11... | collective-permute-start | bytes 5308424 | tf_op jit(solution)/shard_map/ppermute | solution.py:77
  126.9 28.6 %collective-permute-start.14 = (bf16[384,2304]{1,0:T(8,128)(2,1)S(1)}, bf16[384,2304]{1,0:T(8,128)(2,1)S(1)}, u32[]{:S(2)}, u32[]{:S(2)}) collective-permute-start(bf16[384,2304]{1,0:T(8,128)(2,1)S(1)} %collective-permute-done.6.refs_5_), channel_id=1, source_target_pairs={{0,1},{1,0},{2,3},{3,2},{4,5},{5,4},{6,7},{7,6},{8,9},{9,8},{10,11... | collective-permute-start | bytes 5308424 | tf_op jit(solution)/shard_map/ppermute | solution.py:77
  126.9 28.4 %collective-permute-start.10 = (bf16[192,3072]{1,0:T(8,128)(2,1)S(1)}, bf16[192,3072]{1,0:T(8,128)(2,1)S(1)}, u32[]{:S(2)}, u32[]{:S(2)}) collective-permute-start(bf16[192,3072]{1,0:T(8,128)(2,1)S(1)} %get-tuple-element.463), channel_id=1, source_target_pairs={{0,2},{1,3},{2,0},{3,1},{4,6},{5,7},{6,4},{7,5},{8,10},{9,11},{10,... | collective-permute-start | bytes 3538952 | tf_op jit(solution)/shard_map/ppermute | solution.py:77
  127.5 28.1 %collective-permute-start.11 = (bf16[192,3072]{1,0:T(8,128)(2,1)S(1)}, bf16[192,3072]{1,0:T(8,128)(2,1)S(1)}, u32[]{:S(2)}, u32[]{:S(2)}) collective-permute-start(bf16[192,3072]{1,0:T(8,128)(2,1)S(1)} %get-tuple-element.464), channel_id=1, source_target_pairs={{0,4},{1,5},{2,6},{3,7},{4,0},{5,1},{6,2},{7,3},{8,12},{9,13},{10,... | collective-permute-start | bytes 3538952 | tf_op jit(solution)/shard_map/ppermute | solution.py:77
  157.7 56.6 %collective-permute-start.15 = (bf16[384,3072]{1,0:T(8,128)(2,1)S(1)}, bf16[384,3072]{1,0:T(8,128)(2,1)S(1)}, u32[]{:S(2)}, u32[]{:S(2)}) collective-permute-start(bf16[384,3072]{1,0:T(8,128)(2,1)S(1)} %pad_maximum_fusion.1.refs_0_), channel_id=1, source_target_pairs={{0,4},{1,5},{2,6},{3,7},{4,0},{5,1},{6,2},{7,3},{8,12},{9,13},{10,... | collective-permute-start | bytes 7077896 | tf_op jit(solution)/shard_map/ppermute | solution.py:77
  158.3 56.1 %collective-permute-start.16 = (bf16[384,3072]{1,0:T(8,128)(2,1)S(1)}, bf16[384,3072]{1,0:T(8,128)(2,1)S(1)}, u32[]{:S(2)}, u32[]{:S(2)}) collective-permute-start(bf16[384,3072]{1,0:T(8,128)(2,1)S(1)} %pad_maximum_fusion.refs_4_), channel_id=1, source_target_pairs={{0,2},{1,3},{2,0},{3,1},{4,6},{5,7},{6,4},{7,5},{8,10},{9,11},{10,... | collective-permute-start | bytes 7077896 | tf_op jit(solution)/shard_map/ppermute | solution.py:77
  159.8 54.6 %collective-permute-start.17 = (bf16[384,3072]{1,0:T(8,128)(2,1)S(1)}, bf16[384,3072]{1,0:T(8,128)(2,1)S(1)}, u32[]{:S(2)}, u32[]{:S(2)}) collective-permute-start(bf16[384,3072]{1,0:T(8,128)(2,1)S(1)} %pad_maximum_fusion.1.refs_0_), channel_id=1, source_target_pairs={{0,1},{1,0},{2,3},{3,2},{4,5},{5,4},{6,7},{7,6},{8,9},{9,8},{10,11... | collective-permute-start | bytes 7077896 | tf_op jit(solution)/shard_map/ppermute | solution.py:77
  159.8 54.6 %collective-permute-start.18 = (bf16[384,1536]{1,0:T(8,128)(2,1)S(1)}, bf16[384,1536]{1,0:T(8,128)(2,1)S(1)}, u32[]{:S(2)}, u32[]{:S(2)}) collective-permute-start(bf16[384,1536]{1,0:T(8,128)(2,1)S(1)} %bitcast.88), channel_id=1, source_target_pairs={{0,16},{1,17},{2,18},{3,19},{4,20},{5,21},{6,22},{7,23},{8,24},{9,... | collective-permute-start | bytes 3538952 | tf_op jit(solution)/shard_map/ppermute | solution.py:77
  453.3 27.9 %collective-permute-start.74 = (bf16[384,1536]{1,0:T(8,128)(2,1)S(1)}, bf16[384,1536]{1,0:T(8,128)(2,1)S(1)}, u32[]{:S(2)}, u32[]{:S(2)}) collective-permute-start(bf16[384,1536]{1,0:T(8,128)(2,1)S(1)} %convolution_convert_fusion.3), channel_id=1, source_target_pairs={{0,8},{1,9},{2,10},{3,11},{4,12},{5,13},{6,14},{7,15},{8,0},{9,1},... | collective-permute-start | bytes 3538952 | tf_op jit(solution)/shard_map/ppermute | solution.py:77
  453.3 28.0 %collective-permute-start.75 = (bf16[384,1536]{1,0:T(8,128)(2,1)S(1)}, bf16[384,1536]{1,0:T(8,128)(2,1)S(1)}, u32[]{:S(2)}, u32[]{:S(2)}) collective-permute-start(bf16[384,1536]{1,0:T(8,128)(2,1)S(1)} %convolution_convert_fusion.2), channel_id=1, source_target_pairs={{0,2},{1,3},{2,0},{3,1},{4,6},{5,7},{6,4},{7,5},{8,10},{9,11},{10,... | collective-permute-start | bytes 3538952 | tf_op jit(solution)/shard_map/ppermute | solution.py:77
  454.0 27.7 %collective-permute-start.76 = (bf16[384,1536]{1,0:T(8,128)(2,1)S(1)}, bf16[384,1536]{1,0:T(8,128)(2,1)S(1)}, u32[]{:S(2)}, u32[]{:S(2)}) collective-permute-start(bf16[384,1536]{1,0:T(8,128)(2,1)S(1)} %bitcast.90), channel_id=1, source_target_pairs={{0,4},{1,5},{2,6},{3,7},{4,0},{5,1},{6,2},{7,3},{8,12},{9,13},{10,... | collective-permute-start | bytes 3538952 | tf_op jit(solution)/shard_map/ppermute | solution.py:77
  538.9 50.8 %collective-permute-start.89 = (bf16[384,2048]{1,0:T(8,128)(2,1)S(1)}, bf16[384,2048]{1,0:T(8,128)(2,1)S(1)}, u32[]{:S(2)}, u32[]{:S(2)}) collective-permute-start(bf16[384,2048]{1,0:T(8,128)(2,1)S(1)} %get-tuple-element.836), channel_id=1, source_target_pairs={{0,8},{1,9},{2,10},{3,11},{4,12},{5,13},{6,14},{7,15},{8,0},{9,1},... | collective-permute-start | bytes 4718600 | tf_op jit(solution)/shard_map/ppermute | solution.py:77
  538.9 50.7 %collective-permute-start.90 = (bf16[384,2048]{1,0:T(8,128)(2,1)S(1)}, bf16[384,2048]{1,0:T(8,128)(2,1)S(1)}, u32[]{:S(2)}, u32[]{:S(2)}) collective-permute-start(bf16[384,2048]{1,0:T(8,128)(2,1)S(1)} %get-tuple-element.837), channel_id=1, source_target_pairs={{0,2},{1,3},{2,0},{3,1},{4,6},{5,7},{6,4},{7,5},{8,10},{9,11},{10,... | collective-permute-start | bytes 4718600 | tf_op jit(solution)/shard_map/ppermute | solution.py:77
  539.4 50.3 %collective-permute-start.91 = (bf16[384,2048]{1,0:T(8,128)(2,1)S(1)}, bf16[384,2048]{1,0:T(8,128)(2,1)S(1)}, u32[]{:S(2)}, u32[]{:S(2)}) collective-permute-start(bf16[384,2048]{1,0:T(8,128)(2,1)S(1)} %get-tuple-element.838), channel_id=1, source_target_pairs={{0,4},{1,5},{2,6},{3,7},{4,0},{5,1},{6,2},{7,3},{8,12},{9,13},{10,... | collective-permute-start | bytes 4718600 | tf_op jit(solution)/shard_map/ppermute | solution.py:77
  540.6 49.0 %collective-permute-start.93 = (bf16[208,1536]{1,0:T(8,128)(2,1)S(1)}, bf16[208,1536]{1,0:T(8,128)(2,1)S(1)}, u32[]{:S(2)}, u32[]{:S(2)}) collective-permute-start(bf16[208,1536]{1,0:T(8,128)(2,1)S(1)} %copy-done.101), channel_id=1, source_target_pairs={{0,16},{1,17},{2,18},{3,19},{4,20},{5,21},{6,22},{7,23},{8,24},{9,... | collective-permute-start | bytes 1916936 | tf_op jit(solution)/shard_map/ppermute | solution.py:77
  542.7 46.9 %collective-permute-start.92 = (f32[8,8,128]{2,1,0:T(8,128)S(1)}, f32[8,8,128]{2,1,0:T(8,128)S(1)}, u32[]{:S(2)}, u32[]{:S(2)}) collective-permute-start(f32[8,8,128]{2,1,0:T(8,128)S(1)} %slice.1029), channel_id=1, source_target_pairs={{0,8},{1,9},{2,10},{3,11},{4,12},{5,13},{6,14},{7,15},{8,0},{9,1},... | collective-permute-start | bytes 98312 | tf_op jit(solution)/shard_map/ppermute | solution.py:77
  (218 other events, 2246.5 us)

commit v3 on v2

--- a/solution.py
+++ b/solution.py
@@ -96,12 +96,12 @@
 
 
 def settle(halves, targets, widths, me):
-    pieces = [(h, piece, have) for h in range(2) for piece, have in halves[h]]
+    pieces = [(h, piece, have) for h in range(len(halves)) for piece, have in halves[h]]
     total = sum(len(have) for h, piece, have in pieces if h == 0)
     rows = pieces[0][1].shape[0] // len(pieces[0][2])
     if rows % 16:
         outs = [[] for _ in widths]
-        for h in range(2):
+        for h in range(len(halves)):
             have = sum([have for _, have in halves[h]], [])
             table = np.zeros(total, np.int32)
             table[np.array(have)] = np.arange(total)
@@ -157,6 +157,7 @@
     def __init__(self):
         self.flows = {}
         self.done = {}
+        self.count = {}
 
     def turn(self, outs, new=None, step=None):
         names = list(self.flows) if step is None else [n for n in step if n in self.flows]
@@ -178,6 +179,7 @@
         sents = sum([sent for _, _, sent in started], ())
         tied = lax.optimization_barrier(sents + outs)
         for name, flow, sent in started:
+            self.count[name] = self.count.get(name, 0) + 1
             self.flows[name] = (flow, flow.send(tied[: len(sent)]))
             tied = tied[len(sent) :]
         return tied
@@ -203,15 +205,6 @@
             pair = [widen(kept[cut]) + widen(part[cut]) for cut in (slice(half), slice(half, None))]
             pairs.append(pair if kept.ndim == 3 else [narrow(item) for item in pair])
     return [widen(kept) + widen(part) for kept, part in sums]
-
-
-def halve_list_rows(value, masks):
-    for mask in reversed(masks):
-        half = value.shape[0] // 2
-        sent = yield (value[half:],)
-        (got,) = yield hops(sent, (mask,))
-        value = value[:half] + got
-    return value
 
 
 def halve_list(blocks, masks):
@@ -405,7 +398,7 @@
     )(*args)
 
 
-def back(incoming, low, grads, normed, inverse, gain, out=None):
+def back(incoming, low, grads, normed, inverse, gain, out=None, place=0):
     rows, width = grads.shape
     block = LANES
     first = 0 if low is None else width // block
@@ -450,6 +443,7 @@
     line = pl.BlockSpec((1, width), lambda i: (0, 0))
     args = (incoming, grads, normed, inverse, gain)
     specs = [whole(array) for array in args]
+    specs[0] = pl.BlockSpec((rows, incoming.shape[1]), lambda i: (place, 0))
     if low is not None:
         args = args + (low,)
         specs.append(pl.BlockSpec((block, low.shape[1]), lambda i: (jnp.minimum(i, first - 1), 0)))
@@ -478,7 +472,7 @@
     block = min(count, 256)
 
     def body(row_ref, up_ref, value_ref, gate_ref, drop_ref, value_bias_ref, gate_bias_ref, *outs):
-        middle_ref, value_out, gate_out, back_ref, term_ref = outs
+        middle_ref, value_out, gate_out, back_ref = outs
         middle_grad = widen(narrow(dot_t(up_ref[...], drop_ref[...])))
         value = dot_t(row_ref[...], value_ref[...]) + value_bias_ref[...]
         gate = dot_t(row_ref[...], gate_ref[...]) + gate_bias_ref[...]
@@ -490,7 +484,6 @@
         value_out[...] = value_grad
         gate_out[...] = gate_grad
         back_ref[...] = narrow(dot(value_grad, value_ref[...]) + dot(gate_grad, gate_ref[...]))
-        term_ref[...] = narrow(dot(middle, drop_ref[...]))
 
     wide = pl.BlockSpec((block, width), lambda i: (i, 0))
     thin = pl.BlockSpec((block, units), lambda i: (i, 0))
@@ -498,10 +491,10 @@
     return pl.pallas_call(
         body,
         grid=(count // block,),
-        out_shape=[like((count, units), jnp.bfloat16)] * 3 + [like((count, width), jnp.bfloat16)] * 2,
+        out_shape=[like((count, units), jnp.bfloat16)] * 3 + [like((count, width), jnp.bfloat16)],
         in_specs=[wide, wide] + [whole(array) for array in args[2:]],
-        out_specs=[thin] * 3 + [wide] * 2,
-        compiler_params=room(24),
+        out_specs=[thin] * 3 + [wide],
+        compiler_params=room(32),
         cost_estimate=hint(),
     )(*args)
 
@@ -539,8 +532,9 @@
     )(*lefts, *rights)
 
 
-def spin_backward(query, pairs, got, cosine, sine):
-    rows, width = query.shape
+def spin_backward(grads, got, cosine, sine):
+    rows, width = got.shape[0] // 2, got.shape[1]
+    last = grads.shape[0] // rows - 1
 
     def body(cos_ref, sin_ref, query_ref, own_ref, got_ref, out_ref):
         step = pl.program_id(0)
@@ -565,13 +559,13 @@
         body,
         grid=(3,),
         out_shape=jax.ShapeDtypeStruct((rows, 3 * width), jnp.bfloat16),
-        in_specs=[table, table, pl.BlockSpec((rows, width), lambda i: (0, 0)), part, part],
+        in_specs=[table, table, pl.BlockSpec((rows, width), lambda i: (last, 0)), part, part],
         out_specs=pl.BlockSpec((rows, width), lambda i: (0, i)),
         compiler_params=room(8),
         cost_estimate=pl.CostEstimate(
-            flops=24 * query.size, bytes_accessed=16 * query.size, transcendentals=0
+            flops=1 << 20, bytes_accessed=1 << 20, transcendentals=0
         ),
-    )(cosine, sine, query, pairs, got)
+    )(cosine, sine, grads, grads, got)
 
 
 def two_heads(value):
@@ -645,12 +639,12 @@
     def body(*refs):
         query_ref, grad_ref, pair_refs = refs[0], refs[1], refs[2 : 2 + count]
         rest = refs[2 + count :]
-        out_query, out_pair = refs[-2:]
+        out_ref = refs[-1]
 
         def put(part, r, lanes, value):
             for b in range(count):
                 start = b * block + (part * row_count + r) * keys
-                out_pair[start : start + keys, lanes] = narrow(value[b * keys : (b + 1) * keys])
+                out_ref[start : start + keys, lanes] = narrow(value[b * keys : (b + 1) * keys])
 
         for r in range(row_count):
             span = slice(r * frames, (r + 1) * frames)
@@ -664,7 +658,8 @@
                 result = one_row(tdot(score_grad, key))
                 if tables is not None:
                     result = spin(result, rest[0][span, :], rest[1][span, :])
-                out_query[span, lanes] = narrow(result * scale)
+                start = count * block + r * frames
+                out_ref[start : start + frames, lanes] = narrow(result * scale)
                 put(0, r, lanes, dot(score_grad, asked))
                 put(1, r, lanes, dot(narrow(probs), grad))
 
@@ -680,9 +675,9 @@
     return pl.pallas_call(
         body,
         grid=(width // LANES,),
-        out_shape=[like((tokens, width), jnp.bfloat16), like((count * block, width), jnp.bfloat16)],
+        out_shape=like((count * block + tokens, width), jnp.bfloat16),
         in_specs=specs,
-        out_specs=[token_spec, pl.BlockSpec((count * block, LANES), lambda i: (0, i))],
+        out_specs=pl.BlockSpec((count * block + tokens, LANES), lambda i: (0, i)),
         compiler_params=room(12),
         cost_estimate=hint(),
     )(*args)
@@ -691,29 +686,31 @@
 def multiply(left, right):
     rows, depth = left.shape
     width = right.shape[1]
+    block = LANES if width % LANES == 0 else 384 if width % 384 == 0 else width
 
     def body(left_ref, right_ref, out_ref):
         out_ref[...] = narrow(dot(left_ref[...], right_ref[...]))
 
     return pl.pallas_call(
         body,
-        grid=(width // LANES,),
+        grid=(width // block,),
         out_shape=like((rows, width), jnp.bfloat16),
-        in_specs=[whole(left), pl.BlockSpec((depth, LANES), lambda i: (0, i))],
-        out_specs=pl.BlockSpec((rows, LANES), lambda i: (0, i)),
+        in_specs=[whole(left), pl.BlockSpec((depth, block), lambda i: (0, i))],
+        out_specs=pl.BlockSpec((rows, block), lambda i: (0, i)),
         compiler_params=room(12),
         cost_estimate=hint(),
     )(left, right)
 
 
-def weight_sums(lefts, rights):
+def weight_sums(lefts, rights, beside=None):
     rows = lefts[0].shape[1] // 2
     widths = [right.shape[1] for right in rights]
     count = len(lefts)
     if rows % 128:
         sums = [narrow(tdot(left, right)) for left, right in zip(lefts, rights)]
-        sums = jnp.concatenate(sums, 1)
+        sums = jnp.concatenate(sums + ([] if beside is None else [beside]), 1)
         return sums[:rows], sums[rows:]
+    total = sum(widths) + (0 if beside is None else beside.shape[1])
 
     def body(*refs):
         for half in range(2):
@@ -723,20 +720,27 @@
                 start = 0
                 for left, right, width in zip(refs[:count], refs[count : 2 * count], widths):
                     lanes = slice(start, start + width)
-                    refs[2 * count + half][:, lanes] = narrow(tdot(left[...], right[...]))
+                    refs[half - 2][:, lanes] = narrow(tdot(left[...], right[...]))
                     start = start + width
+                if beside is not None:
+                    refs[half - 2][:, start:] = refs[2 * count][...]
 
     specs = [pl.BlockSpec((left.shape[0], rows), lambda i: (0, i)) for left in lefts]
-    out = pl.BlockSpec((rows, sum(widths)), lambda i: (0, 0))
+    specs = specs + [whole(right) for right in rights]
+    args = (*lefts, *rights)
+    if beside is not None:
+        args = args + (beside,)
+        specs.append(pl.BlockSpec((rows, beside.shape[1]), lambda i: (i, 0)))
+    out = pl.BlockSpec((rows, total), lambda i: (0, 0))
     return pl.pallas_call(
         body,
         grid=(2,),
-        out_shape=[like((rows, sum(widths)), jnp.bfloat16)] * 2,
-        in_specs=specs + [whole(right) for right in rights],
+        out_shape=[like((rows, total), jnp.bfloat16)] * 2,
+        in_specs=specs,
         out_specs=[out, out],
         compiler_params=room(14),
         cost_estimate=hint(),
-    )(*lefts, *rights)
+    )(*args)
 
 
 def order_matrix(size, rows, order, me):
@@ -915,12 +919,17 @@
     def cut_tokens(value):
         return [value[cuts[p] : cuts[p + 1]] for p in range(3)]
 
-    def token_pairs(value):
+    def token_pairs(kept, got):
         pairs = []
         for p in range(3):
             first, last = near_count * cuts[p], near_count * cuts[p + 1]
             middle = (first + last) // 2
-            pairs.append((narrow(value[first:middle]), narrow(value[middle:last])))
+            pairs.append(
+                [
+                    narrow(widen(kept[rows]) + widen(got[rows]))
+                    for rows in (slice(first, middle), slice(middle, last))
+                ]
+            )
         return pairs
 
     inputs = frames.reshape(token_count, width)
@@ -1030,11 +1039,17 @@
     feed_rows = traffic.done["all"]
     for rows, up in zip(feed_rows[1:], ups[1:]):
         results.append(feed_block(rows, up, *lows))
-    middles, value_grads, gate_grads, back_sums, term_sums = [list(item) for item in zip(*results)]
+    middles, value_grads, gate_grads, back_sums = [list(item) for item in zip(*results)]
 
     def back_flow():
-        value = yield from halve_list(back_sums, seq_masks)
-        return (yield from halve_pairs(token_pairs(value), near_orders))
+        blocks = back_sums
+        for mask in reversed(seq_masks):
+            half = len(blocks) // 2
+            sent = yield tuple(blocks[half:])
+            got = yield hops(sent, (mask,) * half)
+            if half > 1:
+                blocks = [narrow(widen(a) + widen(b)) for a, b in zip(blocks[:half], got)]
+        return (yield from halve_pairs(token_pairs(blocks[0], got[0]), near_orders))
 
     blocks = len(feed_rows)
     tied = traffic.turn(middles + value_grads + gate_grads, lambda done: {"back": back_flow()})
@@ -1072,11 +1087,23 @@
 
     value_grad, gate_grad, drop_grad, mixed_all = traffic.turn(
         (value_grad, gate_grad, drop_grad, mixed_all),
-        lambda done: {"term": halve_list(term_sums, seq_masks), "unit0": unit_flow(0)},
+        lambda done: {"unit0": unit_flow(0)},
     )
     turned_self = [turn_rows(mixed_all, matrix) for matrix in matrices]
 
-    (*turned_self,) = traffic.turn(turned_self)
+    term_sums = [multiply(middle, drop_low) for middle in middles]
+
+    def term_flow():
+        blocks = term_sums
+        for mask in reversed(seq_masks):
+            half = len(blocks) // 2
+            sent = yield tuple(blocks[half:])
+            got = yield hops(sent, (mask,) * half)
+            if half > 1:
+                blocks = [narrow(widen(a) + widen(b)) for a, b in zip(blocks[:half], got)]
+        return blocks[0], got[0]
+
+    (*turned_self,) = traffic.turn(turned_self, lambda done: {"term": term_flow()})
     for _ in seq_masks[1:]:
         traffic.turn((), step=["term"])
     while "back" in traffic.flows:
@@ -1088,7 +1115,7 @@
     (feed_back,) = traffic.turn(
         (feed_back,),
         lambda done: {
-            "term_near": halve_pairs(token_pairs(done["term"]), near_orders),
+            "term_near": halve_pairs(token_pairs(*done["term"]), near_orders),
         },
     )
     cross_out_grad, grad_gain_three, grad_shift_three, cross_branch, cross_mixed_grad = back(
@@ -1114,38 +1141,42 @@
         (cross_mixed_grad,),
         lambda done: {"dc": double_list(cross_branch, seq_masks), "unit1": unit_flow(1)},
     )
-    asking_grad, memory_grad = attend_back(
+    asked_grad = attend_back(
         asking, [memory], None, cross_mixed_grad, None, row_count, scale
     )
-    asking_grad, memory_grad = traffic.turn(
-        (asking_grad, memory_grad),
-        lambda done: {
-            "dq": double_list(asking_grad, seq_masks),
-            "dm": double_list(memory_grad, seq_masks),
-        },
+    (asked_grad,) = traffic.turn(
+        (asked_grad,),
+        lambda done: {"dq": double_list(asked_grad, seq_masks), "unit2": unit_flow(2)},
     )
     for _ in seq_masks[1:]:
         traffic.turn((), step=["dc"])
     self_out_grad, grad_gain_two, grad_shift_two, self_branch, self_mixed_grad = back(
-        asking_grad, ask_low, cross_out_grad, normed_two, inverse_two, gain_two, self_low
+        asked_grad,
+        ask_low,
+        cross_out_grad,
+        normed_two,
+        inverse_two,
+        gain_two,
+        self_low,
+        memory.shape[0] // token_count,
     )
     (self_mixed_grad,) = traffic.turn(
         (self_mixed_grad,),
-        lambda done: {"da": double_list(self_branch, seq_masks), "unit2": unit_flow(2)},
+        lambda done: {"da": double_list(self_branch, seq_masks)},
     )
     for _ in seq_masks[1:]:
-        traffic.turn((), step=["dq", "dm", "da"])
+        traffic.turn((), step=["dq", "da"])
     cross_pair = weight_pair(turned_cross, jnp.concatenate(traffic.done["dc"], 0))
     layer_output = narrow(
         after_cross + jnp.concatenate(traffic.done["term_near"], 0) + drop_bias
     )
-    ask_pair = weight_pair(turned_ask, jnp.concatenate(traffic.done["dq"], 0))
-    memory_all = traffic.done["dm"]
-    half = memory_grad.shape[0] // 2
+    memory_all = traffic.done["dq"]
+    half = memory.shape[0] // 2
+    ask_pair = weight_pair(turned_ask, jnp.concatenate([part[2 * half :] for part in memory_all], 0))
     memory_pair = weight_pair(
         turned_memory,
         jnp.concatenate([part[:half] for part in memory_all], 0),
-        jnp.concatenate([part[half:] for part in memory_all], 0),
+        jnp.concatenate([part[half : 2 * half] for part in memory_all], 0),
     )
     self_mixed_grad, layer_output = traffic.turn(
         (self_mixed_grad, layer_output),
@@ -1153,23 +1184,28 @@
             "first": halve_pairs([cross_pair, ask_pair, memory_pair], tail_orders),
         },
     )
-    query_back, pair_grad = attend_back(
+    pair_grad = attend_back(
         query, pairs, seen, self_mixed_grad, back_tables, row_count, scale
     )
 
     def shed_frames(value):
+        query_grad = value[-token_count:]
+        count = value.shape[0] - token_count
         for mask in reversed(seq_masks):
-            half = value.shape[0] // 2
-            (sent,) = yield (value[half:],)
+            half = count // 2
+            (sent,) = yield (value[half:count],)
             (got,) = yield hops((sent,), (mask,))
             if mask > seq_masks[0]:
                 value = narrow(widen(value[:half]) + widen(got))
+                count = half
+        if len(seq_masks) > 1:
+            value = jnp.concatenate([value, query_grad], 0)
         return value, got
 
-    (query_back,) = traffic.turn((query_back,), lambda done: {"pair": shed_frames(pair_grad)}, step=[])
+    (pair_grad,) = traffic.turn((pair_grad,), lambda done: {"pair": shed_frames(pair_grad)}, step=[])
     for _ in seq_masks:
-        (query_back,) = traffic.turn((query_back,), step=["pair"])
-    triple_back = spin_backward(query_back, *traffic.done["pair"], *back_tables)
+        traffic.turn((), step=["pair"])
+    triple_back = spin_backward(*traffic.done["pair"], *back_tables)
     (triple_back,) = traffic.turn(
         (triple_back,), lambda done: {"dt": double_list(triple_back, seq_masks)}
     )
@@ -1177,67 +1213,79 @@
         triple_back, triple_low, self_out_grad, normed_one, inverse_one, gain_one
     )
     branch_all = jnp.concatenate(traffic.done["da"], 0)
-    third = width // 3
-    frame_grad, *sums = traffic.turn(
-        (
-            frame_grad,
-            grad_gain_one,
-            grad_shift_one,
-            grad_gain_two,
-            grad_shift_two,
-            grad_gain_three,
-            grad_shift_three,
-        )
-    )
-    sums = jnp.concatenate(sums + [grad_drop_bias], 0).reshape(7, device_count, share)
-    sums = jnp.transpose(sums, (1, 0, 2)).reshape(device_count, 7 * share)
-    sums = jnp.pad(sums, ((0, 0), (0, 1024 - 7 * share)))
-    tail_masks = masks_of(tail_orders[0] + seq_masks)
-    sums = jnp.take(sums, me ^ jnp.asarray(np.array(tail_masks, np.int32)), axis=0)
-    sums = sums.reshape(device_count, 8, 128)
-    for _ in seq_masks[1:]:
-        traffic.turn((), step=["dt"])
+    shares = [0, width // 6, width // 3, width]
+    sums = [
+        grad_gain_one,
+        grad_shift_one,
+        grad_gain_two,
+        grad_shift_two,
+        grad_gain_three,
+        grad_shift_three,
+        grad_drop_bias,
+    ]
+    sums = jnp.pad(jnp.concatenate(sums, 0), ((0, 1), (0, 0)))
+    frame_grad, sums = traffic.turn((frame_grad, sums), lambda done: {"sums": double_list(sums, seq_masks)})
+    for _ in seq_masks:
+        traffic.turn((), step=["dt", "sums"])
     triple_all = jnp.concatenate(traffic.done["dt"], 0)
+    sums = sum(traffic.done["sums"])
+    sums_turned = tdot(matrices[1], narrow(jnp.transpose(sums)))
+    sums_turned = narrow(jnp.pad(sums_turned, ((0, 0), (0, 120))))
     triple_pairs = [
-        tuple(
+        list(
             weight_sums(
                 [turned_triple[p], turned_self[p]],
                 [
                     triple_all[:, p * width : (p + 1) * width],
-                    branch_all[:, p * third : (p + 1) * third],
+                    branch_all[:, shares[p] : shares[p + 1]],
                 ],
+                sums_turned if p == 1 else None,
             )
         )
         for p in range(3)
     ]
-    tied = traffic.turn(
-        sum(triple_pairs, ()), lambda done: {"sums": halve_list_rows(sums, seq_masks)}
-    )
-    triple_pairs = [tied[2 * p : 2 * p + 2] for p in range(3)]
-    while "first" in traffic.flows or "sums" in traffic.flows:
+    while traffic.count["first"] < len(batch_masks) - 1:
         traffic.turn(())
-    sums = traffic.done["sums"]
-    half = sums.shape[0] // 2
-    traffic.turn(
-        (),
-        lambda done: {
-            "tail": halve_pairs(
-                triple_pairs + [(sums[:half], sums[half:])], tail_orders + [tail_orders[0]]
-            ),
-            "unit4": unit_flow(4),
-        },
-    )
-    traffic.turn((), lambda done: {"unit3": unit_flow(3)})
+
+    def tail_first(*which):
+        return once([triple_pairs[p][1] for p in which], [tail_orders[p][-1] for p in which])
+
+    traffic.turn((), lambda done: {"early": tail_first(0, 2)})
+    (triple_pairs[1][1],) = traffic.turn(
+        (triple_pairs[1][1],),
+        lambda done: {"unit4": unit_flow(4)},
+        step=["first"],
+    )
+    traffic.turn((), lambda done: {"late": tail_first(1)}, step=[])
+
+    def tail_rest(done):
+        got = (done["early"][0], done["late"][0], done["early"][1])
+        pairs = []
+        for (kept, _), part in zip(triple_pairs, got):
+            half = kept.shape[0] // 2
+            pairs.append(
+                [
+                    narrow(widen(kept[rows]) + widen(part[rows]))
+                    for rows in (slice(half), slice(half, None))
+                ]
+            )
+        orders = [order[:-1] for order in tail_orders]
+        return {"tail": halve_pairs(pairs, orders), "unit3": unit_flow(3)}
+
+    traffic.turn((), tail_rest)
     while traffic.flows:
         traffic.turn(())
     parts = traffic.done["tail"]
     grad_cross, grad_ask, grad_memory = traffic.done["first"]
-    grad_self = jnp.concatenate([part[:, width:] for part in parts[:3]], 1)
+    grad_self = jnp.concatenate(
+        [part[:, width : width + shares[p + 1] - shares[p]] for p, part in enumerate(parts)], 1
+    )
     drop_sums = jnp.concatenate([traffic.done[name] for name in UNITS[:2]], 0)
     value_sums = jnp.concatenate([traffic.done[name] for name in UNITS[2:4]], 0)
     gate_sums = traffic.done[UNITS[4]]
-    grad_triple = jnp.concatenate([part[:, :width] for part in parts[:3]], 1)
-    sums = parts[3].reshape(1024)[: 7 * share].reshape(7, share)
+    grad_triple = jnp.concatenate([part[:, :width] for part in parts], 1)
+    sums = width + shares[2] - shares[1]
+    sums = jnp.transpose(parts[1][:, sums : sums + 7])
     grad_memory = grad_memory.reshape(2, share // 2, width)[:, : cross_memory.shape[0]]
     grad_memory = jnp.concatenate([grad_memory[0], grad_memory[1]], 1)
     grad_lift = jnp.stack([value_sums, gate_sums[:units]], 0)

time: 667 us -> 651 us (0.976)
  local copies, waits for them, and re-layouts: 49.6 us -> 38.5 us
    convert_element_type x29 -> x35, other arithmetic: 8.56 us -> 15.1 us  [narrow(): return value.astype(jnp.bfloat16)]
    ppermute x107 -> x102, waiting for transfers between devices: 327 us -> 321 us  [hop(): return lax.ppermute(value, AX, [(i, i ^ mask) for i in range(count)])]
    pallas_call x6 -> x8, Pallas kernels: 22 us -> 26.8 us  [the longest x2 14.3 us: attend_back(): pl.pallas_call(body, grid=(width // LANES,), out_shape=like((count * bloc...]
    unnamed x290 -> x254, local copies, waits for them, and re-layouts: 33.5 us -> 30.2 us
    ppermute x107 -> x102, starting transfers between devices: 98.6 us -> 102 us  [hop(): return lax.ppermute(value, AX, [(i, i ^ mask) for i in range(count)])]
  transfers between devices with their start and end apart: 107 -> 102, of which waited for: 48 -> 56; matrix products, arithmetic and copies ran while one was open for 9% -> 8% of each run, Pallas kernels for 14% -> 15%
where the time goes in v3:
time: 651 us; the launch traced here: 643 us
  waiting for transfers between devices  321 us (49%)
  Pallas kernels  109 us (17%)
  starting transfers between devices  102 us (16%)
  other arithmetic  49.6 us (8%)
  local copies, waits for them, and re-layouts  38.5 us (6%)
  matrix products  19.7 us (3%)
    ppermute x102, waiting for transfers between devices, hop(): return lax.ppermute(value, AX, [(i, i ^ mask) for i in range(count)])  321 us
    ppermute x102, starting transfers between devices, hop(): return lax.ppermute(value, AX, [(i, i ^ mask) for i in range(count)])  102 us
    unnamed x254, local copies, waits for them, and re-layouts  30.2 us
    pallas_call x2, Pallas kernels, feed_block(): pl.pallas_call(body, grid=(count // block,), out_shape=[like((count, unit...  19.3 us
    convert_element_type x35, other arithmetic, narrow(): return value.astype(jnp.bfloat16)  15.1 us
    dot_general x11, matrix products, dot(): lax.dot_general(left, right, (((1,), (0,)), ((), ())), preferred_element_...  15 us
    pallas_call x2, Pallas kernels, attend_back(): pl.pallas_call(body, grid=(width // LANES,), out_shape=like((count * bloc...  14.3 us
    pallas_call x2, Pallas kernels, attend(): pl.pallas_call(body, grid=(width // LANES,), out_shape=like((tokens, widt...  14.1 us
  transfers between devices with their start and end apart: 102, of which 56 were waited for; matrix products, arithmetic and copies ran while one was open for 8% of the time, Pallas kernels for 15%

profile of v3, /device:TPU:0, one launch (start us, length us, event | category | flops | bytes accessed | tf_op | source)
XLA Modules:
  0.0 643.0 jit_solution(15204596374934749223)
XLA Ops:
  23.6 6.6 %collective-permute-done = bf16[48,4736]{1,0:T(8,128)(2,1)S(1)} collective-permute-done((bf16[48,4736]{1,0:T(8,128)(2,1)}, bf16[48,4736]{1,0:T(8,128)(2,1)S(1)}, u32[]{:S(2)}, u32[]{:S(2)}) %collective-permute-start) | collective-permute-done | bytes 454688 | tf_op jit(solution)/shard_map/ppermute | solution.py:77
  31.3 20.3 %collective-permute-done.1 = bf16[96,4736]{1,0:T(8,128)(2,1)S(1)} collective-permute-done((bf16[96,4736]{1,0:T(8,128)(2,1)S(1)}, bf16[96,4736]{1,0:T(8,128)(2,1)S(1)}, u32[]{:S(2)}, u32[]{:S(2)}) %collective-permute-start.1) | collective-permute-done | bytes 909344 | tf_op jit(solution)/shard_map/ppermute | solution.py:77
  59.3 22.3 %collective-permute-done.2 = bf16[48,6144]{1,0:T(8,128)(2,1)S(1)} collective-permute-done((bf16[48,6144]{1,0:T(8,128)(2,1)S(1)}, bf16[48,6144]{1,0:T(8,128)(2,1)S(1)}, u32[]{:S(2)}, u32[]{:S(2)}) %collective-permute-start.2) | collective-permute-done | bytes 589856 | tf_op jit(solution)/shard_map/ppermute | solution.py:77
  89.3 35.8 %collective-permute-done.7 = bf16[208,1536]{1,0:T(8,128)(2,1)S(1)} collective-permute-done((bf16[208,1536]{1,0:T(8,128)(2,1)S(1)}, bf16[208,1536]{1,0:T(8,128)(2,1)S(1)}, u32[]{:S(2)}, u32[]{:S(2)}) %collective-permute-start.7) | collective-permute-done | bytes 639008 | tf_op jit(solution)/shard_map/ppermute | solution.py:77
  130.3 26.1 %collective-permute-done.10 = bf16[192,3072]{1,0:T(8,128)(2,1)S(1)} collective-permute-done((bf16[192,3072]{1,0:T(8,128)(2,1)S(1)}, bf16[192,3072]{1,0:T(8,128)(2,1)S(1)}, u32[]{:S(2)}, u32[]{:S(2)}) %collective-permute-start.10) | collective-permute-done | bytes 1179680 | tf_op jit(solution)/shard_map/ppermute | solution.py:77
  164.8 6.9 %shard_map.350 = (bf16[1536,128]{1,0:T(8,128)(2,1)S(1)}, bf16[1536,4608]{1,0:T(8,128)(2,1)S(1)}) custom-call(s32[1]{0:T(128)} %bitcast.13.me_ref, bf16[384,2432]{1,0:T(8,128)(2,1)S(1)} %pad_maximum_fusion.3.refs_0_, bf16[384,2432]{1,0:T(8,128)(2,1)S(1)} %collective-permute-done.5.refs_1_, bf16[384,2432]{1,0:T(8,128)(2,1)S(1)} %collective-permute-done.9.refs_2_, ...), custom_call_target="tpu_custom_call" | custom-call | bytes 909312 | tf_op jit(solution)/shard_map/pallas_call | solution.py:143
  179.2 7.0 %shard_map.352.mixed_ref = bf16[128,1536]{1,0:T(8,128)(2,1)S(1)} custom-call(bf16[128,1536]{1,0:T(8,128)(2,1)S(1)} %get-tuple-element.459.refs_0_, bf16[256,1536]{1,0:T(8,128)(2,1)S(1)} %get-tuple-element.457.refs_1_.refs_2_, bf16[256,1536]{1,0:T(8,128)(2,1)S(1)} %collective-permute-done.19.refs_2_.refs_3_, f32[2,128,64]{2,1,0:T(8,128)S(1)} %compare_convert_fusion.refs_3_.refs_6_), custom_call_target="tpu_custom_call" | custom-call | flops 1048576 | bytes 1048576 | tf_op jit(solution)/shard_map/pallas_call | solution.py:621
  186.3 30.1 %collective-permute-done.18 = bf16[384,1536]{1,0:T(8,128)(2,1)S(1)} collective-permute-done((bf16[384,1536]{1,0:T(8,128)(2,1)}, bf16[384,1536]{1,0:T(8,128)(2,1)S(1)}, u32[]{:S(2)}, u32[]{:S(2)}) %collective-permute-start.18) | collective-permute-done | bytes 1179680 | tf_op jit(solution)/shard_map/ppermute | solution.py:77
  231.2 6.8 %shard_map.353 = (bf16[1536,1536]{1,0:T(8,128)(2,1)S(1)}, bf16[1536,1536]{1,0:T(8,128)(2,1)S(1)}, bf16[1536,1536]{1,0:T(8,128)(2,1)S(1)}, bf16[1536,1536]{1,0:T(8,128)(2,1)}) custom-call(s32[1]{0:T(128)} %bitcast.13.me_ref, bf16[384,3072]{1,0:T(8,128)(2,1)S(1)} %pad_maximum_fusion.1.refs_0_, bf16[384,3072]{1,0:T(8,128)(2,1)S(1)} %copy-done.19, ...), custom_call_target="tpu_custom_call" | custom-call | bytes 1179648 | tf_op jit(solution)/shard_map/pallas_call | solution.py:143
  252.5 7.0 %shard_map.356.mixed_ref = bf16[128,1536]{1,0:T(8,128)(2,1)S(1)} custom-call(bf16[128,1536]{1,0:T(8,128)(2,1)S(1)} %get-tuple-element.521.refs_0_, bf16[512,1536]{1,0:T(8,128)(2,1)S(1)} %shard_map.355.refs_1_.refs_2_), custom_call_target="tpu_custom_call" | custom-call | flops 1048576 | bytes 1048576 | tf_op jit(solution)/shard_map/pallas_call | solution.py:621
  291.6 8.1 %collective-permute-done.43 = bf16[128,1536]{1,0:T(8,128)(2,1)S(1)} collective-permute-done((bf16[128,1536]{1,0:T(8,128)(2,1)S(1)}, bf16[128,1536]{1,0:T(8,128)(2,1)S(1)}, u32[]{:S(2)}, u32[]{:S(2)}) %collective-permute-start.43) | collective-permute-done | bytes 393248 | tf_op jit(solution)/shard_map/ppermute | solution.py:77
  304.0 9.6 %shard_map.358 = (bf16[1024,384]{1,0:T(8,128)(2,1)S(1)}, bf16[1024,384]{1,0:T(8,128)(2,1)S(1)}, bf16[1024,384]{1,0:T(8,128)(2,1)S(1)}, bf16[1024,1536]{1,0:T(8,128)(2,1)S(1)}) custom-call(bf16[1024,1536]{1,0:T(8,128)(2,1)S(1)} %constant_dynamic-update-slice_fusion.11.row_ref.refs_2_, ...), custom_call_target="tpu_custom_call" | custom-call | flops 1048576 | bytes 1048576 | tf_op jit(solution)/shard_map/pallas_call | solution.py:491
  318.4 9.7 %shard_map.359 = (bf16[1024,384]{1,0:T(8,128)(2,1)S(1)}, bf16[1024,384]{1,0:T(8,128)(2,1)S(1)}, bf16[1024,384]{1,0:T(8,128)(2,1)S(1)}, bf16[1024,1536]{1,0:T(8,128)(2,1)S(1)}) custom-call(bf16[1024,1536]{1,0:T(8,128)(2,1)S(1)} %collective-permute-done.46.row_ref.refs_3_, bf16[1024,1536]{1,0:T(8,128)(2,1)S(1)} %copy-done.6, bf16[384,1536]{1,0:T(8,128)(2,1)S(1)} %copy-done.8, ...), custom_call_target="tpu_custom_call" | custom-call | flops 1048576 | bytes 1048576 | tf_op jit(solution)/shard_map/pallas_call | solution.py:491
  364.8 6.6 %collective-permute-done.52 = bf16[96,1536]{1,0:T(8,128)(2,1)S(1)} collective-permute-done((bf16[96,1536]{1,0:T(8,128)(2,1)S(1)}, bf16[96,1536]{1,0:T(8,128)(2,1)S(1)}, u32[]{:S(2)}, u32[]{:S(2)}) %collective-permute-start.52) | collective-permute-done | bytes 294944 | tf_op jit(solution)/shard_map/ppermute | solution.py:77
  407.1 7.0 %shard_map.366.in_ref = bf16[640,1536]{1,0:T(8,128)(2,1)S(1)} custom-call(bf16[128,1536]{1,0:T(8,128)(2,1)S(1)} %copy-done.33, bf16[128,1536]{1,0:T(8,128)(2,1)S(1)} %get-tuple-element.665.refs_1_, bf16[512,1536]{1,0:T(8,128)(2,1)S(1)} %shard_map.355.refs_1_.refs_2_), custom_call_target="tpu_custom_call" | custom-call | flops 1048576 | bytes 1048576 | tf_op jit(solution)/shard_map/pallas_call | solution.py:675
  445.0 7.3 %shard_map.368.query_ref.own_ref = bf16[640,1536]{1,0:T(8,128)(2,1)S(1)} custom-call(bf16[128,1536]{1,0:T(8,128)(2,1)S(1)} %copy-done.31, bf16[128,1536]{1,0:T(8,128)(2,1)S(1)} %get-tuple-element.701.refs_1_, bf16[256,1536]{1,0:T(8,128)(2,1)S(1)} %copy-done.13, bf16[256,1536]{1,0:T(8,128)(2,1)S(1)} %copy-done.15, f32[128,128]{1,0:T(8,128)S(1)} %copy-done.40, ...), custom_call_target="tpu_custom_call" | custom-call | flops 1048576 | bytes 1048576 | tf_op jit(solution)/shard_map/pallas_call | solution.py:675
  455.5 13.4 %collective-permute-done.73 = bf16[384,1536]{1,0:T(8,128)(2,1)S(1)} collective-permute-done((bf16[384,1536]{1,0:T(8,128)(2,1)S(1)}, bf16[384,1536]{1,0:T(8,128)(2,1)S(1)}, u32[]{:S(2)}, u32[]{:S(2)}) %collective-permute-start.73) | collective-permute-done | bytes 1179680 | tf_op jit(solution)/shard_map/ppermute | solution.py:77
  477.8 6.3 shard_map.370
  538.5 27.3 %collective-permute-done.90 = bf16[208,1536]{1,0:T(8,128)(2,1)S(1)} collective-permute-done((bf16[208,1536]{1,0:T(8,128)(2,1)S(1)}, bf16[208,1536]{1,0:T(8,128)(2,1)S(1)}, u32[]{:S(2)}, u32[]{:S(2)}) %collective-permute-start.90) | collective-permute-done | bytes 639008 | tf_op jit(solution)/shard_map/ppermute | solution.py:77
  565.8 6.6 %collective-permute-done.85 = bf16[384,1792]{1,0:T(8,128)(2,1)S(1)} collective-permute-done((bf16[384,1792]{1,0:T(8,128)(2,1)}, bf16[384,1792]{1,0:T(8,128)(2,1)S(1)}, u32[]{:S(2)}, u32[]{:S(2)}) %collective-permute-start.85) | collective-permute-done | bytes 1376288 | tf_op jit(solution)/shard_map/ppermute | solution.py:77
  580.5 9.1 %collective-permute-done.95 = bf16[96,1536]{1,0:T(8,128)(2,1)S(1)} collective-permute-done((bf16[96,1536]{1,0:T(8,128)(2,1)S(1)}, bf16[96,1536]{1,0:T(8,128)(2,1)S(1)}, u32[]{:S(2)}, u32[]{:S(2)}) %collective-permute-start.95) | collective-permute-done | bytes 294944 | tf_op jit(solution)/shard_map/ppermute | solution.py:77
  591.7 7.5 %collective-permute-done.93 = bf16[192,1920]{1,0:T(8,128)(2,1)S(1)} collective-permute-done((bf16[192,1920]{1,0:T(8,128)(2,1)S(1)}, bf16[192,1920]{1,0:T(8,128)(2,1)S(1)}, u32[]{:S(2)}, u32[]{:S(2)}) %collective-permute-start.93) | collective-permute-done | bytes 737312 | tf_op jit(solution)/shard_map/ppermute | solution.py:77
  604.4 11.8 %collective-permute-done.96 = bf16[96,1792]{1,0:T(8,128)(2,1)S(1)} collective-permute-done((bf16[96,1792]{1,0:T(8,128)(2,1)S(1)}, bf16[96,1792]{1,0:T(8,128)(2,1)S(1)}, u32[]{:S(2)}, u32[]{:S(2)}) %collective-permute-start.96) | collective-permute-done | bytes 344096 | tf_op jit(solution)/shard_map/ppermute | solution.py:77
  626.1 7.9 %collective-permute-done.100 = bf16[48,1920]{1,0:T(8,128)(2,1)S(1)} collective-permute-done((bf16[48,1920]{1,0:T(8,128)(2,1)S(1)}, bf16[48,1920]{1,0:T(8,128)(2,1)S(1)}, u32[]{:S(2)}, u32[]{:S(2)}) %collective-permute-start.100) | collective-permute-done | bytes 184352 | tf_op jit(solution)/shard_map/ppermute | solution.py:77
  (675 shorter events, 332.5 us)
Async XLA Ops:
  5.8 24.4 %collective-permute-start = (bf16[48,4736]{1,0:T(8,128)(2,1)}, bf16[48,4736]{1,0:T(8,128)(2,1)S(1)}, u32[]{:S(2)}, u32[]{:S(2)}) collective-permute-start(bf16[48,4736]{1,0:T(8,128)(2,1)} %pad_maximum_fusion.32), channel_id=1, source_target_pairs={{0,16},{1,17},{2,18},{3,19},{4,20},{5,21},{6,22},{7,23},{8,24},{9,... | collective-permute-start | bytes 1363976 | tf_op jit(solution)/shard_map/ppermute | solution.py:77
  52.8 28.8 %collective-permute-start.2 = (bf16[48,6144]{1,0:T(8,128)(2,1)S(1)}, bf16[48,6144]{1,0:T(8,128)(2,1)S(1)}, u32[]{:S(2)}, u32[]{:S(2)}) collective-permute-start(bf16[48,6144]{1,0:T(8,128)(2,1)S(1)} %maximum_maximum_fusion), channel_id=1, source_target_pairs={{0,16},{1,17},{2,18},{3,19},{4,20},{5,21},{6,22},{7,23},{8,24},{9,... | collective-permute-start | bytes 1769480 | tf_op jit(solution)/shard_map/ppermute | solution.py:77
  56.2 25.5 %collective-permute-start.4 = (bf16[192,2304]{1,0:T(8,128)(2,1)S(1)}, bf16[192,2304]{1,0:T(8,128)(2,1)S(1)}, u32[]{:S(2)}, u32[]{:S(2)}) collective-permute-start(bf16[192,2304]{1,0:T(8,128)(2,1)S(1)} %slice.704), channel_id=1, source_target_pairs={{0,4},{1,5},{2,6},{3,7},{4,0},{5,1},{6,2},{7,3},{8,12},{9,13},{10,... | collective-permute-start | bytes 2654216 | tf_op jit(solution)/shard_map/ppermute | solution.py:77
  82.0 44.9 %collective-permute-start.5 = (bf16[384,2432]{1,0:T(8,128)(2,1)S(1)}, bf16[384,2432]{1,0:T(8,128)(2,1)S(1)}, u32[]{:S(2)}, u32[]{:S(2)}) collective-permute-start(bf16[384,2432]{1,0:T(8,128)(2,1)S(1)} %pad_maximum_fusion.3.refs_0_), channel_id=1, source_target_pairs={{0,4},{1,5},{2,6},{3,7},{4,0},{5,1},{6,2},{7,3},{8,12},{9,13},{10,... | collective-permute-start | bytes 5603336 | tf_op jit(solution)/shard_map/ppermute | solution.py:77
  83.6 43.3 %collective-permute-start.9 = (bf16[384,2432]{1,0:T(8,128)(2,1)S(1)}, bf16[384,2432]{1,0:T(8,128)(2,1)S(1)}, u32[]{:S(2)}, u32[]{:S(2)}) collective-permute-start(bf16[384,2432]{1,0:T(8,128)(2,1)S(1)} %pad_maximum_fusion.3.refs_0_), channel_id=1, source_target_pairs={{0,1},{1,0},{2,3},{3,2},{4,5},{5,4},{6,7},{7,6},{8,9},{9,8},{10,11... | collective-permute-start | bytes 5603336 | tf_op jit(solution)/shard_map/ppermute | solution.py:77
  83.6 43.3 %collective-permute-start.6 = (bf16[384,2304]{1,0:T(8,128)(2,1)S(1)}, bf16[384,2304]{1,0:T(8,128)(2,1)S(1)}, u32[]{:S(2)}, u32[]{:S(2)}) collective-permute-start(bf16[384,2304]{1,0:T(8,128)(2,1)S(1)} %pad_maximum_fusion.5.refs_4_), channel_id=1, source_target_pairs={{0,2},{1,3},{2,0},{3,1},{4,6},{5,7},{6,4},{7,5},{8,10},{9,11},{10,... | collective-permute-start | bytes 5308424 | tf_op jit(solution)/shard_map/ppermute | solution.py:77
  85.1 41.8 %collective-permute-start.8 = (bf16[96,6144]{1,0:T(8,128)(2,1)S(1)}, bf16[96,6144]{1,0:T(8,128)(2,1)S(1)}, u32[]{:S(2)}, u32[]{:S(2)}) collective-permute-start(bf16[96,6144]{1,0:T(8,128)(2,1)S(1)} %pad_maximum_fusion.9), channel_id=1, source_target_pairs={{0,8},{1,9},{2,10},{3,11},{4,12},{5,13},{6,14},{7,15},{8,0},{9,1},... | collective-permute-start | bytes 3538952 | tf_op jit(solution)/shard_map/ppermute | solution.py:77
  85.8 39.3 %collective-permute-start.7 = (bf16[208,1536]{1,0:T(8,128)(2,1)S(1)}, bf16[208,1536]{1,0:T(8,128)(2,1)S(1)}, u32[]{:S(2)}, u32[]{:S(2)}) collective-permute-start(bf16[208,1536]{1,0:T(8,128)(2,1)S(1)} %fusion.25), channel_id=1, source_target_pairs={{0,16},{1,17},{2,18},{3,19},{4,20},{5,21},{6,22},{7,23},{8,24},{9,... | collective-permute-start | bytes 1916936 | tf_op jit(solution)/shard_map/ppermute | solution.py:77
  127.2 32.0 %collective-permute-start.13 = (bf16[384,2432]{1,0:T(8,128)(2,1)S(1)}, bf16[384,2432]{1,0:T(8,128)(2,1)S(1)}, u32[]{:S(2)}, u32[]{:S(2)}) collective-permute-start(bf16[384,2432]{1,0:T(8,128)(2,1)S(1)} %collective-permute-done.5.refs_1_), channel_id=1, source_target_pairs={{0,1},{1,0},{2,3},{3,2},{4,5},{5,4},{6,7},{7,6},{8,9},{9,8},{10,11... | collective-permute-start | bytes 5603336 | tf_op jit(solution)/shard_map/ppermute | solution.py:77
  127.2 29.5 %collective-permute-start.12 = (bf16[384,2304]{1,0:T(8,128)(2,1)S(1)}, bf16[384,2304]{1,0:T(8,128)(2,1)S(1)}, u32[]{:S(2)}, u32[]{:S(2)}) collective-permute-start(bf16[384,2304]{1,0:T(8,128)(2,1)S(1)} %pad_maximum_fusion.5.refs_4_), channel_id=1, source_target_pairs={{0,1},{1,0},{2,3},{3,2},{4,5},{5,4},{6,7},{7,6},{8,9},{9,8},{10,11... | collective-permute-start | bytes 5308424 | tf_op jit(solution)/shard_map/ppermute | solution.py:77
  128.1 29.9 %collective-permute-start.14 = (bf16[384,2304]{1,0:T(8,128)(2,1)S(1)}, bf16[384,2304]{1,0:T(8,128)(2,1)S(1)}, u32[]{:S(2)}, u32[]{:S(2)}) collective-permute-start(bf16[384,2304]{1,0:T(8,128)(2,1)S(1)} %collective-permute-done.6.refs_5_), channel_id=1, source_target_pairs={{0,1},{1,0},{2,3},{3,2},{4,5},{5,4},{6,7},{7,6},{8,9},{9,8},{10,11... | collective-permute-start | bytes 5308424 | tf_op jit(solution)/shard_map/ppermute | solution.py:77
  128.1 28.4 %collective-permute-start.10 = (bf16[192,3072]{1,0:T(8,128)(2,1)S(1)}, bf16[192,3072]{1,0:T(8,128)(2,1)S(1)}, u32[]{:S(2)}, u32[]{:S(2)}) collective-permute-start(bf16[192,3072]{1,0:T(8,128)(2,1)S(1)} %get-tuple-element.417), channel_id=1, source_target_pairs={{0,2},{1,3},{2,0},{3,1},{4,6},{5,7},{6,4},{7,5},{8,10},{9,11},{10,... | collective-permute-start | bytes 3538952 | tf_op jit(solution)/shard_map/ppermute | solution.py:77
  128.6 28.1 %collective-permute-start.11 = (bf16[192,3072]{1,0:T(8,128)(2,1)S(1)}, bf16[192,3072]{1,0:T(8,128)(2,1)S(1)}, u32[]{:S(2)}, u32[]{:S(2)}) collective-permute-start(bf16[192,3072]{1,0:T(8,128)(2,1)S(1)} %get-tuple-element.418), channel_id=1, source_target_pairs={{0,4},{1,5},{2,6},{3,7},{4,0},{5,1},{6,2},{7,3},{8,12},{9,13},{10,... | collective-permute-start | bytes 3538952 | tf_op jit(solution)/shard_map/ppermute | solution.py:77
  159.5 56.8 %collective-permute-start.15 = (bf16[384,3072]{1,0:T(8,128)(2,1)S(1)}, bf16[384,3072]{1,0:T(8,128)(2,1)S(1)}, u32[]{:S(2)}, u32[]{:S(2)}) collective-permute-start(bf16[384,3072]{1,0:T(8,128)(2,1)S(1)} %pad_maximum_fusion.1.refs_0_), channel_id=1, source_target_pairs={{0,4},{1,5},{2,6},{3,7},{4,0},{5,1},{6,2},{7,3},{8,12},{9,13},{10,... | collective-permute-start | bytes 7077896 | tf_op jit(solution)/shard_map/ppermute | solution.py:77
  160.1 56.3 %collective-permute-start.16 = (bf16[384,3072]{1,0:T(8,128)(2,1)S(1)}, bf16[384,3072]{1,0:T(8,128)(2,1)S(1)}, u32[]{:S(2)}, u32[]{:S(2)}) collective-permute-start(bf16[384,3072]{1,0:T(8,128)(2,1)S(1)} %pad_maximum_fusion.refs_4_), channel_id=1, source_target_pairs={{0,2},{1,3},{2,0},{3,1},{4,6},{5,7},{6,4},{7,5},{8,10},{9,11},{10,... | collective-permute-start | bytes 7077896 | tf_op jit(solution)/shard_map/ppermute | solution.py:77
  161.6 54.8 %collective-permute-start.17 = (bf16[384,3072]{1,0:T(8,128)(2,1)S(1)}, bf16[384,3072]{1,0:T(8,128)(2,1)}, u32[]{:S(2)}, u32[]{:S(2)}) collective-permute-start(bf16[384,3072]{1,0:T(8,128)(2,1)S(1)} %pad_maximum_fusion.1.refs_0_), channel_id=1, source_target_pairs={{0,1},{1,0},{2,3},{3,2},{4,5},{5,4},{6,7},{7,6},{8,9},{9,8},{10,11... | collective-permute-start | bytes 7077896 | tf_op jit(solution)/shard_map/ppermute | solution.py:77
  161.6 54.8 %collective-permute-start.18 = (bf16[384,1536]{1,0:T(8,128)(2,1)}, bf16[384,1536]{1,0:T(8,128)(2,1)S(1)}, u32[]{:S(2)}, u32[]{:S(2)}) collective-permute-start(bf16[384,1536]{1,0:T(8,128)(2,1)} %bitcast.11), channel_id=1, source_target_pairs={{0,16},{1,17},{2,18},{3,19},{4,20},{5,21},{6,22},{7,23},{8,24},{9,... | collective-permute-start | bytes 3538952 | tf_op jit(solution)/shard_map/ppermute | solution.py:77
  441.2 27.7 %collective-permute-start.73 = (bf16[384,1536]{1,0:T(8,128)(2,1)S(1)}, bf16[384,1536]{1,0:T(8,128)(2,1)S(1)}, u32[]{:S(2)}, u32[]{:S(2)}) collective-permute-start(bf16[384,1536]{1,0:T(8,128)(2,1)S(1)} %convolution_convert_fusion.3), channel_id=1, source_target_pairs={{0,8},{1,9},{2,10},{3,11},{4,12},{5,13},{6,14},{7,15},{8,0},{9,1},... | collective-permute-start | bytes 3538952 | tf_op jit(solution)/shard_map/ppermute | solution.py:77
  441.3 27.7 %collective-permute-start.74 = (bf16[384,1536]{1,0:T(8,128)(2,1)S(1)}, bf16[384,1536]{1,0:T(8,128)(2,1)S(1)}, u32[]{:S(2)}, u32[]{:S(2)}) collective-permute-start(bf16[384,1536]{1,0:T(8,128)(2,1)S(1)} %convolution_convert_fusion.2), channel_id=1, source_target_pairs={{0,2},{1,3},{2,0},{3,1},{4,6},{5,7},{6,4},{7,5},{8,10},{9,11},{10,... | collective-permute-start | bytes 3538952 | tf_op jit(solution)/shard_map/ppermute | solution.py:77
  442.6 27.3 %collective-permute-start.75 = (bf16[384,1536]{1,0:T(8,128)(2,1)S(1)}, bf16[384,1536]{1,0:T(8,128)(2,1)S(1)}, u32[]{:S(2)}, u32[]{:S(2)}) collective-permute-start(bf16[384,1536]{1,0:T(8,128)(2,1)S(1)} %bitcast.81), channel_id=1, source_target_pairs={{0,4},{1,5},{2,6},{3,7},{4,0},{5,1},{6,2},{7,3},{8,12},{9,13},{10,... | collective-permute-start | bytes 3538952 | tf_op jit(solution)/shard_map/ppermute | solution.py:77
  521.3 51.1 %collective-permute-start.85 = (bf16[384,1792]{1,0:T(8,128)(2,1)}, bf16[384,1792]{1,0:T(8,128)(2,1)S(1)}, u32[]{:S(2)}, u32[]{:S(2)}) collective-permute-start(bf16[384,1792]{1,0:T(8,128)(2,1)} %copy-done.62), channel_id=1, source_target_pairs={{0,8},{1,9},{2,10},{3,11},{4,12},{5,13},{6,14},{7,15},{8,0},{9,1},... | collective-permute-start | bytes 4128776 | tf_op jit(solution)/shard_map/ppermute | solution.py:77
  521.5 50.9 %collective-permute-start.86 = (bf16[384,2560]{1,0:T(8,128)(2,1)S(1)}, bf16[384,2560]{1,0:T(8,128)(2,1)S(1)}, u32[]{:S(2)}, u32[]{:S(2)}) collective-permute-start(bf16[384,2560]{1,0:T(8,128)(2,1)S(1)} %copy-done.61), channel_id=1, source_target_pairs={{0,4},{1,5},{2,6},{3,7},{4,0},{5,1},{6,2},{7,3},{8,12},{9,13},{10,... | collective-permute-start | bytes 5898248 | tf_op jit(solution)/shard_map/ppermute | solution.py:77
  533.0 39.4 %collective-permute-start.91 = (bf16[384,1920]{1,0:T(8,128)(2,1)S(1)}, bf16[384,1920]{1,0:T(8,128)(2,1)S(1)}, u32[]{:S(2)}, u32[]{:S(2)}) collective-permute-start(bf16[384,1920]{1,0:T(8,128)(2,1)S(1)} %get-tuple-element.756), channel_id=1, source_target_pairs={{0,2},{1,3},{2,0},{3,1},{4,6},{5,7},{6,4},{7,5},{8,10},{9,11},{10,... | collective-permute-start | bytes 4423688 | tf_op jit(solution)/shard_map/ppermute | solution.py:77
  534.3 31.5 %collective-permute-start.90 = (bf16[208,1536]{1,0:T(8,128)(2,1)S(1)}, bf16[208,1536]{1,0:T(8,128)(2,1)S(1)}, u32[]{:S(2)}, u32[]{:S(2)}) collective-permute-start(bf16[208,1536]{1,0:T(8,128)(2,1)S(1)} %copy-done.87), channel_id=1, source_target_pairs={{0,16},{1,17},{2,18},{3,19},{4,20},{5,21},{6,22},{7,23},{8,24},{9,... | collective-permute-start | bytes 1916936 | tf_op jit(solution)/shard_map/ppermute | solution.py:77
  (199 other events, 2199.2 us)

commit v4 on v3

--- a/solution.py
+++ b/solution.py
@@ -7,7 +7,8 @@
 from jax.sharding import PartitionSpec as P
 
 HEAD_DIM = 64
-LANES = 512
+LANES = 1536
+SPAN = 512
 UNITS = ["unit0", "unit1", "unit2", "unit3", "unit4"]
 EPS = 1e-05
 NEG = -1e30
@@ -605,22 +606,22 @@
         query_ref, pair_refs, out_ref = refs[0], refs[1 : 1 + count], refs[-1]
         for r in range(row_count):
             span = slice(r * frames, (r + 1) * frames)
-            for j in range(0, LANES, 128):
+            for j in range(0, SPAN, 128):
                 lanes = slice(j, j + 128)
                 asked = two_heads(query_ref[span, lanes])
                 key, value = [pair_rows(pair_refs, p, r, lanes, row_count) for p in range(2)]
                 probs = row_probs(asked, key, refs[1 + count][r] if seen is not None else None)
                 out_ref[span, lanes] = narrow(one_row(tdot(narrow(probs), value)))
 
-    token_spec = pl.BlockSpec((tokens, LANES), lambda i: (0, i))
+    token_spec = pl.BlockSpec((tokens, SPAN), lambda i: (0, i))
     args = (query, *pairs)
-    specs = [token_spec] + [pl.BlockSpec((pairs[0].shape[0], LANES), lambda i: (0, i))] * count
+    specs = [token_spec] + [pl.BlockSpec((pairs[0].shape[0], SPAN), lambda i: (0, i))] * count
     if seen is not None:
         args = args + (seen,)
         specs.append(whole(seen))
     return pl.pallas_call(
         body,
-        grid=(width // LANES,),
+        grid=(width // SPAN,),
         out_shape=like((tokens, width), jnp.bfloat16),
         in_specs=specs,
         out_specs=token_spec,
@@ -648,7 +649,7 @@
 
         for r in range(row_count):
             span = slice(r * frames, (r + 1) * frames)
-            for j in range(0, LANES, 128):
+            for j in range(0, SPAN, 128):
                 lanes = slice(j, j + 128)
                 asked = two_heads(query_ref[span, lanes])
                 grad = two_heads(grad_ref[span, lanes])
@@ -663,8 +664,8 @@
                 put(0, r, lanes, dot(score_grad, asked))
                 put(1, r, lanes, dot(narrow(probs), grad))
 
-    token_spec = pl.BlockSpec((tokens, LANES), lambda i: (0, i))
-    specs = [token_spec] * 2 + [pl.BlockSpec((block, LANES), lambda i: (0, i))] * count
+    token_spec = pl.BlockSpec((tokens, SPAN), lambda i: (0, i))
+    specs = [token_spec] * 2 + [pl.BlockSpec((block, SPAN), lambda i: (0, i))] * count
     args = (query, grads, *pairs)
     if tables is not None:
         specs = specs + [whole(table) for table in tables]
@@ -674,10 +675,10 @@
         args = args + (seen,)
     return pl.pallas_call(
         body,
-        grid=(width // LANES,),
+        grid=(width // SPAN,),
         out_shape=like((count * block + tokens, width), jnp.bfloat16),
         in_specs=specs,
-        out_specs=pl.BlockSpec((count * block + tokens, LANES), lambda i: (0, i)),
+        out_specs=pl.BlockSpec((count * block + tokens, SPAN), lambda i: (0, i)),
         compiler_params=room(12),
         cost_estimate=hint(),
     )(*args)
@@ -738,7 +739,7 @@
         out_shape=[like((rows, total), jnp.bfloat16)] * 2,
         in_specs=specs,
         out_specs=[out, out],
-        compiler_params=room(14),
+        compiler_params=room(20),
         cost_estimate=hint(),
     )(*args)
 
@@ -797,7 +798,7 @@
     units = feed_output.shape[0]
 
     vectors = [first_gain, first_shift, second_gain, second_shift, third_gain, third_shift, feed_offset]
-    vectors = jnp.pad(jnp.stack(vectors, 1), ((0, 0), (0, 128 - len(vectors))))
+    vectors = jnp.transpose(jnp.pad(jnp.stack(vectors, 0), ((0, 128 - len(vectors)), (0, 0))))
     split = 3 * width // 2
     group_one = narrow(jnp.concatenate([vectors, self_project], 1))
     memory_rows = ((0, share // 2 - cross_memory.shape[0]), (0, 0))
@@ -1015,18 +1016,14 @@
     hidden_all, mixed_all, asked_all, cross_all = [
         jnp.concatenate(traffic.done[name], 0) for name in ("hidden", "mixed", "asked", "crossed")
     ]
-    turned_triple = [turn_rows(hidden_all, matrix) for matrix in matrices]
-    turned_cross = turn_rows(cross_all, matrices[0])
-    turned_ask = turn_rows(asked_all, matrices[1])
-
     def rows_there(done):
         if "rows" not in done:
             return {}
         done["rows"] = jnp.concatenate(done["rows"], 0)
         return {"all": double_list(done["rows"], seq_masks)}
 
-    turned_cross, turned_ask, mixed_all, *turned_triple = traffic.turn(
-        [turned_cross, turned_ask, mixed_all] + turned_triple, rows_there
+    hidden_all, mixed_all, asked_all, cross_all = traffic.turn(
+        (hidden_all, mixed_all, asked_all, cross_all), rows_there
     )
     while "rows" in traffic.flows:
         traffic.turn((), rows_there)
@@ -1055,10 +1052,12 @@
     tied = traffic.turn(middles + value_grads + gate_grads, lambda done: {"back": back_flow()})
     middles, value_grads, gate_grads = tied[:blocks], tied[blocks : 2 * blocks], tied[2 * blocks :]
     drop_grad = unit_grad(middles, ups, False)[0]
-    tied = traffic.turn((drop_grad, *value_grads, *gate_grads))
+    tied = traffic.turn((drop_grad, hidden_all, *value_grads, *gate_grads))
     for _ in seq_masks[1:]:
         tied = traffic.turn(tied)
-    drop_grad, value_grads, gate_grads = tied[0], tied[1 : 1 + blocks], tied[1 + blocks :]
+    drop_grad, hidden_all, tied = tied[0], tied[1], tied[2:]
+    value_grads, gate_grads = tied[:blocks], tied[blocks:]
+    turned_triple = [turn_rows(hidden_all, matrix) for matrix in matrices]
     value_grad, value_bias_grad = unit_grad(value_grads, feed_rows, True)
     gate_grad, gate_bias_grad = unit_grad(gate_grads, feed_rows, True)
 
@@ -1085,8 +1084,8 @@
         half = units // 2
         return halve_rows(blocks, p % 2 * half, (p % 2 + 1) * half, far)
 
-    value_grad, gate_grad, drop_grad, mixed_all = traffic.turn(
-        (value_grad, gate_grad, drop_grad, mixed_all),
+    value_grad, gate_grad, drop_grad, mixed_all, *turned_triple = traffic.turn(
+        [value_grad, gate_grad, drop_grad, mixed_all] + turned_triple,
         lambda done: {"unit0": unit_flow(0)},
     )
     turned_self = [turn_rows(mixed_all, matrix) for matrix in matrices]
@@ -1103,11 +1102,15 @@
                 blocks = [narrow(widen(a) + widen(b)) for a, b in zip(blocks[:half], got)]
         return blocks[0], got[0]
 
-    (*turned_self,) = traffic.turn(turned_self, lambda done: {"term": term_flow()})
+    cross_all, asked_all, *turned_self = traffic.turn(
+        [cross_all, asked_all] + turned_self, lambda done: {"term": term_flow()}
+    )
+    turned_cross = turn_rows(cross_all, matrices[0])
+    turned_ask = turn_rows(asked_all, matrices[1])
     for _ in seq_masks[1:]:
         traffic.turn((), step=["term"])
     while "back" in traffic.flows:
-        traffic.turn((), step=["back", "term"])
+        turned_cross, turned_ask = traffic.turn((turned_cross, turned_ask), step=["back", "term"])
 
     while "back" in traffic.flows:
         unit_sums = list(traffic.turn(unit_sums, step=["back", "term"]))
@@ -1231,26 +1234,23 @@
     sums = sum(traffic.done["sums"])
     sums_turned = tdot(matrices[1], narrow(jnp.transpose(sums)))
     sums_turned = narrow(jnp.pad(sums_turned, ((0, 0), (0, 120))))
-    triple_pairs = [
-        list(
-            weight_sums(
-                [turned_triple[p], turned_self[p]],
-                [
-                    triple_all[:, p * width : (p + 1) * width],
-                    branch_all[:, shares[p] : shares[p + 1]],
-                ],
-                sums_turned if p == 1 else None,
-            )
-        )
-        for p in range(3)
-    ]
+
+    def triple_pair(p, beside=None):
+        grads = [
+            triple_all[:, p * width : (p + 1) * width],
+            branch_all[:, shares[p] : shares[p + 1]],
+        ]
+        return list(weight_sums([turned_triple[p], turned_self[p]], grads, beside))
+
+    triple_pairs = [triple_pair(0), None, triple_pair(2)]
     while traffic.count["first"] < len(batch_masks) - 1:
         traffic.turn(())
 
     def tail_first(*which):
         return once([triple_pairs[p][1] for p in which], [tail_orders[p][-1] for p in which])
 
-    traffic.turn((), lambda done: {"early": tail_first(0, 2)})
+    (sums_turned,) = traffic.turn((sums_turned,), lambda done: {"early": tail_first(0, 2)})
+    triple_pairs[1] = triple_pair(1, sums_turned)
     (triple_pairs[1][1],) = traffic.turn(
         (triple_pairs[1][1],),
         lambda done: {"unit4": unit_flow(4)},

time: 651 us -> 647 us (level)
  other arithmetic: 49.6 us -> 57.2 us
    unnamed x254 -> x239, local copies, waits for them, and re-layouts: 30.2 us -> 27 us
  transfers between devices with their start and end apart: 102 -> 102, of which waited for: 56 -> 56; matrix products, arithmetic and copies ran while one was open for 8% -> 8% of each run, Pallas kernels for 15% -> 14%
where the time goes in v4:
time: 647 us; the launch traced here: 639 us
  waiting for transfers between devices  325 us (50%)
  Pallas kernels  103 us (16%)
  starting transfers between devices  97 us (15%)
  other arithmetic  57.2 us (9%)
  local copies, waits for them, and re-layouts  35.3 us (5%)
  matrix products  18.1 us (3%)
    ppermute x102, waiting for transfers between devices, hop(): return lax.ppermute(value, AX, [(i, i ^ mask) for i in range(count)])  325 us
    ppermute x102, starting transfers between devices, hop(): return lax.ppermute(value, AX, [(i, i ^ mask) for i in range(count)])  97 us
    unnamed x239, local copies, waits for them, and re-layouts  27 us
    pallas_call x2, Pallas kernels, feed_block(): pl.pallas_call(body, grid=(count // block,), out_shape=[like((count, unit...  19.3 us
    convert_element_type x35, other arithmetic, narrow(): return value.astype(jnp.bfloat16)  18.2 us
    pallas_call x2, Pallas kernels, attend(): pl.pallas_call(body, grid=(width // SPAN,), out_shape=like((tokens, width...  14.5 us
    pallas_call x2, Pallas kernels, attend_back(): pl.pallas_call(body, grid=(width // SPAN,), out_shape=like((count * block...  14.5 us
    pallas_call x2, Pallas kernels, settle(): pl.pallas_call(body, out_shape=[jax.ShapeDtypeStruct((total * rows, width...  13.7 us
  transfers between devices with their start and end apart: 102, of which 56 were waited for; matrix products, arithmetic and copies ran while one was open for 8% of the time, Pallas kernels for 14%

profile of v4, /device:TPU:0, one launch (start us, length us, event | category | flops | bytes accessed | tf_op | source)
XLA Modules:
  0.0 639.4 jit_solution(1615013544786811781)
XLA Ops:
  23.7 6.5 %collective-permute-done = bf16[48,4736]{1,0:T(8,128)(2,1)S(1)} collective-permute-done((bf16[48,4736]{1,0:T(8,128)(2,1)}, bf16[48,4736]{1,0:T(8,128)(2,1)S(1)}, u32[]{:S(2)}, u32[]{:S(2)}) %collective-permute-start) | collective-permute-done | bytes 454688 | tf_op jit(solution)/shard_map/ppermute | solution.py:78
  31.3 20.3 %collective-permute-done.1 = bf16[96,4736]{1,0:T(8,128)(2,1)S(1)} collective-permute-done((bf16[96,4736]{1,0:T(8,128)(2,1)S(1)}, bf16[96,4736]{1,0:T(8,128)(2,1)S(1)}, u32[]{:S(2)}, u32[]{:S(2)}) %collective-permute-start.1) | collective-permute-done | bytes 909344 | tf_op jit(solution)/shard_map/ppermute | solution.py:78
  59.3 22.3 %collective-permute-done.2 = bf16[48,6144]{1,0:T(8,128)(2,1)S(1)} collective-permute-done((bf16[48,6144]{1,0:T(8,128)(2,1)S(1)}, bf16[48,6144]{1,0:T(8,128)(2,1)S(1)}, u32[]{:S(2)}, u32[]{:S(2)}) %collective-permute-start.2) | collective-permute-done | bytes 589856 | tf_op jit(solution)/shard_map/ppermute | solution.py:78
  89.3 35.8 %collective-permute-done.7 = bf16[208,1536]{1,0:T(8,128)(2,1)S(1)} collective-permute-done((bf16[208,1536]{1,0:T(8,128)(2,1)S(1)}, bf16[208,1536]{1,0:T(8,128)(2,1)S(1)}, u32[]{:S(2)}, u32[]{:S(2)}) %collective-permute-start.7) | collective-permute-done | bytes 639008 | tf_op jit(solution)/shard_map/ppermute | solution.py:78
  130.3 26.1 %collective-permute-done.10 = bf16[192,3072]{1,0:T(8,128)(2,1)S(1)} collective-permute-done((bf16[192,3072]{1,0:T(8,128)(2,1)S(1)}, bf16[192,3072]{1,0:T(8,128)(2,1)S(1)}, u32[]{:S(2)}, u32[]{:S(2)}) %collective-permute-start.10) | collective-permute-done | bytes 1179680 | tf_op jit(solution)/shard_map/ppermute | solution.py:78
  164.9 6.9 %shard_map.350 = (bf16[1536,128]{1,0:T(8,128)(2,1)S(1)}, bf16[1536,4608]{1,0:T(8,128)(2,1)S(1)}) custom-call(s32[1]{0:T(128)} %bitcast.14.me_ref, bf16[384,2432]{1,0:T(8,128)(2,1)S(1)} %pad_maximum_fusion.3.refs_0_, bf16[384,2432]{1,0:T(8,128)(2,1)S(1)} %collective-permute-done.5.refs_1_, bf16[384,2432]{1,0:T(8,128)(2,1)S(1)} %collective-permute-done.9.refs_2_, ...), custom_call_target="tpu_custom_call" | custom-call | bytes 909312 | tf_op jit(solution)/shard_map/pallas_call | solution.py:144
  179.2 7.0 %shard_map.352.mixed_ref = bf16[128,1536]{1,0:T(8,128)(2,1)S(1)} custom-call(bf16[128,1536]{1,0:T(8,128)(2,1)S(1)} %get-tuple-element.473.refs_0_, bf16[256,1536]{1,0:T(8,128)(2,1)S(1)} %get-tuple-element.471.refs_1_.refs_2_, bf16[256,1536]{1,0:T(8,128)(2,1)S(1)} %collective-permute-done.19.refs_2_.refs_3_, f32[2,128,64]{2,1,0:T(8,128)S(1)} %compare_convert_fusion.refs_3_.refs_6_), custom_call_target="tpu_custom_call" | custom-call | flops 1048576 | bytes 1048576 | tf_op jit(solution)/shard_map/pallas_call | solution.py:622
  186.3 30.0 %collective-permute-done.18 = bf16[384,1536]{1,0:T(8,128)(2,1)S(1)} collective-permute-done((bf16[384,1536]{1,0:T(8,128)(2,1)}, bf16[384,1536]{1,0:T(8,128)(2,1)S(1)}, u32[]{:S(2)}, u32[]{:S(2)}) %collective-permute-start.18) | collective-permute-done | bytes 1179680 | tf_op jit(solution)/shard_map/ppermute | solution.py:78
  231.3 6.8 %shard_map.353 = (bf16[1536,1536]{1,0:T(8,128)(2,1)S(1)}, bf16[1536,1536]{1,0:T(8,128)(2,1)S(1)}, bf16[1536,1536]{1,0:T(8,128)(2,1)S(1)}, bf16[1536,1536]{1,0:T(8,128)(2,1)}) custom-call(s32[1]{0:T(128)} %bitcast.14.me_ref, bf16[384,3072]{1,0:T(8,128)(2,1)S(1)} %pad_maximum_fusion.1.refs_0_, bf16[384,3072]{1,0:T(8,128)(2,1)S(1)} %copy-done.19, ...), custom_call_target="tpu_custom_call" | custom-call | bytes 1179648 | tf_op jit(solution)/shard_map/pallas_call | solution.py:144
  250.2 7.4 %shard_map.356.mixed_ref = bf16[128,1536]{1,0:T(8,128)(2,1)S(1)} custom-call(bf16[128,1536]{1,0:T(8,128)(2,1)S(1)} %get-tuple-element.535.refs_0_, bf16[512,1536]{1,0:T(8,128)(2,1)S(1)} %shard_map.355.refs_1_.refs_2_), custom_call_target="tpu_custom_call" | custom-call | flops 1048576 | bytes 1048576 | tf_op jit(solution)/shard_map/pallas_call | solution.py:622
  287.0 9.1 %collective-permute-done.43 = bf16[128,1536]{1,0:T(8,128)(2,1)S(1)} collective-permute-done((bf16[128,1536]{1,0:T(8,128)(2,1)S(1)}, bf16[128,1536]{1,0:T(8,128)(2,1)S(1)}, u32[]{:S(2)}, u32[]{:S(2)}) %collective-permute-start.43) | collective-permute-done | bytes 393248 | tf_op jit(solution)/shard_map/ppermute | solution.py:78
  301.0 9.6 %shard_map.358 = (bf16[1024,384]{1,0:T(8,128)(2,1)S(1)}, bf16[1024,384]{1,0:T(8,128)(2,1)S(1)}, bf16[1024,384]{1,0:T(8,128)(2,1)S(1)}, bf16[1024,1536]{1,0:T(8,128)(2,1)S(1)}) custom-call(bf16[1024,1536]{1,0:T(8,128)(2,1)S(1)} %constant_dynamic-update-slice_fusion.9.row_ref.refs_2_, ...), custom_call_target="tpu_custom_call" | custom-call | flops 1048576 | bytes 1048576 | tf_op jit(solution)/shard_map/pallas_call | solution.py:492
  315.3 9.7 %shard_map.359 = (bf16[1024,384]{1,0:T(8,128)(2,1)S(1)}, bf16[1024,384]{1,0:T(8,128)(2,1)S(1)}, bf16[1024,384]{1,0:T(8,128)(2,1)S(1)}, bf16[1024,1536]{1,0:T(8,128)(2,1)S(1)}) custom-call(bf16[1024,1536]{1,0:T(8,128)(2,1)S(1)} %collective-permute-done.46.row_ref.refs_3_, bf16[1024,1536]{1,0:T(8,128)(2,1)S(1)} %copy-done.6, bf16[384,1536]{1,0:T(8,128)(2,1)S(1)} %copy-done.8, ...), custom_call_target="tpu_custom_call" | custom-call | flops 1048576 | bytes 1048576 | tf_op jit(solution)/shard_map/pallas_call | solution.py:492
  360.8 7.5 %collective-permute-done.52 = bf16[96,1536]{1,0:T(8,128)(2,1)S(1)} collective-permute-done((bf16[96,1536]{1,0:T(8,128)(2,1)S(1)}, bf16[96,1536]{1,0:T(8,128)(2,1)S(1)}, u32[]{:S(2)}, u32[]{:S(2)}) %collective-permute-start.52) | collective-permute-done | bytes 294944 | tf_op jit(solution)/shard_map/ppermute | solution.py:78
  404.0 7.2 %shard_map.366.in_ref = bf16[640,1536]{1,0:T(8,128)(2,1)S(1)} custom-call(bf16[128,1536]{1,0:T(8,128)(2,1)S(1)} %copy-done.33, bf16[128,1536]{1,0:T(8,128)(2,1)S(1)} %get-tuple-element.691.refs_1_, bf16[512,1536]{1,0:T(8,128)(2,1)S(1)} %shard_map.355.refs_1_.refs_2_), custom_call_target="tpu_custom_call" | custom-call | flops 1048576 | bytes 1048576 | tf_op jit(solution)/shard_map/pallas_call | solution.py:676
  425.5 6.9 %collective-permute-done.71 = bf16[96,1536]{1,0:T(8,128)(2,1)S(1)} collective-permute-done((bf16[96,1536]{1,0:T(8,128)(2,1)S(1)}, bf16[96,1536]{1,0:T(8,128)(2,1)S(1)}, u32[]{:S(2)}, u32[]{:S(2)}) %collective-permute-start.71) | collective-permute-done | bytes 294944 | tf_op jit(solution)/shard_map/ppermute | solution.py:78
  439.0 7.3 %shard_map.368.query_ref.own_ref = bf16[640,1536]{1,0:T(8,128)(2,1)S(1)} custom-call(bf16[128,1536]{1,0:T(8,128)(2,1)S(1)} %copy-done.31, bf16[128,1536]{1,0:T(8,128)(2,1)S(1)} %get-tuple-element.727.refs_1_, bf16[256,1536]{1,0:T(8,128)(2,1)S(1)} %copy-done.13, bf16[256,1536]{1,0:T(8,128)(2,1)S(1)} %copy-done.15, f32[128,128]{1,0:T(8,128)S(1)} %copy-done.40, ...), custom_call_target="tpu_custom_call" | custom-call | flops 1048576 | bytes 1048576 | tf_op jit(solution)/shard_map/pallas_call | solution.py:676
  449.8 15.1 %collective-permute-done.73 = bf16[384,1536]{1,0:T(8,128)(2,1)S(1)} collective-permute-done((bf16[384,1536]{1,0:T(8,128)(2,1)S(1)}, bf16[384,1536]{1,0:T(8,128)(2,1)S(1)}, u32[]{:S(2)}, u32[]{:S(2)}) %collective-permute-start.73) | collective-permute-done | bytes 1179680 | tf_op jit(solution)/shard_map/ppermute | solution.py:78
  478.5 6.8 %collective-permute-done.77 = bf16[192,1536]{1,0:T(8,128)(2,1)} collective-permute-done((bf16[192,1536]{1,0:T(8,128)(2,1)}, bf16[192,1536]{1,0:T(8,128)(2,1)}, u32[]{:S(2)}, u32[]{:S(2)}) %collective-permute-start.77) | collective-permute-done | bytes 589856 | tf_op jit(solution)/shard_map/ppermute | solution.py:78
  535.9 28.6 %collective-permute-done.90 = bf16[208,1536]{1,0:T(8,128)(2,1)S(1)} collective-permute-done((bf16[208,1536]{1,0:T(8,128)(2,1)S(1)}, bf16[208,1536]{1,0:T(8,128)(2,1)S(1)}, u32[]{:S(2)}, u32[]{:S(2)}) %collective-permute-start.90) | collective-permute-done | bytes 639008 | tf_op jit(solution)/shard_map/ppermute | solution.py:78
  578.5 7.9 %collective-permute-done.95 = bf16[96,1536]{1,0:T(8,128)(2,1)S(1)} collective-permute-done((bf16[96,1536]{1,0:T(8,128)(2,1)S(1)}, bf16[96,1536]{1,0:T(8,128)(2,1)S(1)}, u32[]{:S(2)}, u32[]{:S(2)}) %collective-permute-start.95) | collective-permute-done | bytes 294944 | tf_op jit(solution)/shard_map/ppermute | solution.py:78
  588.3 9.4 %collective-permute-done.93 = bf16[192,1920]{1,0:T(8,128)(2,1)S(1)} collective-permute-done((bf16[192,1920]{1,0:T(8,128)(2,1)S(1)}, bf16[192,1920]{1,0:T(8,128)(2,1)S(1)}, u32[]{:S(2)}, u32[]{:S(2)}) %collective-permute-start.93) | collective-permute-done | bytes 737312 | tf_op jit(solution)/shard_map/ppermute | solution.py:78
  601.2 12.7 %collective-permute-done.96 = bf16[96,1792]{1,0:T(8,128)(2,1)S(1)} collective-permute-done((bf16[96,1792]{1,0:T(8,128)(2,1)S(1)}, bf16[96,1792]{1,0:T(8,128)(2,1)S(1)}, u32[]{:S(2)}, u32[]{:S(2)}) %collective-permute-start.96) | collective-permute-done | bytes 344096 | tf_op jit(solution)/shard_map/ppermute | solution.py:78
  622.5 8.2 %collective-permute-done.100 = bf16[48,1920]{1,0:T(8,128)(2,1)S(1)} collective-permute-done((bf16[48,1920]{1,0:T(8,128)(2,1)S(1)}, bf16[48,1920]{1,0:T(8,128)(2,1)S(1)}, u32[]{:S(2)}, u32[]{:S(2)}) %collective-permute-start.100) | collective-permute-done | bytes 184352 | tf_op jit(solution)/shard_map/ppermute | solution.py:78
  (662 shorter events, 320.8 us)
Async XLA Ops:
  5.8 24.4 %collective-permute-start = (bf16[48,4736]{1,0:T(8,128)(2,1)}, bf16[48,4736]{1,0:T(8,128)(2,1)S(1)}, u32[]{:S(2)}, u32[]{:S(2)}) collective-permute-start(bf16[48,4736]{1,0:T(8,128)(2,1)} %pad_maximum_fusion.35), channel_id=1, source_target_pairs={{0,16},{1,17},{2,18},{3,19},{4,20},{5,21},{6,22},{7,23},{8,24},{9,... | collective-permute-start | bytes 1363976 | tf_op jit(solution)/shard_map/ppermute | solution.py:78
  52.8 28.8 %collective-permute-start.2 = (bf16[48,6144]{1,0:T(8,128)(2,1)S(1)}, bf16[48,6144]{1,0:T(8,128)(2,1)S(1)}, u32[]{:S(2)}, u32[]{:S(2)}) collective-permute-start(bf16[48,6144]{1,0:T(8,128)(2,1)S(1)} %maximum_maximum_fusion), channel_id=1, source_target_pairs={{0,16},{1,17},{2,18},{3,19},{4,20},{5,21},{6,22},{7,23},{8,24},{9,... | collective-permute-start | bytes 1769480 | tf_op jit(solution)/shard_map/ppermute | solution.py:78
  56.2 25.5 %collective-permute-start.4 = (bf16[192,2304]{1,0:T(8,128)(2,1)S(1)}, bf16[192,2304]{1,0:T(8,128)(2,1)S(1)}, u32[]{:S(2)}, u32[]{:S(2)}) collective-permute-start(bf16[192,2304]{1,0:T(8,128)(2,1)S(1)} %slice.704), channel_id=1, source_target_pairs={{0,4},{1,5},{2,6},{3,7},{4,0},{5,1},{6,2},{7,3},{8,12},{9,13},{10,... | collective-permute-start | bytes 2654216 | tf_op jit(solution)/shard_map/ppermute | solution.py:78
  82.0 44.9 %collective-permute-start.5 = (bf16[384,2432]{1,0:T(8,128)(2,1)S(1)}, bf16[384,2432]{1,0:T(8,128)(2,1)S(1)}, u32[]{:S(2)}, u32[]{:S(2)}) collective-permute-start(bf16[384,2432]{1,0:T(8,128)(2,1)S(1)} %pad_maximum_fusion.3.refs_0_), channel_id=1, source_target_pairs={{0,4},{1,5},{2,6},{3,7},{4,0},{5,1},{6,2},{7,3},{8,12},{9,13},{10,... | collective-permute-start | bytes 5603336 | tf_op jit(solution)/shard_map/ppermute | solution.py:78
  83.6 43.3 %collective-permute-start.9 = (bf16[384,2432]{1,0:T(8,128)(2,1)S(1)}, bf16[384,2432]{1,0:T(8,128)(2,1)S(1)}, u32[]{:S(2)}, u32[]{:S(2)}) collective-permute-start(bf16[384,2432]{1,0:T(8,128)(2,1)S(1)} %pad_maximum_fusion.3.refs_0_), channel_id=1, source_target_pairs={{0,1},{1,0},{2,3},{3,2},{4,5},{5,4},{6,7},{7,6},{8,9},{9,8},{10,11... | collective-permute-start | bytes 5603336 | tf_op jit(solution)/shard_map/ppermute | solution.py:78
  83.6 43.3 %collective-permute-start.6 = (bf16[384,2304]{1,0:T(8,128)(2,1)S(1)}, bf16[384,2304]{1,0:T(8,128)(2,1)S(1)}, u32[]{:S(2)}, u32[]{:S(2)}) collective-permute-start(bf16[384,2304]{1,0:T(8,128)(2,1)S(1)} %pad_maximum_fusion.5.refs_4_), channel_id=1, source_target_pairs={{0,2},{1,3},{2,0},{3,1},{4,6},{5,7},{6,4},{7,5},{8,10},{9,11},{10,... | collective-permute-start | bytes 5308424 | tf_op jit(solution)/shard_map/ppermute | solution.py:78
  85.1 41.8 %collective-permute-start.8 = (bf16[96,6144]{1,0:T(8,128)(2,1)S(1)}, bf16[96,6144]{1,0:T(8,128)(2,1)S(1)}, u32[]{:S(2)}, u32[]{:S(2)}) collective-permute-start(bf16[96,6144]{1,0:T(8,128)(2,1)S(1)} %pad_maximum_fusion.9), channel_id=1, source_target_pairs={{0,8},{1,9},{2,10},{3,11},{4,12},{5,13},{6,14},{7,15},{8,0},{9,1},... | collective-permute-start | bytes 3538952 | tf_op jit(solution)/shard_map/ppermute | solution.py:78
  85.8 39.3 %collective-permute-start.7 = (bf16[208,1536]{1,0:T(8,128)(2,1)S(1)}, bf16[208,1536]{1,0:T(8,128)(2,1)S(1)}, u32[]{:S(2)}, u32[]{:S(2)}) collective-permute-start(bf16[208,1536]{1,0:T(8,128)(2,1)S(1)} %fusion.19), channel_id=1, source_target_pairs={{0,16},{1,17},{2,18},{3,19},{4,20},{5,21},{6,22},{7,23},{8,24},{9,... | collective-permute-start | bytes 1916936 | tf_op jit(solution)/shard_map/ppermute | solution.py:78
  127.2 32.1 %collective-permute-start.13 = (bf16[384,2432]{1,0:T(8,128)(2,1)S(1)}, bf16[384,2432]{1,0:T(8,128)(2,1)S(1)}, u32[]{:S(2)}, u32[]{:S(2)}) collective-permute-start(bf16[384,2432]{1,0:T(8,128)(2,1)S(1)} %collective-permute-done.5.refs_1_), channel_id=1, source_target_pairs={{0,1},{1,0},{2,3},{3,2},{4,5},{5,4},{6,7},{7,6},{8,9},{9,8},{10,11... | collective-permute-start | bytes 5603336 | tf_op jit(solution)/shard_map/ppermute | solution.py:78
  127.2 29.5 %collective-permute-start.12 = (bf16[384,2304]{1,0:T(8,128)(2,1)S(1)}, bf16[384,2304]{1,0:T(8,128)(2,1)S(1)}, u32[]{:S(2)}, u32[]{:S(2)}) collective-permute-start(bf16[384,2304]{1,0:T(8,128)(2,1)S(1)} %pad_maximum_fusion.5.refs_4_), channel_id=1, source_target_pairs={{0,1},{1,0},{2,3},{3,2},{4,5},{5,4},{6,7},{7,6},{8,9},{9,8},{10,11... | collective-permute-start | bytes 5308424 | tf_op jit(solution)/shard_map/ppermute | solution.py:78
  128.1 29.9 %collective-permute-start.14 = (bf16[384,2304]{1,0:T(8,128)(2,1)S(1)}, bf16[384,2304]{1,0:T(8,128)(2,1)S(1)}, u32[]{:S(2)}, u32[]{:S(2)}) collective-permute-start(bf16[384,2304]{1,0:T(8,128)(2,1)S(1)} %collective-permute-done.6.refs_5_), channel_id=1, source_target_pairs={{0,1},{1,0},{2,3},{3,2},{4,5},{5,4},{6,7},{7,6},{8,9},{9,8},{10,11... | collective-permute-start | bytes 5308424 | tf_op jit(solution)/shard_map/ppermute | solution.py:78
  128.1 28.4 %collective-permute-start.10 = (bf16[192,3072]{1,0:T(8,128)(2,1)S(1)}, bf16[192,3072]{1,0:T(8,128)(2,1)S(1)}, u32[]{:S(2)}, u32[]{:S(2)}) collective-permute-start(bf16[192,3072]{1,0:T(8,128)(2,1)S(1)} %get-tuple-element.431), channel_id=1, source_target_pairs={{0,2},{1,3},{2,0},{3,1},{4,6},{5,7},{6,4},{7,5},{8,10},{9,11},{10,... | collective-permute-start | bytes 3538952 | tf_op jit(solution)/shard_map/ppermute | solution.py:78
  128.6 28.1 %collective-permute-start.11 = (bf16[192,3072]{1,0:T(8,128)(2,1)S(1)}, bf16[192,3072]{1,0:T(8,128)(2,1)S(1)}, u32[]{:S(2)}, u32[]{:S(2)}) collective-permute-start(bf16[192,3072]{1,0:T(8,128)(2,1)S(1)} %get-tuple-element.432), channel_id=1, source_target_pairs={{0,4},{1,5},{2,6},{3,7},{4,0},{5,1},{6,2},{7,3},{8,12},{9,13},{10,... | collective-permute-start | bytes 3538952 | tf_op jit(solution)/shard_map/ppermute | solution.py:78
  159.6 56.8 %collective-permute-start.15 = (bf16[384,3072]{1,0:T(8,128)(2,1)S(1)}, bf16[384,3072]{1,0:T(8,128)(2,1)S(1)}, u32[]{:S(2)}, u32[]{:S(2)}) collective-permute-start(bf16[384,3072]{1,0:T(8,128)(2,1)S(1)} %pad_maximum_fusion.1.refs_0_), channel_id=1, source_target_pairs={{0,4},{1,5},{2,6},{3,7},{4,0},{5,1},{6,2},{7,3},{8,12},{9,13},{10,... | collective-permute-start | bytes 7077896 | tf_op jit(solution)/shard_map/ppermute | solution.py:78
  160.1 56.3 %collective-permute-start.16 = (bf16[384,3072]{1,0:T(8,128)(2,1)S(1)}, bf16[384,3072]{1,0:T(8,128)(2,1)S(1)}, u32[]{:S(2)}, u32[]{:S(2)}) collective-permute-start(bf16[384,3072]{1,0:T(8,128)(2,1)S(1)} %pad_maximum_fusion.refs_4_), channel_id=1, source_target_pairs={{0,2},{1,3},{2,0},{3,1},{4,6},{5,7},{6,4},{7,5},{8,10},{9,11},{10,... | collective-permute-start | bytes 7077896 | tf_op jit(solution)/shard_map/ppermute | solution.py:78
  161.6 54.8 %collective-permute-start.17 = (bf16[384,3072]{1,0:T(8,128)(2,1)S(1)}, bf16[384,3072]{1,0:T(8,128)(2,1)}, u32[]{:S(2)}, u32[]{:S(2)}) collective-permute-start(bf16[384,3072]{1,0:T(8,128)(2,1)S(1)} %pad_maximum_fusion.1.refs_0_), channel_id=1, source_target_pairs={{0,1},{1,0},{2,3},{3,2},{4,5},{5,4},{6,7},{7,6},{8,9},{9,8},{10,11... | collective-permute-start | bytes 7077896 | tf_op jit(solution)/shard_map/ppermute | solution.py:78
  161.6 54.8 %collective-permute-start.18 = (bf16[384,1536]{1,0:T(8,128)(2,1)}, bf16[384,1536]{1,0:T(8,128)(2,1)S(1)}, u32[]{:S(2)}, u32[]{:S(2)}) collective-permute-start(bf16[384,1536]{1,0:T(8,128)(2,1)} %bitcast.12), channel_id=1, source_target_pairs={{0,16},{1,17},{2,18},{3,19},{4,20},{5,21},{6,22},{7,23},{8,24},{9,... | collective-permute-start | bytes 3538952 | tf_op jit(solution)/shard_map/ppermute | solution.py:78
  436.9 28.0 %collective-permute-start.73 = (bf16[384,1536]{1,0:T(8,128)(2,1)S(1)}, bf16[384,1536]{1,0:T(8,128)(2,1)S(1)}, u32[]{:S(2)}, u32[]{:S(2)}) collective-permute-start(bf16[384,1536]{1,0:T(8,128)(2,1)S(1)} %convolution_convert_fusion.3), channel_id=1, source_target_pairs={{0,8},{1,9},{2,10},{3,11},{4,12},{5,13},{6,14},{7,15},{8,0},{9,1},... | collective-permute-start | bytes 3538952 | tf_op jit(solution)/shard_map/ppermute | solution.py:78
  436.9 28.0 %collective-permute-start.74 = (bf16[384,1536]{1,0:T(8,128)(2,1)S(1)}, bf16[384,1536]{1,0:T(8,128)(2,1)S(1)}, u32[]{:S(2)}, u32[]{:S(2)}) collective-permute-start(bf16[384,1536]{1,0:T(8,128)(2,1)S(1)} %convolution_convert_fusion.2), channel_id=1, source_target_pairs={{0,2},{1,3},{2,0},{3,1},{4,6},{5,7},{6,4},{7,5},{8,10},{9,11},{10,... | collective-permute-start | bytes 3538952 | tf_op jit(solution)/shard_map/ppermute | solution.py:78
  437.9 27.5 %collective-permute-start.75 = (bf16[384,1536]{1,0:T(8,128)(2,1)S(1)}, bf16[384,1536]{1,0:T(8,128)(2,1)S(1)}, u32[]{:S(2)}, u32[]{:S(2)}) collective-permute-start(bf16[384,1536]{1,0:T(8,128)(2,1)S(1)} %bitcast.85), channel_id=1, source_target_pairs={{0,4},{1,5},{2,6},{3,7},{4,0},{5,1},{6,2},{7,3},{8,12},{9,13},{10,... | collective-permute-start | bytes 3538952 | tf_op jit(solution)/shard_map/ppermute | solution.py:78
  519.5 50.3 %collective-permute-start.85 = (bf16[384,1792]{1,0:T(8,128)(2,1)}, bf16[384,1792]{1,0:T(8,128)(2,1)S(1)}, u32[]{:S(2)}, u32[]{:S(2)}) collective-permute-start(bf16[384,1792]{1,0:T(8,128)(2,1)} %copy-done.62), channel_id=1, source_target_pairs={{0,8},{1,9},{2,10},{3,11},{4,12},{5,13},{6,14},{7,15},{8,0},{9,1},... | collective-permute-start | bytes 4128776 | tf_op jit(solution)/shard_map/ppermute | solution.py:78
  519.5 50.3 %collective-permute-start.86 = (bf16[384,2560]{1,0:T(8,128)(2,1)S(1)}, bf16[384,2560]{1,0:T(8,128)(2,1)S(1)}, u32[]{:S(2)}, u32[]{:S(2)}) collective-permute-start(bf16[384,2560]{1,0:T(8,128)(2,1)S(1)} %copy-done.61), channel_id=1, source_target_pairs={{0,4},{1,5},{2,6},{3,7},{4,0},{5,1},{6,2},{7,3},{8,12},{9,13},{10,... | collective-permute-start | bytes 5898248 | tf_op jit(solution)/shard_map/ppermute | solution.py:78
  530.9 39.0 %collective-permute-start.91 = (bf16[384,1920]{1,0:T(8,128)(2,1)S(1)}, bf16[384,1920]{1,0:T(8,128)(2,1)S(1)}, u32[]{:S(2)}, u32[]{:S(2)}) collective-permute-start(bf16[384,1920]{1,0:T(8,128)(2,1)S(1)} %get-tuple-element.784), channel_id=1, source_target_pairs={{0,2},{1,3},{2,0},{3,1},{4,6},{5,7},{6,4},{7,5},{8,10},{9,11},{10,... | collective-permute-start | bytes 4423688 | tf_op jit(solution)/shard_map/ppermute | solution.py:78
  531.8 32.8 %collective-permute-start.90 = (bf16[208,1536]{1,0:T(8,128)(2,1)S(1)}, bf16[208,1536]{1,0:T(8,128)(2,1)S(1)}, u32[]{:S(2)}, u32[]{:S(2)}) collective-permute-start(bf16[208,1536]{1,0:T(8,128)(2,1)S(1)} %copy-done.87), channel_id=1, source_target_pairs={{0,16},{1,17},{2,18},{3,19},{4,20},{5,21},{6,22},{7,23},{8,24},{9,... | collective-permute-start | bytes 1916936 | tf_op jit(solution)/shard_map/ppermute | solution.py:78
  (192 other events, 2099.6 us)

commit v5 on v4

--- a/solution.py
+++ b/solution.py
@@ -1210,7 +1210,8 @@
         traffic.turn((), step=["pair"])
     triple_back = spin_backward(*traffic.done["pair"], *back_tables)
     (triple_back,) = traffic.turn(
-        (triple_back,), lambda done: {"dt": double_list(triple_back, seq_masks)}
+        (triple_back,),
+        lambda done: {"dt": double_list(triple_back, seq_masks), "unit3": unit_flow(3)},
     )
     frame_grad, grad_gain_one, grad_shift_one = back(
         triple_back, triple_low, self_out_grad, normed_one, inverse_one, gain_one
@@ -1270,7 +1271,7 @@
                 ]
             )
         orders = [order[:-1] for order in tail_orders]
-        return {"tail": halve_pairs(pairs, orders), "unit3": unit_flow(3)}
+        return {"tail": halve_pairs(pairs, orders)}
 
     traffic.turn((), tail_rest)
     while traffic.flows:

time: 647 us -> 660 us (1.020)
  waiting for transfers between devices: 325 us -> 333 us
    ppermute x102, waiting for transfers between devices: 325 us -> 333 us  [hop(): return lax.ppermute(value, AX, [(i, i ^ mask) for i in range(count)])]
    unnamed x239 -> x233, local copies, waits for them, and re-layouts: 27 us -> 27.6 us
  transfers between devices with their start and end apart: 102 -> 102, of which waited for: 56 -> 55; matrix products, arithmetic and copies ran while one was open for 8% -> 8% of each run, Pallas kernels for 14% -> 14%
where the time goes in v5:
time: 660 us; the launch traced here: 652 us
  waiting for transfers between devices  333 us (50%)
  Pallas kernels  103 us (16%)
  starting transfers between devices  101 us (15%)
  other arithmetic  56.6 us (9%)
  local copies, waits for them, and re-layouts  35.9 us (5%)
  matrix products  18.2 us (3%)
    ppermute x102, waiting for transfers between devices, hop(): return lax.ppermute(value, AX, [(i, i ^ mask) for i in range(count)])  333 us
    ppermute x102, starting transfers between devices, hop(): return lax.ppermute(value, AX, [(i, i ^ mask) for i in range(count)])  101 us
    unnamed x233, local copies, waits for them, and re-layouts  27.6 us
    pallas_call x2, Pallas kernels, feed_block(): pl.pallas_call(body, grid=(count // block,), out_shape=[like((count, unit...  19.3 us
    convert_element_type x35, other arithmetic, narrow(): return value.astype(jnp.bfloat16)  18.4 us
    pallas_call x2, Pallas kernels, attend_back(): pl.pallas_call(body, grid=(width // SPAN,), out_shape=like((count * block...  14.5 us
    pallas_call x2, Pallas kernels, attend(): pl.pallas_call(body, grid=(width // SPAN,), out_shape=like((tokens, width...  14.5 us
    pallas_call x2, Pallas kernels, settle(): pl.pallas_call(body, out_shape=[jax.ShapeDtypeStruct((total * rows, width...  13.7 us
  transfers between devices with their start and end apart: 102, of which 55 were waited for; matrix products, arithmetic and copies ran while one was open for 8% of the time, Pallas kernels for 14%

profile of v5, /device:TPU:0, one launch (start us, length us, event | category | flops | bytes accessed | tf_op | source)
XLA Modules:
  0.0 651.7 jit_solution(16701443568861202661)
XLA Ops:
  23.7 6.5 %collective-permute-done = bf16[48,4736]{1,0:T(8,128)(2,1)S(1)} collective-permute-done((bf16[48,4736]{1,0:T(8,128)(2,1)}, bf16[48,4736]{1,0:T(8,128)(2,1)S(1)}, u32[]{:S(2)}, u32[]{:S(2)}) %collective-permute-start) | collective-permute-done | bytes 454688 | tf_op jit(solution)/shard_map/ppermute | solution.py:78
  31.3 20.3 %collective-permute-done.1 = bf16[96,4736]{1,0:T(8,128)(2,1)S(1)} collective-permute-done((bf16[96,4736]{1,0:T(8,128)(2,1)S(1)}, bf16[96,4736]{1,0:T(8,128)(2,1)S(1)}, u32[]{:S(2)}, u32[]{:S(2)}) %collective-permute-start.1) | collective-permute-done | bytes 909344 | tf_op jit(solution)/shard_map/ppermute | solution.py:78
  59.3 22.3 %collective-permute-done.2 = bf16[48,6144]{1,0:T(8,128)(2,1)S(1)} collective-permute-done((bf16[48,6144]{1,0:T(8,128)(2,1)S(1)}, bf16[48,6144]{1,0:T(8,128)(2,1)S(1)}, u32[]{:S(2)}, u32[]{:S(2)}) %collective-permute-start.2) | collective-permute-done | bytes 589856 | tf_op jit(solution)/shard_map/ppermute | solution.py:78
  89.3 35.8 %collective-permute-done.7 = bf16[208,1536]{1,0:T(8,128)(2,1)S(1)} collective-permute-done((bf16[208,1536]{1,0:T(8,128)(2,1)S(1)}, bf16[208,1536]{1,0:T(8,128)(2,1)S(1)}, u32[]{:S(2)}, u32[]{:S(2)}) %collective-permute-start.7) | collective-permute-done | bytes 639008 | tf_op jit(solution)/shard_map/ppermute | solution.py:78
  130.3 26.1 %collective-permute-done.10 = bf16[192,3072]{1,0:T(8,128)(2,1)S(1)} collective-permute-done((bf16[192,3072]{1,0:T(8,128)(2,1)S(1)}, bf16[192,3072]{1,0:T(8,128)(2,1)S(1)}, u32[]{:S(2)}, u32[]{:S(2)}) %collective-permute-start.10) | collective-permute-done | bytes 1179680 | tf_op jit(solution)/shard_map/ppermute | solution.py:78
  164.9 6.9 %shard_map.350 = (bf16[1536,128]{1,0:T(8,128)(2,1)S(1)}, bf16[1536,4608]{1,0:T(8,128)(2,1)S(1)}) custom-call(s32[1]{0:T(128)} %bitcast.14.me_ref, bf16[384,2432]{1,0:T(8,128)(2,1)S(1)} %pad_maximum_fusion.3.refs_0_, bf16[384,2432]{1,0:T(8,128)(2,1)S(1)} %collective-permute-done.5.refs_1_, bf16[384,2432]{1,0:T(8,128)(2,1)S(1)} %collective-permute-done.9.refs_2_, ...), custom_call_target="tpu_custom_call" | custom-call | bytes 909312 | tf_op jit(solution)/shard_map/pallas_call | solution.py:144
  179.2 7.0 %shard_map.352.mixed_ref = bf16[128,1536]{1,0:T(8,128)(2,1)S(1)} custom-call(bf16[128,1536]{1,0:T(8,128)(2,1)S(1)} %get-tuple-element.473.refs_0_, bf16[256,1536]{1,0:T(8,128)(2,1)S(1)} %get-tuple-element.471.refs_1_.refs_2_, bf16[256,1536]{1,0:T(8,128)(2,1)S(1)} %collective-permute-done.19.refs_2_.refs_3_, f32[2,128,64]{2,1,0:T(8,128)S(1)} %compare_convert_fusion.refs_3_.refs_6_), custom_call_target="tpu_custom_call" | custom-call | flops 1048576 | bytes 1048576 | tf_op jit(solution)/shard_map/pallas_call | solution.py:622
  186.3 30.1 %collective-permute-done.18 = bf16[384,1536]{1,0:T(8,128)(2,1)S(1)} collective-permute-done((bf16[384,1536]{1,0:T(8,128)(2,1)}, bf16[384,1536]{1,0:T(8,128)(2,1)S(1)}, u32[]{:S(2)}, u32[]{:S(2)}) %collective-permute-start.18) | collective-permute-done | bytes 1179680 | tf_op jit(solution)/shard_map/ppermute | solution.py:78
  231.3 6.8 %shard_map.353 = (bf16[1536,1536]{1,0:T(8,128)(2,1)S(1)}, bf16[1536,1536]{1,0:T(8,128)(2,1)S(1)}, bf16[1536,1536]{1,0:T(8,128)(2,1)S(1)}, bf16[1536,1536]{1,0:T(8,128)(2,1)}) custom-call(s32[1]{0:T(128)} %bitcast.14.me_ref, bf16[384,3072]{1,0:T(8,128)(2,1)S(1)} %pad_maximum_fusion.1.refs_0_, bf16[384,3072]{1,0:T(8,128)(2,1)S(1)} %copy-done.19, ...), custom_call_target="tpu_custom_call" | custom-call | bytes 1179648 | tf_op jit(solution)/shard_map/pallas_call | solution.py:144
  250.2 7.4 %shard_map.356.mixed_ref = bf16[128,1536]{1,0:T(8,128)(2,1)S(1)} custom-call(bf16[128,1536]{1,0:T(8,128)(2,1)S(1)} %get-tuple-element.535.refs_0_, bf16[512,1536]{1,0:T(8,128)(2,1)S(1)} %shard_map.355.refs_1_.refs_2_), custom_call_target="tpu_custom_call" | custom-call | flops 1048576 | bytes 1048576 | tf_op jit(solution)/shard_map/pallas_call | solution.py:622
  287.0 9.1 %collective-permute-done.43 = bf16[128,1536]{1,0:T(8,128)(2,1)S(1)} collective-permute-done((bf16[128,1536]{1,0:T(8,128)(2,1)S(1)}, bf16[128,1536]{1,0:T(8,128)(2,1)S(1)}, u32[]{:S(2)}, u32[]{:S(2)}) %collective-permute-start.43) | collective-permute-done | bytes 393248 | tf_op jit(solution)/shard_map/ppermute | solution.py:78
  301.0 9.6 %shard_map.358 = (bf16[1024,384]{1,0:T(8,128)(2,1)S(1)}, bf16[1024,384]{1,0:T(8,128)(2,1)S(1)}, bf16[1024,384]{1,0:T(8,128)(2,1)S(1)}, bf16[1024,1536]{1,0:T(8,128)(2,1)S(1)}) custom-call(bf16[1024,1536]{1,0:T(8,128)(2,1)S(1)} %constant_dynamic-update-slice_fusion.9.row_ref.refs_2_, ...), custom_call_target="tpu_custom_call" | custom-call | flops 1048576 | bytes 1048576 | tf_op jit(solution)/shard_map/pallas_call | solution.py:492
  315.3 9.7 %shard_map.359 = (bf16[1024,384]{1,0:T(8,128)(2,1)S(1)}, bf16[1024,384]{1,0:T(8,128)(2,1)S(1)}, bf16[1024,384]{1,0:T(8,128)(2,1)S(1)}, bf16[1024,1536]{1,0:T(8,128)(2,1)S(1)}) custom-call(bf16[1024,1536]{1,0:T(8,128)(2,1)S(1)} %collective-permute-done.46.row_ref.refs_3_, bf16[1024,1536]{1,0:T(8,128)(2,1)S(1)} %copy-done.6, bf16[384,1536]{1,0:T(8,128)(2,1)S(1)} %copy-done.8, ...), custom_call_target="tpu_custom_call" | custom-call | flops 1048576 | bytes 1048576 | tf_op jit(solution)/shard_map/pallas_call | solution.py:492
  360.8 7.6 %collective-permute-done.52 = bf16[96,1536]{1,0:T(8,128)(2,1)S(1)} collective-permute-done((bf16[96,1536]{1,0:T(8,128)(2,1)S(1)}, bf16[96,1536]{1,0:T(8,128)(2,1)S(1)}, u32[]{:S(2)}, u32[]{:S(2)}) %collective-permute-start.52) | collective-permute-done | bytes 294944 | tf_op jit(solution)/shard_map/ppermute | solution.py:78
  388.2 6.5 collective-permute-done.61
  403.4 7.2 %shard_map.366.in_ref = bf16[640,1536]{1,0:T(8,128)(2,1)S(1)} custom-call(bf16[128,1536]{1,0:T(8,128)(2,1)S(1)} %copy-done.33, bf16[128,1536]{1,0:T(8,128)(2,1)S(1)} %get-tuple-element.691.refs_1_, bf16[512,1536]{1,0:T(8,128)(2,1)S(1)} %shard_map.355.refs_1_.refs_2_), custom_call_target="tpu_custom_call" | custom-call | flops 1048576 | bytes 1048576 | tf_op jit(solution)/shard_map/pallas_call | solution.py:676
  425.7 7.4 %collective-permute-done.71 = bf16[96,1536]{1,0:T(8,128)(2,1)S(1)} collective-permute-done((bf16[96,1536]{1,0:T(8,128)(2,1)S(1)}, bf16[96,1536]{1,0:T(8,128)(2,1)S(1)}, u32[]{:S(2)}, u32[]{:S(2)}) %collective-permute-start.71) | collective-permute-done | bytes 294944 | tf_op jit(solution)/shard_map/ppermute | solution.py:78
  440.6 7.3 %shard_map.368.query_ref.own_ref = bf16[640,1536]{1,0:T(8,128)(2,1)S(1)} custom-call(bf16[128,1536]{1,0:T(8,128)(2,1)S(1)} %copy-done.31, bf16[128,1536]{1,0:T(8,128)(2,1)S(1)} %get-tuple-element.727.refs_1_, bf16[256,1536]{1,0:T(8,128)(2,1)S(1)} %copy-done.13, bf16[256,1536]{1,0:T(8,128)(2,1)S(1)} %copy-done.15, f32[128,128]{1,0:T(8,128)S(1)} %copy-done.40, ...), custom_call_target="tpu_custom_call" | custom-call | flops 1048576 | bytes 1048576 | tf_op jit(solution)/shard_map/pallas_call | solution.py:676
  451.3 13.9 %collective-permute-done.73 = bf16[384,1536]{1,0:T(8,128)(2,1)S(1)} collective-permute-done((bf16[384,1536]{1,0:T(8,128)(2,1)S(1)}, bf16[384,1536]{1,0:T(8,128)(2,1)S(1)}, u32[]{:S(2)}, u32[]{:S(2)}) %collective-permute-start.73) | collective-permute-done | bytes 1179680 | tf_op jit(solution)/shard_map/ppermute | solution.py:78
  481.3 6.0 collective-permute-done.81
  545.1 36.2 %collective-permute-done.91 = bf16[208,1536]{1,0:T(8,128)(2,1)S(1)} collective-permute-done((bf16[208,1536]{1,0:T(8,128)(2,1)S(1)}, bf16[208,1536]{1,0:T(8,128)(2,1)S(1)}, u32[]{:S(2)}, u32[]{:S(2)}) %collective-permute-start.91) | collective-permute-done | bytes 639008 | tf_op jit(solution)/shard_map/ppermute | solution.py:78
  590.0 12.8 %collective-permute-done.93 = bf16[192,1792]{1,0:T(8,128)(2,1)S(1)} collective-permute-done((bf16[192,1792]{1,0:T(8,128)(2,1)S(1)}, bf16[192,1792]{1,0:T(8,128)(2,1)S(1)}, u32[]{:S(2)}, u32[]{:S(2)}) %collective-permute-start.93) | collective-permute-done | bytes 688160 | tf_op jit(solution)/shard_map/ppermute | solution.py:78
  612.7 12.9 %collective-permute-done.96 = bf16[96,1792]{1,0:T(8,128)(2,1)S(1)} collective-permute-done((bf16[96,1792]{1,0:T(8,128)(2,1)S(1)}, bf16[96,1792]{1,0:T(8,128)(2,1)S(1)}, u32[]{:S(2)}, u32[]{:S(2)}) %collective-permute-start.96) | collective-permute-done | bytes 344096 | tf_op jit(solution)/shard_map/ppermute | solution.py:78
  634.3 9.3 %collective-permute-done.100 = bf16[48,1920]{1,0:T(8,128)(2,1)S(1)} collective-permute-done((bf16[48,1920]{1,0:T(8,128)(2,1)S(1)}, bf16[48,1920]{1,0:T(8,128)(2,1)S(1)}, u32[]{:S(2)}, u32[]{:S(2)}) %collective-permute-start.100) | collective-permute-done | bytes 184352 | tf_op jit(solution)/shard_map/ppermute | solution.py:78
  (656 shorter events, 323.3 us)
Async XLA Ops:
  5.8 24.4 %collective-permute-start = (bf16[48,4736]{1,0:T(8,128)(2,1)}, bf16[48,4736]{1,0:T(8,128)(2,1)S(1)}, u32[]{:S(2)}, u32[]{:S(2)}) collective-permute-start(bf16[48,4736]{1,0:T(8,128)(2,1)} %pad_maximum_fusion.35), channel_id=1, source_target_pairs={{0,16},{1,17},{2,18},{3,19},{4,20},{5,21},{6,22},{7,23},{8,24},{9,... | collective-permute-start | bytes 1363976 | tf_op jit(solution)/shard_map/ppermute | solution.py:78
  52.8 28.8 %collective-permute-start.2 = (bf16[48,6144]{1,0:T(8,128)(2,1)S(1)}, bf16[48,6144]{1,0:T(8,128)(2,1)S(1)}, u32[]{:S(2)}, u32[]{:S(2)}) collective-permute-start(bf16[48,6144]{1,0:T(8,128)(2,1)S(1)} %maximum_maximum_fusion), channel_id=1, source_target_pairs={{0,16},{1,17},{2,18},{3,19},{4,20},{5,21},{6,22},{7,23},{8,24},{9,... | collective-permute-start | bytes 1769480 | tf_op jit(solution)/shard_map/ppermute | solution.py:78
  56.2 25.5 %collective-permute-start.4 = (bf16[192,2304]{1,0:T(8,128)(2,1)S(1)}, bf16[192,2304]{1,0:T(8,128)(2,1)S(1)}, u32[]{:S(2)}, u32[]{:S(2)}) collective-permute-start(bf16[192,2304]{1,0:T(8,128)(2,1)S(1)} %slice.704), channel_id=1, source_target_pairs={{0,4},{1,5},{2,6},{3,7},{4,0},{5,1},{6,2},{7,3},{8,12},{9,13},{10,... | collective-permute-start | bytes 2654216 | tf_op jit(solution)/shard_map/ppermute | solution.py:78
  82.0 44.9 %collective-permute-start.5 = (bf16[384,2432]{1,0:T(8,128)(2,1)S(1)}, bf16[384,2432]{1,0:T(8,128)(2,1)S(1)}, u32[]{:S(2)}, u32[]{:S(2)}) collective-permute-start(bf16[384,2432]{1,0:T(8,128)(2,1)S(1)} %pad_maximum_fusion.3.refs_0_), channel_id=1, source_target_pairs={{0,4},{1,5},{2,6},{3,7},{4,0},{5,1},{6,2},{7,3},{8,12},{9,13},{10,... | collective-permute-start | bytes 5603336 | tf_op jit(solution)/shard_map/ppermute | solution.py:78
  83.6 43.3 %collective-permute-start.9 = (bf16[384,2432]{1,0:T(8,128)(2,1)S(1)}, bf16[384,2432]{1,0:T(8,128)(2,1)S(1)}, u32[]{:S(2)}, u32[]{:S(2)}) collective-permute-start(bf16[384,2432]{1,0:T(8,128)(2,1)S(1)} %pad_maximum_fusion.3.refs_0_), channel_id=1, source_target_pairs={{0,1},{1,0},{2,3},{3,2},{4,5},{5,4},{6,7},{7,6},{8,9},{9,8},{10,11... | collective-permute-start | bytes 5603336 | tf_op jit(solution)/shard_map/ppermute | solution.py:78
  83.6 43.3 %collective-permute-start.6 = (bf16[384,2304]{1,0:T(8,128)(2,1)S(1)}, bf16[384,2304]{1,0:T(8,128)(2,1)S(1)}, u32[]{:S(2)}, u32[]{:S(2)}) collective-permute-start(bf16[384,2304]{1,0:T(8,128)(2,1)S(1)} %pad_maximum_fusion.5.refs_4_), channel_id=1, source_target_pairs={{0,2},{1,3},{2,0},{3,1},{4,6},{5,7},{6,4},{7,5},{8,10},{9,11},{10,... | collective-permute-start | bytes 5308424 | tf_op jit(solution)/shard_map/ppermute | solution.py:78
  85.1 41.8 %collective-permute-start.8 = (bf16[96,6144]{1,0:T(8,128)(2,1)S(1)}, bf16[96,6144]{1,0:T(8,128)(2,1)S(1)}, u32[]{:S(2)}, u32[]{:S(2)}) collective-permute-start(bf16[96,6144]{1,0:T(8,128)(2,1)S(1)} %pad_maximum_fusion.9), channel_id=1, source_target_pairs={{0,8},{1,9},{2,10},{3,11},{4,12},{5,13},{6,14},{7,15},{8,0},{9,1},... | collective-permute-start | bytes 3538952 | tf_op jit(solution)/shard_map/ppermute | solution.py:78
  85.8 39.3 %collective-permute-start.7 = (bf16[208,1536]{1,0:T(8,128)(2,1)S(1)}, bf16[208,1536]{1,0:T(8,128)(2,1)S(1)}, u32[]{:S(2)}, u32[]{:S(2)}) collective-permute-start(bf16[208,1536]{1,0:T(8,128)(2,1)S(1)} %fusion.19), channel_id=1, source_target_pairs={{0,16},{1,17},{2,18},{3,19},{4,20},{5,21},{6,22},{7,23},{8,24},{9,... | collective-permute-start | bytes 1916936 | tf_op jit(solution)/shard_map/ppermute | solution.py:78
  127.2 32.0 %collective-permute-start.13 = (bf16[384,2432]{1,0:T(8,128)(2,1)S(1)}, bf16[384,2432]{1,0:T(8,128)(2,1)S(1)}, u32[]{:S(2)}, u32[]{:S(2)}) collective-permute-start(bf16[384,2432]{1,0:T(8,128)(2,1)S(1)} %collective-permute-done.5.refs_1_), channel_id=1, source_target_pairs={{0,1},{1,0},{2,3},{3,2},{4,5},{5,4},{6,7},{7,6},{8,9},{9,8},{10,11... | collective-permute-start | bytes 5603336 | tf_op jit(solution)/shard_map/ppermute | solution.py:78
  127.2 29.5 %collective-permute-start.12 = (bf16[384,2304]{1,0:T(8,128)(2,1)S(1)}, bf16[384,2304]{1,0:T(8,128)(2,1)S(1)}, u32[]{:S(2)}, u32[]{:S(2)}) collective-permute-start(bf16[384,2304]{1,0:T(8,128)(2,1)S(1)} %pad_maximum_fusion.5.refs_4_), channel_id=1, source_target_pairs={{0,1},{1,0},{2,3},{3,2},{4,5},{5,4},{6,7},{7,6},{8,9},{9,8},{10,11... | collective-permute-start | bytes 5308424 | tf_op jit(solution)/shard_map/ppermute | solution.py:78
  128.1 29.9 %collective-permute-start.14 = (bf16[384,2304]{1,0:T(8,128)(2,1)S(1)}, bf16[384,2304]{1,0:T(8,128)(2,1)S(1)}, u32[]{:S(2)}, u32[]{:S(2)}) collective-permute-start(bf16[384,2304]{1,0:T(8,128)(2,1)S(1)} %collective-permute-done.6.refs_5_), channel_id=1, source_target_pairs={{0,1},{1,0},{2,3},{3,2},{4,5},{5,4},{6,7},{7,6},{8,9},{9,8},{10,11... | collective-permute-start | bytes 5308424 | tf_op jit(solution)/shard_map/ppermute | solution.py:78
  128.1 28.4 %collective-permute-start.10 = (bf16[192,3072]{1,0:T(8,128)(2,1)S(1)}, bf16[192,3072]{1,0:T(8,128)(2,1)S(1)}, u32[]{:S(2)}, u32[]{:S(2)}) collective-permute-start(bf16[192,3072]{1,0:T(8,128)(2,1)S(1)} %get-tuple-element.431), channel_id=1, source_target_pairs={{0,2},{1,3},{2,0},{3,1},{4,6},{5,7},{6,4},{7,5},{8,10},{9,11},{10,... | collective-permute-start | bytes 3538952 | tf_op jit(solution)/shard_map/ppermute | solution.py:78
  128.6 28.1 %collective-permute-start.11 = (bf16[192,3072]{1,0:T(8,128)(2,1)S(1)}, bf16[192,3072]{1,0:T(8,128)(2,1)S(1)}, u32[]{:S(2)}, u32[]{:S(2)}) collective-permute-start(bf16[192,3072]{1,0:T(8,128)(2,1)S(1)} %get-tuple-element.432), channel_id=1, source_target_pairs={{0,4},{1,5},{2,6},{3,7},{4,0},{5,1},{6,2},{7,3},{8,12},{9,13},{10,... | collective-permute-start | bytes 3538952 | tf_op jit(solution)/shard_map/ppermute | solution.py:78
  159.5 56.8 %collective-permute-start.15 = (bf16[384,3072]{1,0:T(8,128)(2,1)S(1)}, bf16[384,3072]{1,0:T(8,128)(2,1)S(1)}, u32[]{:S(2)}, u32[]{:S(2)}) collective-permute-start(bf16[384,3072]{1,0:T(8,128)(2,1)S(1)} %pad_maximum_fusion.1.refs_0_), channel_id=1, source_target_pairs={{0,4},{1,5},{2,6},{3,7},{4,0},{5,1},{6,2},{7,3},{8,12},{9,13},{10,... | collective-permute-start | bytes 7077896 | tf_op jit(solution)/shard_map/ppermute | solution.py:78
  160.1 56.3 %collective-permute-start.16 = (bf16[384,3072]{1,0:T(8,128)(2,1)S(1)}, bf16[384,3072]{1,0:T(8,128)(2,1)S(1)}, u32[]{:S(2)}, u32[]{:S(2)}) collective-permute-start(bf16[384,3072]{1,0:T(8,128)(2,1)S(1)} %pad_maximum_fusion.refs_4_), channel_id=1, source_target_pairs={{0,2},{1,3},{2,0},{3,1},{4,6},{5,7},{6,4},{7,5},{8,10},{9,11},{10,... | collective-permute-start | bytes 7077896 | tf_op jit(solution)/shard_map/ppermute | solution.py:78
  161.6 54.8 %collective-permute-start.17 = (bf16[384,3072]{1,0:T(8,128)(2,1)S(1)}, bf16[384,3072]{1,0:T(8,128)(2,1)}, u32[]{:S(2)}, u32[]{:S(2)}) collective-permute-start(bf16[384,3072]{1,0:T(8,128)(2,1)S(1)} %pad_maximum_fusion.1.refs_0_), channel_id=1, source_target_pairs={{0,1},{1,0},{2,3},{3,2},{4,5},{5,4},{6,7},{7,6},{8,9},{9,8},{10,11... | collective-permute-start | bytes 7077896 | tf_op jit(solution)/shard_map/ppermute | solution.py:78
  161.6 54.8 %collective-permute-start.18 = (bf16[384,1536]{1,0:T(8,128)(2,1)}, bf16[384,1536]{1,0:T(8,128)(2,1)S(1)}, u32[]{:S(2)}, u32[]{:S(2)}) collective-permute-start(bf16[384,1536]{1,0:T(8,128)(2,1)} %bitcast.12), channel_id=1, source_target_pairs={{0,16},{1,17},{2,18},{3,19},{4,20},{5,21},{6,22},{7,23},{8,24},{9,... | collective-permute-start | bytes 3538952 | tf_op jit(solution)/shard_map/ppermute | solution.py:78
  437.5 27.8 %collective-permute-start.73 = (bf16[384,1536]{1,0:T(8,128)(2,1)S(1)}, bf16[384,1536]{1,0:T(8,128)(2,1)S(1)}, u32[]{:S(2)}, u32[]{:S(2)}) collective-permute-start(bf16[384,1536]{1,0:T(8,128)(2,1)S(1)} %convolution_convert_fusion.3), channel_id=1, source_target_pairs={{0,8},{1,9},{2,10},{3,11},{4,12},{5,13},{6,14},{7,15},{8,0},{9,1},... | collective-permute-start | bytes 3538952 | tf_op jit(solution)/shard_map/ppermute | solution.py:78
  437.6 27.8 %collective-permute-start.74 = (bf16[384,1536]{1,0:T(8,128)(2,1)S(1)}, bf16[384,1536]{1,0:T(8,128)(2,1)S(1)}, u32[]{:S(2)}, u32[]{:S(2)}) collective-permute-start(bf16[384,1536]{1,0:T(8,128)(2,1)S(1)} %convolution_convert_fusion.2), channel_id=1, source_target_pairs={{0,2},{1,3},{2,0},{3,1},{4,6},{5,7},{6,4},{7,5},{8,10},{9,11},{10,... | collective-permute-start | bytes 3538952 | tf_op jit(solution)/shard_map/ppermute | solution.py:78
  438.8 27.6 %collective-permute-start.75 = (bf16[384,1536]{1,0:T(8,128)(2,1)S(1)}, bf16[384,1536]{1,0:T(8,128)(2,1)S(1)}, u32[]{:S(2)}, u32[]{:S(2)}) collective-permute-start(bf16[384,1536]{1,0:T(8,128)(2,1)S(1)} %bitcast.85), channel_id=1, source_target_pairs={{0,4},{1,5},{2,6},{3,7},{4,0},{5,1},{6,2},{7,3},{8,12},{9,13},{10,... | collective-permute-start | bytes 3538952 | tf_op jit(solution)/shard_map/ppermute | solution.py:78
  524.0 59.5 %collective-permute-start.87 = (bf16[384,2560]{1,0:T(8,128)(2,1)}, bf16[384,2560]{1,0:T(8,128)(2,1)S(1)}, u32[]{:S(2)}, u32[]{:S(2)}) collective-permute-start(bf16[384,2560]{1,0:T(8,128)(2,1)} %copy-done.60), channel_id=1, source_target_pairs={{0,4},{1,5},{2,6},{3,7},{4,0},{5,1},{6,2},{7,3},{8,12},{9,13},{10,... | collective-permute-start | bytes 5898248 | tf_op jit(solution)/shard_map/ppermute | solution.py:78
  536.4 47.0 %collective-permute-start.92 = (bf16[384,1920]{1,0:T(8,128)(2,1)S(1)}, bf16[384,1920]{1,0:T(8,128)(2,1)S(1)}, u32[]{:S(2)}, u32[]{:S(2)}) collective-permute-start(bf16[384,1920]{1,0:T(8,128)(2,1)S(1)} %get-tuple-element.785), channel_id=1, source_target_pairs={{0,2},{1,3},{2,0},{3,1},{4,6},{5,7},{6,4},{7,5},{8,10},{9,11},{10,... | collective-permute-start | bytes 4423688 | tf_op jit(solution)/shard_map/ppermute | solution.py:78
  537.9 45.6 %collective-permute-start.86 = (bf16[384,1792]{1,0:T(8,128)(2,1)S(1)}, bf16[384,1792]{1,0:T(8,128)(2,1)S(1)}, u32[]{:S(2)}, u32[]{:S(2)}) collective-permute-start(bf16[384,1792]{1,0:T(8,128)(2,1)S(1)} %copy-done.62), channel_id=1, source_target_pairs={{0,8},{1,9},{2,10},{3,11},{4,12},{5,13},{6,14},{7,15},{8,0},{9,1},... | collective-permute-start | bytes 4128776 | tf_op jit(solution)/shard_map/ppermute | solution.py:78
  538.0 43.3 %collective-permute-start.91 = (bf16[208,1536]{1,0:T(8,128)(2,1)S(1)}, bf16[208,1536]{1,0:T(8,128)(2,1)S(1)}, u32[]{:S(2)}, u32[]{:S(2)}) collective-permute-start(bf16[208,1536]{1,0:T(8,128)(2,1)S(1)} %copy-done.85), channel_id=1, source_target_pairs={{0,16},{1,17},{2,18},{3,19},{4,20},{5,21},{6,22},{7,23},{8,24},{9,... | collective-permute-start | bytes 1916936 | tf_op jit(solution)/shard_map/ppermute | solution.py:78
  (189 other events, 2110.6 us)
